TPU v7x, 128 devices: a whole 4x4x4 slice. The times are simulated.
128 devices in a mesh: face: 4 (over x), tile: 32 (over y, z, core).
Axes of the slice: x: 4, y: 4, z: 4, core: 2. Of those that a mesh axis runs over, the one named last changes fastest.
Arguments:
- atmos_state: float32 [4, 8, 768, 3072], P(None, None, 'tile', 'face'), may hold values from -6 to 6
- courant: float32 [3, 768, 3072], P(None, 'tile', 'face'), may hold values from 0.04 to 0.15
- level_weights: float32 [4, 8], replicated, may hold values from 0.2 to 1
- remap_tiles: bfloat16 [36864, 128, 128], P(('face', 'tile')), may hold values from -0.25 to 0.25
- src_block: int32 [128, 288], P(('face', 'tile')), may hold values from 0 to 143
- owner: int32 [128, 288, 1], P(('face', 'tile')), may hold values from 0 to 127; in each aligned block of 288 rows (0 to 287, 288 to 575, ..., all dimensions but the last counted through in order) at most 5 rows name the same one
- offset: int32 [128, 288], P(('face', 'tile')), may hold values from 0 to 63
- tile_index: int32 [128, 288], P(('face', 'tile')), may hold values from 0 to 287, each once within a row
- ocean_state: float32 [4, 8, 256, 4096], P(None, None, 'face', 'tile'), may hold values from -6 to 6
- mixing: float32 [256, 4096], P('face', 'tile'), may hold values from 0.05 to 0.4
- land_mask: int32 [256, 4096], P('face', 'tile'), may hold values 0 or 1
Outputs:
- air_state: float32 [4, 8, 768, 3072], P(None, None, 'tile', 'face')
- ocean_out: float32 [4, 8, 256, 4096], P(None, None, 'face', 'tile')
- atmos_surface: float32 [4, 768, 3072], P(None, 'tile', 'face')
Inputs may be any that keep to these rules, and one draw needn't show every extreme that they name: Among the 288 entries of one device, no owner is named more than 5 times, a bound that some block reaches. `tile_index`: each device's entries use each of its 288 stored tiles exactly once.
All inputs are finite; a program needn't handle non-finite values. No bound on the sum of `land_mask` on one device may be relied on, other than what follows from the above.
Results may differ from a plain program's by a relative error of at most 0.0033.
Values may be sent and summed in bfloat16 or wider, within the bound.
No kernel may reach another device: no remote copies, remote signals or barrier semaphores. Data moves between devices by JAX's collectives and lax.ppermute only.
A program may use at most 64 MiB of HBM per device.

v0:
```python
import jax
import jax.numpy as jnp
from jax import lax
from jax.sharding import PartitionSpec as P

STEPS = 3


def padded(cells, sides, width, closed):
    for axis, dim in sides:
        count = lax.axis_size(axis)
        ends = count if closed else count - 1
        head = lax.slice_in_dim(cells, 0, width, axis=dim)
        tail = lax.slice_in_dim(cells, cells.shape[dim] - width, cells.shape[dim], axis=dim)
        cells = jnp.concatenate(
            [
                lax.ppermute(tail, axis, [(i, (i + 1) % count) for i in range(ends)]),
                cells,
                lax.ppermute(head, axis, [((i + 1) % count, i) for i in range(ends)]),
            ],
            axis=dim,
        )
    return cells


def advance(air_state, coefs, west_cells, east_cells, south_cells, north_cells):
    along_x, along_y, spread = (coefs[0], coefs[1], coefs[2])
    return (
        air_state
        - along_x * (air_state - west_cells)
        - along_y * (air_state - south_cells)
        + spread * (east_cells + west_cells + north_cells + south_cells - 4.0 * air_state)
    )


def shards(
    atmos_state,
    courant,
    level_weights,
    remap_tiles,
    src_block,
    owner,
    offset,
    tile_index,
    ocean_state,
    mixing,
    land_mask,
):
    faces = lax.axis_size("face")
    tile_count = lax.axis_size("tile")
    devices = faces * tile_count
    fields, levels, rows_here, cols_here = atmos_state.shape
    entries = remap_tiles.shape[0]
    block_size = remap_tiles.shape[1]
    capacity = max(2, (2 * entries + devices - 1) // devices)
    slot_count = devices * capacity
    air_state = atmos_state
    for step_index in range(STEPS):
        widened = padded(air_state, (("face", 3),), 1, True)
        row_padded = padded(air_state, (("tile", 2),), 1, False)
        air_state = advance(
            air_state,
            courant,
            widened[..., :-2],
            widened[..., 2:],
            row_padded[:, :, :-2],
            row_padded[:, :, 2:],
        )
    air_flux = jnp.einsum(
        "fl,flrc->frc", level_weights, air_state, precision=lax.Precision.HIGHEST
    ).astype(jnp.bfloat16)
    flux_blocks = air_flux.reshape(fields, -1, block_size)
    tile_ids = jnp.arange(entries, dtype=jnp.int32)
    pick = (tile_index[0][:, None] == tile_ids[None, :]).astype(jnp.int32)
    tile_src = jnp.sum(pick * src_block[0][:, None], axis=0)
    tile_owner = jnp.sum(pick * owner[0, :, 0][:, None], axis=0)
    tile_offset = jnp.sum(pick * offset[0][:, None], axis=0)
    source_rows = flux_blocks[:, tile_src, :]
    contribution = jnp.einsum(
        "fjk,jkm->jfm", source_rows, remap_tiles, preferred_element_type=jnp.float32
    )
    earlier = tile_ids[None, :] < tile_ids[:, None]
    same_owner = tile_owner[:, None] == tile_owner[None, :]
    slot_rank = jnp.sum((earlier & same_owner).astype(jnp.int32), axis=1)
    destination = tile_owner * capacity + slot_rank
    slot_ids = jnp.arange(slot_count, dtype=jnp.int32)
    routing = slot_ids[:, None] == destination[None, :]
    outgoing = jnp.dot(
        routing.astype(jnp.float32),
        contribution.reshape(entries, fields * block_size),
        precision=lax.Precision.HIGHEST,
    )
    outgoing_offset = jnp.sum(routing.astype(jnp.int32) * (tile_offset + 1)[None, :], axis=1) - 1
    incoming, incoming_offset = (
        lax.all_to_all(
            outgoing.reshape(devices, capacity, fields * block_size),
            ("face", "tile"),
            split_axis=0,
            concat_axis=0,
            tiled=True,
        ),
        lax.all_to_all(
            outgoing_offset.reshape(devices, capacity),
            ("face", "tile"),
            split_axis=0,
            concat_axis=0,
            tiled=True,
        ),
    )
    incoming = incoming.reshape(slot_count, fields * block_size)
    incoming_offset = incoming_offset.reshape(slot_count)
    ocean_rows = ocean_state.shape[2]
    placing = (jnp.arange(ocean_rows, dtype=jnp.int32)[:, None] == incoming_offset[None, :]).astype(
        jnp.float32
    )
    ocean_flux = (
        jnp.dot(placing, incoming, precision=lax.Precision.HIGHEST)
        .reshape(ocean_rows, fields, block_size)
        .transpose(1, 0, 2)
    )
    wet_cells = land_mask.astype(jnp.float32)
    forced = ocean_state.at[:, 0].add(wet_cells * ocean_flux)
    level_above = jnp.concatenate([forced[:, :1], forced[:, :-1]], axis=1)
    level_below = jnp.concatenate([forced[:, 1:], forced[:, -1:]], axis=1)
    ocean_out = forced + wet_cells * mixing * (level_above + level_below - 2.0 * forced)
    sea_surface = (wet_cells * ocean_out[:, 0]).astype(jnp.bfloat16)
    surface_rows = sea_surface.transpose(1, 0, 2).reshape(ocean_rows, fields * block_size)
    returning = jnp.dot(
        placing.astype(jnp.bfloat16).T, surface_rows, preferred_element_type=jnp.float32
    ).astype(jnp.bfloat16)
    returned = lax.all_to_all(
        returning.reshape(devices, capacity, fields * block_size),
        ("face", "tile"),
        split_axis=0,
        concat_axis=0,
        tiled=True,
    )
    returned = returned.reshape(slot_count, fields * block_size)
    back_tiles = (
        jnp.dot(routing.astype(jnp.bfloat16).T, returned, preferred_element_type=jnp.float32)
        .astype(jnp.bfloat16)
        .reshape(entries, fields, block_size)
    )
    back_terms = jnp.einsum(
        "jfm,jkm->jfk", back_tiles, remap_tiles, preferred_element_type=jnp.float32
    )
    source_blocks = flux_blocks.shape[1]
    collect = (jnp.arange(source_blocks, dtype=jnp.int32)[:, None] == tile_src[None, :]).astype(
        jnp.float32
    )
    gathered = jnp.dot(
        collect, back_terms.reshape(entries, fields * block_size), precision=lax.Precision.HIGHEST
    )
    atmos_surface = (
        gathered.reshape(source_blocks, fields, block_size)
        .transpose(1, 0, 2)
        .reshape(fields, rows_here, cols_here)
    )
    return (air_state, ocean_out, atmos_surface)


def solution(mesh):
    return jax.shard_map(
        shards,
        mesh=mesh,
        in_specs=(
            P(None, None, "tile", "face"),
            P(None, "tile", "face"),
            P(),
            P(("face", "tile"), None, None),
            P(("face", "tile"), None),
            P(("face", "tile"), None, None),
            P(("face", "tile"), None),
            P(("face", "tile"), None),
            P(None, None, "face", "tile"),
            P("face", "tile"),
            P("face", "tile"),
        ),
        out_specs=(
            P(None, None, "tile", "face"),
            P(None, None, "face", "tile"),
            P(None, "tile", "face"),
        ),
        check_vma=False,
    )
```

profile of v0, /device:TPU:1, one launch (start us, length us, event | category | flops | bytes accessed | tf_op | source)
XLA Modules:
  0.0 169.3 jit_solution(15335709029131641811)
XLA Ops:
  1.9 2.4 %copy.57 = f32[4,8,24,768]{3,1,2,0:T(8,128)S(1)} copy(f32[4,8,24,768]{3,2,1,0:T(8,128)} %param.13) | data formatting | bytes 4718592 | tf_op args[0]
  9.3 4.9 %collective-permute-start.1 = (f32[4,8,1,768]{3,1,2,0:T(8,128)}, f32[4,8,1,768]{3,1,2,0:T(8,128)}, u32[]{:S(2)}, u32[]{:S(2)}) collective-permute-start(f32[4,8,1,768]{3,1,2,0:T(8,128)} %get-tuple-element.34), channel_id=1, source_target_pairs={{0,1},{1,2},{2,3},{3,4},{4,5},{5,6},{6,7},{7,8},{8,9},{9,10},{10,1... | collective-permute-start | bytes 294920 | tf_op jit(solution)/shard_map/ppermute | solution.py:17
  17.7 9.0 %all-to-all-start = ((s32[128,1,5]{2,1,0:T(1,128)}), s32[128,1,5]{2,1,0:T(1,128)S(1)}, u32[]{:S(2)}, u32[]{:S(2)}) async-start(s32[128,1,5]{2,1,0:T(1,128)} %bitcast.83), calls=%async_computation | async-start | bytes 131072 | tf_op jit(solution)/shard_map/all_to_all | solution.py:102
  27.7 3.6 %fusion.28 = f32[4,8,24,768]{3,1,2,0:T(8,128)S(1)} fusion(f32[4,8,1,768]{3,1,2,0:T(8,128)} %collective-permute-done.3, f32[4,8,24,768]{3,1,2,0:T(8,128)S(1)} %copy.57, f32[4,8,24,1]{3,1,2,0:T(8,128)} %collective-permute-done.2, f32[4,8,1,768]{3,1,2,0:T(8,128)} %collective-permute-done.1, f32[4,8,24,1]{3,1,2,0:T(8,128)} %collective-permute-done, ...), kind=kLoop, calls=%fused_computation.38 | loop fusion | flops 10027008 | bytes 5142528 | tf_op jit(solution)/shard_map/add | solution.py:29
  34.3 4.2 %collective-permute-start.5 = (f32[4,8,1,768]{3,1,2,0:T(8,128)S(1)}, f32[4,8,1,768]{3,1,2,0:T(8,128)S(1)}, u32[]{:S(2)}, u32[]{:S(2)}) collective-permute-start(f32[4,8,1,768]{3,1,2,0:T(8,128)S(1)} %get-tuple-element.30), channel_id=1, source_target_pairs={{0,1},{1,2},{2,3},{3,4},{4,5},{5,6},{6,7},{7,8},{8,9},{9,10},{10,1... | collective-permute-start | bytes 294920 | tf_op jit(solution)/shard_map/ppermute | solution.py:17
  44.4 2.4 %fusion.16 = f32[4,8,24,768]{3,1,2,0:T(8,128)S(1)} fusion(f32[4,8,1,768]{3,1,2,0:T(8,128)S(1)} %collective-permute-done.7, f32[4,8,24,768]{3,1,2,0:T(8,128)S(1)} %fusion.28, f32[4,8,24,1]{3,1,2,0:T(8,128)S(1)} %collective-permute-done.6, f32[4,8,1,768]{3,1,2,0:T(8,128)S(1)} %collective-permute-done.5, f32[4,8,24,1]{3,1,2,0:T(8,128)S(1)} %collective-permute-done.4, ...), kind=kLoop, calls=%fused_computation.22 | loop fusion | flops 10027008 | bytes 5142528 | tf_op jit(solution)/shard_map/add | solution.py:29
  48.6 3.2 %collective-permute-start.11 = (f32[4,8,1,768]{3,1,2,0:T(8,128)S(1)}, f32[4,8,1,768]{3,1,2,0:T(8,128)S(1)}, u32[]{:S(2)}, u32[]{:S(2)}) collective-permute-start(f32[4,8,1,768]{3,1,2,0:T(8,128)S(1)} %get-tuple-element.27), channel_id=1, source_target_pairs={{1,0},{2,1},{3,2},{4,3},{5,4},{6,5},{7,6},{8,7},{9,8},{10,9},{11,1... | collective-permute-start | bytes 294920 | tf_op jit(solution)/shard_map/ppermute | solution.py:19
  51.9 3.5 %collective-permute-start.9 = (f32[4,8,1,768]{3,1,2,0:T(8,128)S(1)}, f32[4,8,1,768]{3,1,2,0:T(8,128)S(1)}, u32[]{:S(2)}, u32[]{:S(2)}) collective-permute-start(f32[4,8,1,768]{3,1,2,0:T(8,128)S(1)} %get-tuple-element.26), channel_id=1, source_target_pairs={{0,1},{1,2},{2,3},{3,4},{4,5},{5,6},{6,7},{7,8},{8,9},{9,10},{10,1... | collective-permute-start | bytes 294920 | tf_op jit(solution)/shard_map/ppermute | solution.py:17
  55.4 2.4 %collective-permute-done.10 = f32[4,8,24,1]{3,1,2,0:T(8,128)S(1)} collective-permute-done((f32[4,8,24,1]{3,1,2,0:T(8,128)S(1)}, f32[4,8,24,1]{3,1,2,0:T(8,128)S(1)}, u32[]{:S(2)}, u32[]{:S(2)}) %collective-permute-start.10) | collective-permute-done | bytes 3104 | tf_op jit(solution)/shard_map/ppermute | solution.py:19
  59.1 2.4 %fusion.4 = f32[4,8,24,768]{3,1,2,0:T(8,128)S(1)} fusion(f32[4,8,1,768]{3,1,2,0:T(8,128)S(1)} %collective-permute-done.11, f32[4,8,24,768]{3,1,2,0:T(8,128)S(1)} %fusion.16, f32[4,8,24,1]{3,1,2,0:T(8,128)S(1)} %collective-permute-done.10, f32[4,8,1,768]{3,1,2,0:T(8,128)S(1)} %collective-permute-done.9, f32[4,8,24,1]{3,1,2,0:T(8,128)S(1)} %collective-permute-done.8, ...), kind=kLoop, calls=%fused_computation.6 | loop fusion | flops 10027008 | bytes 5142528 | tf_op jit(solution)/shard_map/add | solution.py:29
  67.6 2.7 %gather_fusion = bf16[288,4,128]{2,1,0:T(4,128)(2,1)} fusion(bf16[4,144,128]{2,0,1:T(4,128)(2,1)} %copy.68, s32[1024]{0:T(1024)S(1)} %pad_clamp_fusion), kind=kCustom, calls=%fused_computation | custom fusion | bytes 590976 | tf_op jit(solution)/shard_map/gather | solution.py:78
  70.3 7.2 %fusion.50 = f32[288,4,128]{2,1,0:T(4,128)} fusion(bf16[288,128,128]{2,1,0:T(8,128)(2,1)} %param.16, bf16[288,4,128]{2,1,0:T(4,128)(2,1)} %gather_fusion), kind=kOutput, calls=%fused_computation.77 | convolution fusion | flops 37748736 | bytes 10321920 | tf_op jit(solution)/shard_map/fjk,jkm->jfm/dot_general | solution.py:79
  77.5 2.1 %reshape.166 = f32[288,512,1]{1,0,2:T(8,128)} reshape(f32[288,4,128]{2,1,0:T(4,128)} %fusion.50) | data formatting | bytes 1179648 | tf_op jit(solution)/shard_map/reshape | solution.py:90
  79.6 2.4 %fusion.42 = f32[128,5,512]{2,0,1:T(8,128)S(1)} fusion(f32[288,512,1]{1,0,2:T(8,128)} %reshape.166, s32[128,5]{0,1:T(8,128)S(1)} %multiply_add_fusion, s32[288]{0:T(512)S(1)} %get-tuple-element.41), kind=kOutput, calls=%fused_computation.62 | convolution fusion | flops 1132646400 | bytes 1904256 | tf_op jit(solution)/shard_map/dot_general | solution.py:88
  82.0 2.1 %copy.69 = f32[128,5,512]{2,1,0:T(8,128)} copy(f32[128,5,512]{2,0,1:T(8,128)S(1)} %fusion.42) | data formatting | bytes 2621440 | tf_op jit(solution)/shard_map/dot_general | solution.py:88
  84.1 10.6 %all-to-all-start.1 = ((f32[128,5,512]{2,1,0:T(8,128)}), f32[128,5,512]{2,1,0:T(8,128)}, u32[]{:S(2)}, u32[]{:S(2)}) async-start(f32[128,5,512]{2,1,0:T(8,128)} %copy.69), calls=%async_computation.1 | async-start | bytes 4194304 | tf_op jit(solution)/shard_map/all_to_all | solution.py:95
  98.6 26.4 %all-to-all-done.1 = f32[128,5,512]{2,1,0:T(8,128)} async-done(((f32[128,5,512]{2,1,0:T(8,128)}), f32[128,5,512]{2,1,0:T(8,128)}, u32[]{:S(2)}, u32[]{:S(2)}) %all-to-all-start.1) | async-done | bytes 1310752 | tf_op jit(solution)/shard_map/all_to_all | solution.py:95
  124.9 2.5 %reshape.148 = f32[640,512]{1,0:T(8,128)} reshape(f32[128,5,512]{2,1,0:T(8,128)} %all-to-all-done.1) | data formatting | bytes 2621440 | tf_op jit(solution)/shard_map/reshape | solution.py:110
  127.4 2.8 %copy.70 = f32[512,640]{1,0:T(8,128)} copy(f32[512,640]{0,1:T(8,128)} %bitcast.79) | data formatting | bytes 2621440 | tf_op jit(solution)/shard_map/dot_general | solution.py:117
  130.2 2.1 %fusion.38 = f32[4,1,64,128]{3,2,1,0:T(8,128)S(1)} fusion(f32[4,128,640]{2,1,0:T(8,128)} %bitcast.80, f32[4,8,64,128]{3,2,1,0:T(8,128)S(1)} %copy.97, s32[640]{0:T(1024)S(1)} %eq.100, f32[64,128]{1,0:T(8,128)S(1)} %convert_element_type.29), kind=kOutput, calls=%fused_computation.55 | convolution fusion | flops 251764736 | bytes 1608192 | tf_op jit(solution)/shard_map/dot_general | solution.py:117
  135.5 4.8 %all-to-all-start.2 = ((bf16[128,5,512]{2,1,0:T(8,128)(2,1)}), bf16[128,5,512]{2,1,0:T(8,128)(2,1)S(1)}, u32[]{:S(2)}, u32[]{:S(2)}) async-start(bf16[128,5,512]{2,1,0:T(8,128)(2,1)} %reshape.151), calls=%async_computation.2 | async-start | bytes 2097152 | tf_op jit(solution)/shard_map/all_to_all | solution.py:131
  140.3 2.1 %copy.75 = f32[4,8,24,768]{3,2,1,0:T(8,128)} copy(f32[4,8,24,768]{3,1,2,0:T(8,128)S(1)} %fusion.4) | data formatting | bytes 4718592
  142.5 17.3 %all-to-all-done.2 = bf16[128,5,512]{2,1,0:T(8,128)(2,1)S(1)} async-done(((bf16[128,5,512]{2,1,0:T(8,128)(2,1)}), bf16[128,5,512]{2,1,0:T(8,128)(2,1)S(1)}, u32[]{:S(2)}, u32[]{:S(2)}) %all-to-all-start.2) | async-done | bytes 655392 | tf_op jit(solution)/shard_map/all_to_all | solution.py:131
  160.6 7.4 %fusion.73 = f32[288,4,128]{2,1,0:T(4,128)S(1)} fusion(bf16[288,4,128]{2,1,0:T(4,128)(2,1)S(1)} %reshape.153, bf16[288,128,128]{2,1,0:T(8,128)(2,1)} %param.16), kind=kOutput, calls=%fused_computation.114 | convolution fusion | flops 37748736 | bytes 10321920 | tf_op jit(solution)/shard_map/jfm,jkm->jfk/dot_general | solution.py:144
  (75 shorter events, 37.7 us)
Async XLA Ops:
  0.6 60.9 %copy-start = (f32[4,8]{1,0:T(4,128)S(1)}, f32[4,8]{1,0:T(4,128)}, u32[]{:S(2)}) copy-start(f32[4,8]{1,0:T(4,128)} %param.15) | copy-start | bytes 388
  1.9 14.2 %copy-start.3 = (s32[1,288]{1,0:T(1,128)S(1)}, s32[1,288]{1,0:T(1,128)}, u32[]{:S(2)}) copy-start(s32[1,288]{1,0:T(1,128)} %param.20) | copy-start | bytes 3460
  1.9 14.3 %copy-start.4 = (s32[1,288,1]{1,2,0:T(1,128)S(1)}, s32[1,288,1]{1,2,0:T(1,128)}, u32[]{:S(2)}) copy-start(s32[1,288,1]{1,2,0:T(1,128)} %param.18) | copy-start | bytes 3460
  1.9 14.3 %copy-start.5 = (s32[1,288]{1,0:T(1,128)S(1)}, s32[1,288]{1,0:T(1,128)}, u32[]{:S(2)}) copy-start(s32[1,288]{1,0:T(1,128)} %param.19) | copy-start | bytes 3460
  1.9 14.3 %copy-start.6 = (s32[1,288]{1,0:T(1,128)S(1)}, s32[1,288]{1,0:T(1,128)}, u32[]{:S(2)}) copy-start(s32[1,288]{1,0:T(1,128)} %param.17) | copy-start | bytes 3460
  5.3 22.4 %collective-permute-start = (f32[4,8,24,1]{3,1,2,0:T(8,128)}, f32[4,8,24,1]{3,1,2,0:T(8,128)}, u32[]{:S(2)}, u32[]{:S(2)}) collective-permute-start(f32[4,8,24,1]{3,1,2,0:T(8,128)} %get-tuple-element.32), channel_id=1, source_target_pairs={{0,32},{32,64},{64,96},{96,0},{1,33},{33,65},{65,97},{97,1},{2,34}... | collective-permute-start | bytes 9224 | tf_op jit(solution)/shard_map/ppermute | solution.py:17
  7.4 20.3 %collective-permute-start.2 = (f32[4,8,24,1]{3,1,2,0:T(8,128)}, f32[4,8,24,1]{3,1,2,0:T(8,128)}, u32[]{:S(2)}, u32[]{:S(2)}) collective-permute-start(f32[4,8,24,1]{3,1,2,0:T(8,128)} %get-tuple-element.33), channel_id=1, source_target_pairs={{32,0},{64,32},{96,64},{0,96},{33,1},{65,33},{97,65},{1,97},{34,2}... | collective-permute-start | bytes 9224 | tf_op jit(solution)/shard_map/ppermute | solution.py:19
  9.3 18.4 %collective-permute-start.1 = (f32[4,8,1,768]{3,1,2,0:T(8,128)}, f32[4,8,1,768]{3,1,2,0:T(8,128)}, u32[]{:S(2)}, u32[]{:S(2)}) collective-permute-start(f32[4,8,1,768]{3,1,2,0:T(8,128)} %get-tuple-element.34), channel_id=1, source_target_pairs={{0,1},{1,2},{2,3},{3,4},{4,5},{5,6},{6,7},{7,8},{8,9},{9,10},{10,1... | collective-permute-start | bytes 294920 | tf_op jit(solution)/shard_map/ppermute | solution.py:17
  14.2 13.5 %collective-permute-start.3 = (f32[4,8,1,768]{3,1,2,0:T(8,128)}, f32[4,8,1,768]{3,1,2,0:T(8,128)}, u32[]{:S(2)}, u32[]{:S(2)}) collective-permute-start(f32[4,8,1,768]{3,1,2,0:T(8,128)} %get-tuple-element.35), channel_id=1, source_target_pairs={{1,0},{2,1},{3,2},{4,3},{5,4},{6,5},{7,6},{8,7},{9,8},{10,9},{11,1... | collective-permute-start | bytes 294920 | tf_op jit(solution)/shard_map/ppermute | solution.py:19
  17.7 66.4 %all-to-all-start = ((s32[128,1,5]{2,1,0:T(1,128)}), s32[128,1,5]{2,1,0:T(1,128)S(1)}, u32[]{:S(2)}, u32[]{:S(2)}) async-start(s32[128,1,5]{2,1,0:T(1,128)} %bitcast.83), calls=%async_computation | async-start | bytes 131072 | tf_op jit(solution)/shard_map/all_to_all | solution.py:102
  31.5 10.8 %collective-permute-start.4 = (f32[4,8,24,1]{3,1,2,0:T(8,128)S(1)}, f32[4,8,24,1]{3,1,2,0:T(8,128)S(1)}, u32[]{:S(2)}, u32[]{:S(2)}) collective-permute-start(f32[4,8,24,1]{3,1,2,0:T(8,128)S(1)} %get-tuple-element.28), channel_id=1, source_target_pairs={{0,32},{32,64},{64,96},{96,0},{1,33},{33,65},{65,97},{97,1},{2,34}... | collective-permute-start | bytes 9224 | tf_op jit(solution)/shard_map/ppermute | solution.py:17
  33.0 10.0 %collective-permute-start.6 = (f32[4,8,24,1]{3,1,2,0:T(8,128)S(1)}, f32[4,8,24,1]{3,1,2,0:T(8,128)S(1)}, u32[]{:S(2)}, u32[]{:S(2)}) collective-permute-start(f32[4,8,24,1]{3,1,2,0:T(8,128)S(1)} %get-tuple-element.29), channel_id=1, source_target_pairs={{32,0},{64,32},{96,64},{0,96},{33,1},{65,33},{97,65},{1,97},{34,2}... | collective-permute-start | bytes 9224 | tf_op jit(solution)/shard_map/ppermute | solution.py:19
  34.3 8.7 %collective-permute-start.5 = (f32[4,8,1,768]{3,1,2,0:T(8,128)S(1)}, f32[4,8,1,768]{3,1,2,0:T(8,128)S(1)}, u32[]{:S(2)}, u32[]{:S(2)}) collective-permute-start(f32[4,8,1,768]{3,1,2,0:T(8,128)S(1)} %get-tuple-element.30), channel_id=1, source_target_pairs={{0,1},{1,2},{2,3},{3,4},{4,5},{5,6},{6,7},{7,8},{8,9},{9,10},{10,1... | collective-permute-start | bytes 294920 | tf_op jit(solution)/shard_map/ppermute | solution.py:17
  38.5 5.9 %collective-permute-start.7 = (f32[4,8,1,768]{3,1,2,0:T(8,128)S(1)}, f32[4,8,1,768]{3,1,2,0:T(8,128)S(1)}, u32[]{:S(2)}, u32[]{:S(2)}) collective-permute-start(f32[4,8,1,768]{3,1,2,0:T(8,128)S(1)} %get-tuple-element.31), channel_id=1, source_target_pairs={{1,0},{2,1},{3,2},{4,3},{5,4},{6,5},{7,6},{8,7},{9,8},{10,9},{11,1... | collective-permute-start | bytes 294920 | tf_op jit(solution)/shard_map/ppermute | solution.py:19
  47.0 10.7 %collective-permute-start.10 = (f32[4,8,24,1]{3,1,2,0:T(8,128)S(1)}, f32[4,8,24,1]{3,1,2,0:T(8,128)S(1)}, u32[]{:S(2)}, u32[]{:S(2)}) collective-permute-start(f32[4,8,24,1]{3,1,2,0:T(8,128)S(1)} %get-tuple-element.25), channel_id=1, source_target_pairs={{32,0},{64,32},{96,64},{0,96},{33,1},{65,33},{97,65},{1,97},{34,2}... | collective-permute-start | bytes 9224 | tf_op jit(solution)/shard_map/ppermute | solution.py:19
  48.6 10.5 %collective-permute-start.8 = (f32[4,8,24,1]{3,1,2,0:T(8,128)S(1)}, f32[4,8,24,1]{3,1,2,0:T(8,128)S(1)}, u32[]{:S(2)}, u32[]{:S(2)}) collective-permute-start(f32[4,8,24,1]{3,1,2,0:T(8,128)S(1)} %get-tuple-element.24), channel_id=1, source_target_pairs={{0,32},{32,64},{64,96},{96,0},{1,33},{33,65},{65,97},{97,1},{2,34}... | collective-permute-start | bytes 9224 | tf_op jit(solution)/shard_map/ppermute | solution.py:17
  48.6 10.5 %collective-permute-start.11 = (f32[4,8,1,768]{3,1,2,0:T(8,128)S(1)}, f32[4,8,1,768]{3,1,2,0:T(8,128)S(1)}, u32[]{:S(2)}, u32[]{:S(2)}) collective-permute-start(f32[4,8,1,768]{3,1,2,0:T(8,128)S(1)} %get-tuple-element.27), channel_id=1, source_target_pairs={{1,0},{2,1},{3,2},{4,3},{5,4},{6,5},{7,6},{8,7},{9,8},{10,9},{11,1... | collective-permute-start | bytes 294920 | tf_op jit(solution)/shard_map/ppermute | solution.py:19
  51.9 7.2 %collective-permute-start.9 = (f32[4,8,1,768]{3,1,2,0:T(8,128)S(1)}, f32[4,8,1,768]{3,1,2,0:T(8,128)S(1)}, u32[]{:S(2)}, u32[]{:S(2)}) collective-permute-start(f32[4,8,1,768]{3,1,2,0:T(8,128)S(1)} %get-tuple-element.26), channel_id=1, source_target_pairs={{0,1},{1,2},{2,3},{3,4},{4,5},{5,6},{6,7},{7,8},{8,9},{9,10},{10,1... | collective-permute-start | bytes 294920 | tf_op jit(solution)/shard_map/ppermute | solution.py:17
  84.1 10.6 %copy-start.2 = (s32[64,128]{1,0:T(8,128)S(1)}, s32[64,128]{1,0:T(8,128)}, u32[]{:S(2)}) copy-start(s32[64,128]{1,0:T(8,128)} %param.23) | copy-start | bytes 98308
  84.1 40.8 %all-to-all-start.1 = ((f32[128,5,512]{2,1,0:T(8,128)}), f32[128,5,512]{2,1,0:T(8,128)}, u32[]{:S(2)}, u32[]{:S(2)}) async-start(f32[128,5,512]{2,1,0:T(8,128)} %copy.69), calls=%async_computation.1 | async-start | bytes 4194304 | tf_op jit(solution)/shard_map/all_to_all | solution.py:95
  133.0 1.0 copy-start.1
  135.5 24.2 %all-to-all-start.2 = ((bf16[128,5,512]{2,1,0:T(8,128)(2,1)}), bf16[128,5,512]{2,1,0:T(8,128)(2,1)S(1)}, u32[]{:S(2)}, u32[]{:S(2)}) async-start(bf16[128,5,512]{2,1,0:T(8,128)(2,1)} %reshape.151), calls=%async_computation.2 | async-start | bytes 2097152 | tf_op jit(solution)/shard_map/all_to_all | solution.py:131
where the time goes:
time: 170 us; the launch traced here: 169 us
  starting transfers between devices  51.7 us (30%)
  waiting for transfers between devices  51.3 us (30%)
  local copies, waits for them, and re-layouts  31 us (18%)
  matrix products  22.4 us (13%)
  other arithmetic  11.7 us (7%)
    all_to_all x1, waiting for transfers between devices, shards(): lax.all_to_all(outgoing.reshape(devices, capacity, fields * block_size),...  26.4 us
    all_to_all x1, waiting for transfers between devices, shards(): lax.all_to_all(returning.reshape(devices, capacity, fields * block_size),...  17.3 us
    ppermute x6, starting transfers between devices, padded(): lax.ppermute(tail, axis, [(i, (i + 1) % count) for i in range(ends)])  16 us
    ppermute x6, starting transfers between devices, padded(): lax.ppermute(head, axis, [((i + 1) % count, i) for i in range(ends)])  11.3 us
    all_to_all x1, starting transfers between devices, shards(): lax.all_to_all(outgoing.reshape(devices, capacity, fields * block_size),...  10.6 us
    all_to_all x1, starting transfers between devices, shards(): lax.all_to_all(outgoing_offset.reshape(devices, capacity), ('face', 'tile...  8.99 us
    add x3, other arithmetic, advance(): air_state - along_x * (air_state - west_cells)  8.43 us
    dot_general x1, matrix products, shards(): jnp.einsum('jfm,jkm->jfk', back_tiles, remap_tiles, preferred_element_typ...  7.4 us
  transfers between devices with their start and end apart: 15, of which 7 were waited for; matrix products, arithmetic and copies ran while one was open for 24% of the time, Pallas kernels for 0%

commit v1 on v0

v1 whole, which is shorter than its diff:
```python
import functools

import jax
import jax.numpy as jnp
from jax import lax
from jax.experimental import pallas as pl
from jax.experimental.pallas import tpu as pltpu
from jax.sharding import PartitionSpec as P

STEPS = 3
FIELDS, LEVELS, ROWS, COLS, BLK = 4, 8, 24, 768, 128
PLANES = 36
ENTRIES, DEVICES, CAP, OCEAN_ROWS = 288, 128, 5, 64
CHUNK = 22
BACK = CAP * FIELDS
GROUP = 36
f32, bf16 = jnp.float32, jnp.bfloat16


def iota(shape, dim):
    return lax.broadcasted_iota(jnp.int32, shape, dim)


def roll(x, shift, axis):
    shift = shift % x.shape[axis]
    return pltpu.roll(x, shift, axis) if shift else x


def params(mib=48):
    return pltpu.CompilerParams(vmem_limit_bytes=mib << 20)


def pack_rows(air_ref, cour_ref, out_ref, at_top):
    sub = iota((8, COLS), 0)
    first = 0 if at_top else 3

    def rows(p):
        if p < 32:
            return air_ref[p // LEVELS, p % LEVELS]
        if p < 35:
            return cour_ref[p - 32]
        return jnp.zeros((8, COLS), f32)

    def pair(p):
        return jnp.where(sub < 4, roll(rows(p), first, 0), roll(rows(p + 1), first + 4, 0))

    for p in range(0, PLANES, 4):
        out_ref[p * 4 : p * 4 + 16, :] = jnp.concatenate([pair(p), pair(p + 2)], 0).astype(bf16)


def row_kernel(top_air, bot_air, top_cour, bot_cour, sib_ref, nxt_ref):
    odd = lax.axis_index("tile") % 2

    @pl.when(odd == 1)
    def _():
        pack_rows(top_air, top_cour, sib_ref, True)
        pack_rows(bot_air, bot_cour, nxt_ref, False)

    @pl.when(odd == 0)
    def _():
        pack_rows(bot_air, bot_cour, sib_ref, False)
        pack_rows(top_air, top_cour, nxt_ref, True)


def row_messages(air, courant):
    shape = jax.ShapeDtypeStruct((PLANES * 4, COLS), bf16)
    return pl.pallas_call(
        row_kernel,
        out_shape=(shape, shape),
        grid=(1,),
        in_specs=[
            pl.BlockSpec((FIELDS, LEVELS, 8, COLS), lambda i: (0, 0, 0, 0)),
            pl.BlockSpec((FIELDS, LEVELS, 8, COLS), lambda i: (0, 0, 2, 0)),
            pl.BlockSpec((3, 8, COLS), lambda i: (0, 0, 0)),
            pl.BlockSpec((3, 8, COLS), lambda i: (0, 2, 0)),
        ],
        out_specs=(pl.BlockSpec((PLANES * 4, COLS), lambda i: (0, 0)),) * 2,
        compiler_params=params(),
        cost_estimate=pl.CostEstimate(flops=400000, bytes_accessed=2000000, transcendentals=0),
        name="row_messages",
    )(air, air, courant, courant)


def halo_rows(north, south, plane):
    base = plane // 2 * 8
    n, s = north[base : base + 8], south[base : base + 8]
    sub = iota(n.shape, 0)
    if plane % 2:
        return jnp.where(sub < 3, roll(n, 4, 0), roll(s, 1, 0))
    return jnp.where(sub < 3, n, roll(s, 5, 0))


def north_south(sib, nxt):
    odd = lax.axis_index("tile") % 2 == 1
    a, b = sib[...].astype(f32), nxt[...].astype(f32)
    return jnp.where(odd, b, a), jnp.where(odd, a, b)


def strip_kernel(w_air, e_air, w_cour, e_cour, w_sib, w_nxt, e_sib, e_nxt, strip, coef, send_w, send_e):
    lane = iota((32, 128), 1)
    place = lane % 16
    for side, (air, cour, sib, nxt, send) in enumerate(
        ((w_air, w_cour, w_sib, w_nxt, send_w), (e_air, e_cour, e_sib, e_nxt, send_e))
    ):
        north, south = north_south(sib, nxt)
        own = lane < 6 if side == 0 else lane >= 122
        shift = 3 if side == 0 else 6

        def plane(p):
            rows = air[p // LEVELS, p % LEVELS] if p < 32 else cour[p - 32]
            whole = jnp.concatenate([rows, halo_rows(north, south, p)], 0)
            return jnp.where(own, whole, 0.0)

        middle = (place >= 3) & (place < 6)
        message = jnp.zeros((32, 128), f32)
        for f in range(FIELDS):
            total = roll(plane(f * LEVELS), shift, 1)
            for l in range(1, LEVELS):
                total = total + roll(plane(f * LEVELS + l), l * 16 + shift, 1)
            strip[side, f] = total
            message = message + roll(jnp.where(middle, total, 0.0), 3 * f - 3, 1)
        for k in range(3):
            total = roll(plane(32 + k), shift, 1)
            for s in (16, 32, 64):
                total = total + roll(total, s, 1)
            coef[side, k] = total
            message = message + roll(jnp.where(middle & (lane // 16 == k), total, 0.0), 9, 1)
        send[...] = message


def column_messages(air, courant, sib, nxt):
    message = jax.ShapeDtypeStruct((32, 128), f32)
    row_spec = lambda c: pl.BlockSpec((PLANES * 4, 128), lambda i: (0, c))
    return pl.pallas_call(
        strip_kernel,
        out_shape=(
            jax.ShapeDtypeStruct((2, FIELDS, 32, 128), f32),
            jax.ShapeDtypeStruct((2, 3, 32, 128), f32),
            message,
            message,
        ),
        grid=(1,),
        in_specs=[
            pl.BlockSpec((FIELDS, LEVELS, ROWS, 128), lambda i: (0, 0, 0, 0)),
            pl.BlockSpec((FIELDS, LEVELS, ROWS, 128), lambda i: (0, 0, 0, 5)),
            pl.BlockSpec((3, ROWS, 128), lambda i: (0, 0, 0)),
            pl.BlockSpec((3, ROWS, 128), lambda i: (0, 0, 5)),
            row_spec(0),
            row_spec(0),
            row_spec(5),
            row_spec(5),
        ],
        out_specs=(
            pl.BlockSpec((2, FIELDS, 32, 128), lambda i: (0, 0, 0, 0)),
            pl.BlockSpec((2, 3, 32, 128), lambda i: (0, 0, 0, 0)),
            pl.BlockSpec((32, 128), lambda i: (0, 0)),
            pl.BlockSpec((32, 128), lambda i: (0, 0)),
        ),
        compiler_params=params(),
        cost_estimate=pl.CostEstimate(flops=400000, bytes_accessed=1200000, transcendentals=0),
        name="column_messages",
    )(air, air, courant, courant, sib, nxt, sib, nxt)


def coefficients(cx, cy, kd):
    return 1.0 - cx - cy - 4.0 * kd, cx + kd, cy + kd, kd


def step(q, c):
    return (
        q * c[0]
        + roll(q, 1, 1) * c[1]
        + roll(q, 1, 0) * c[2]
        + (roll(q, -1, 1) + roll(q, -1, 0)) * c[3]
    )


def main_kernel(weights, air, cour, sib, nxt, cour_sib, cour_nxt, out, flux, coef):
    f = pl.program_id(0)

    @pl.when(f == 0)
    def _():
        north, south = north_south(cour_sib, cour_nxt)
        three = [jnp.concatenate([cour[k], halo_rows(north, south, k)], 0) for k in range(3)]
        for k, c in enumerate(coefficients(*three)):
            coef[k] = c

    north, south = north_south(sib, nxt)
    total = None
    for l in range(LEVELS):
        q = jnp.concatenate([air[0, l], halo_rows(north, south, l)], 0)
        for _ in range(STEPS):
            q = step(q, coef)
        out[0, l] = q[:ROWS]
        term = weights[f, l] * q[:ROWS]
        total = term if l == 0 else total + term
    total = total.astype(bf16).astype(f32)
    for c in range(COLS // BLK):
        flux[pl.ds(c * FIELDS + f, ROWS, stride=24), :] = total[:, c * BLK : (c + 1) * BLK]


def main_stencil(weights, air, courant, sib, nxt):
    rows = pl.BlockSpec((32, COLS), lambda f: (f, 0))
    tail = pl.BlockSpec((16, COLS), lambda f: (8, 0))
    return pl.pallas_call(
        main_kernel,
        out_shape=(
            jax.ShapeDtypeStruct((FIELDS, LEVELS, ROWS, COLS), f32),
            jax.ShapeDtypeStruct((ROWS * 24, BLK), f32),
        ),
        grid=(FIELDS,),
        in_specs=[
            pl.BlockSpec(memory_space=pltpu.SMEM),
            pl.BlockSpec((1, LEVELS, ROWS, COLS), lambda f: (f, 0, 0, 0)),
            pl.BlockSpec((3, ROWS, COLS), lambda f: (0, 0, 0)),
            rows,
            rows,
            tail,
            tail,
        ],
        out_specs=(
            pl.BlockSpec((1, LEVELS, ROWS, COLS), lambda f: (f, 0, 0, 0)),
            pl.BlockSpec((ROWS * 24, BLK), lambda f: (0, 0)),
        ),
        scratch_shapes=[pltpu.VMEM((4, 32, COLS), f32)],
        compiler_params=params(),
        cost_estimate=pl.CostEstimate(flops=30000000, bytes_accessed=6000000, transcendentals=0),
        name="main_stencil",
    )(weights, air, courant, sib, nxt, sib, nxt)


def fix_edges(weights, strip, coef, from_w, from_e, fixed, flux):
    lane = iota((32, 128), 1)
    place = lane % 16
    for side, received in enumerate((from_w, from_e)):
        got = received[...]
        first = 0 if side == 0 else 6
        here = (place >= first) & (place < first + 3)
        three = []
        for k in range(3):
            c = jnp.where((lane // 16 == k) & (place >= 12) & (place < 15), got, 0.0)
            c = roll(c, first - 12, 1)
            for s in (16, 32, 64):
                c = c + roll(c, s, 1)
            three.append(jnp.where(here, c, coef[side, k]))
        coefs = coefficients(*three)
        for f in range(FIELDS):
            q = jnp.where(here, roll(got, first - 3 * f, 1), strip[side, f])
            for _ in range(STEPS):
                q = step(q, coefs)
            q = q[:ROWS]
            fixed[side, f] = q
            scale = jnp.zeros((1, 128), f32)
            for l in range(LEVELS):
                scale = jnp.where(iota((1, 128), 1) // 16 == l, weights[f, l], scale)
            total = q * scale
            for s in (64, 32, 16):
                total = total + roll(total, s, 1)
            total = total.astype(bf16).astype(f32)
            column = iota((ROWS, 128), 1)
            at = pl.ds(8 + f + (0 if side == 0 else 20), ROWS, stride=24)
            if side == 0:
                flux[at, :] = jnp.where(column < 3, roll(total, -3, 1), flux[at, :])
            else:
                flux[at, :] = jnp.where(column >= 125, roll(total, 122, 1), flux[at, :])


def block_rows(ref, at, low):
    half = iota((8, BLK), 0) < 4
    if low:
        return jnp.where(half, ref[pl.ds(at + 8, 8), :], 0.0)
    return jnp.where(half, 0.0, ref[pl.ds(at + 4, 8), :])


def four_rows(ref, at):
    left = jnp.concatenate([block_rows(ref, at[0], True), block_rows(ref, at[2], True)], 0)
    right = jnp.concatenate([block_rows(ref, at[1], False), block_rows(ref, at[3], False)], 0)
    return jnp.concatenate([left, right], 1).astype(bf16)


def four_results(r):
    return r[0:4, :BLK], r[4:8, :BLK], r[8:12, BLK:], r[12:16, BLK:]


def send_kernel(
    src, row, weights, flux_in, strip, coef, from_w, from_e, offsets, tiles, out, fixed, flux, total
):
    g = pl.program_id(0)

    @pl.when(g == 0)
    def _():
        flux[0:8, :] = jnp.zeros((8, BLK), f32)
        flux[8 : 8 + ROWS * 24, :] = flux_in[...]
        flux[8 + ROWS * 24 :, :] = jnp.zeros((8, BLK), f32)
        fix_edges(weights, strip, coef, from_w, from_e, fixed, flux)
        total[...] = jnp.zeros(total.shape, f32)
        total[pl.ds(BACK, DEVICES, stride=CHUNK), :] = offsets[...]

    for t in range(0, GROUP, 4):
        at = [src[g * GROUP + t + i] for i in range(4)]
        w = jnp.concatenate(
            [
                jnp.concatenate([tiles[t], tiles[t + 1]], 0),
                jnp.concatenate([tiles[t + 2], tiles[t + 3]], 0),
            ],
            1,
        )
        r = jnp.dot(four_rows(flux, at), w, preferred_element_type=f32)
        for i, piece in enumerate(four_results(r)):
            total[pl.ds(row[g * GROUP + t + i], 4), :] = piece

    @pl.when(g == ENTRIES // GROUP - 1)
    def _():
        out[...] = total[...].astype(bf16)


def send_blocks(src, row, weights, flux, strip, coef, from_w, from_e, offsets, tiles):
    whole = lambda *shape: pl.BlockSpec(shape, lambda g: (0,) * len(shape))
    smem = pl.BlockSpec(memory_space=pltpu.SMEM)
    return pl.pallas_call(
        send_kernel,
        out_shape=(
            jax.ShapeDtypeStruct((DEVICES * CHUNK, BLK), bf16),
            jax.ShapeDtypeStruct((2, FIELDS, ROWS, 128), f32),
        ),
        grid=(ENTRIES // GROUP,),
        in_specs=[
            smem,
            smem,
            smem,
            whole(ROWS * 24, BLK),
            whole(2, FIELDS, 32, 128),
            whole(2, 3, 32, 128),
            whole(32, 128),
            whole(32, 128),
            whole(DEVICES, 128),
            pl.BlockSpec((GROUP, BLK, BLK), lambda g: (g, 0, 0)),
        ],
        out_specs=(whole(DEVICES * CHUNK, BLK), whole(2, FIELDS, ROWS, 128)),
        scratch_shapes=[
            pltpu.VMEM((ROWS * 24 + 16, BLK), f32),
            pltpu.VMEM((DEVICES * CHUNK, BLK), f32),
        ],
        compiler_params=params(),
        cost_estimate=pl.CostEstimate(flops=40000000, bytes_accessed=11000000, transcendentals=0),
        name="send_blocks",
    )(src, row, weights, flux, strip, coef, from_w, from_e, offsets, tiles)


def patch_kernel(fixed, air, out):
    column = iota((ROWS, 128), 1)

    def patch(west):
        for f in range(FIELDS):
            q = fixed[0, f]
            for l in range(LEVELS):
                first = 0 if west else 125
                new = roll(q, first - (l * 16 + 3), 1)
                keep = column >= 3 if west else column < 125
                out[f, l] = jnp.where(keep, air[f, l], new)

    @pl.when(pl.program_id(0) == 0)
    def _():
        patch(True)

    @pl.when(pl.program_id(0) == 1)
    def _():
        patch(False)


def patch_columns(fixed, air):
    lanes = pl.BlockSpec((FIELDS, LEVELS, ROWS, 128), lambda i: (0, 0, 0, 5 * i))
    return pl.pallas_call(
        patch_kernel,
        out_shape=jax.ShapeDtypeStruct(air.shape, f32),
        grid=(2,),
        in_specs=[pl.BlockSpec((1, FIELDS, ROWS, 128), lambda i: (i, 0, 0, 0)), lanes],
        out_specs=lanes,
        input_output_aliases={1: 0},
        compiler_params=params(),
        cost_estimate=pl.CostEstimate(flops=400000, bytes_accessed=1600000, transcendentals=0),
        name="patch_columns",
    )(fixed, air)


def ocean_kernel(payload, ocean, mixing, mask, out, back, got, ret):
    got[...] = payload[...].astype(f32)
    offsets = got[pl.ds(BACK, DEVICES, stride=CHUNK), :]
    by_slot = offsets.T
    blocks = iota((OCEAN_ROWS, DEVICES), 0).astype(f32)
    flux = None
    for j in range(CAP):
        place = (by_slot[j : j + 1, :] == blocks).astype(f32).astype(bf16)
        data = jnp.concatenate(
            [got[pl.ds(j * FIELDS + f, DEVICES, stride=CHUNK), :] for f in range(FIELDS)], 1
        ).astype(bf16)
        part = jnp.dot(place, data, preferred_element_type=f32)
        flux = part if j == 0 else flux + part
    wet = mask[...].astype(f32)
    mix = wet * mixing[...]
    surface = []
    for f in range(FIELDS):
        q = [ocean[f, l] for l in range(8)]
        q[0] = q[0] + wet * flux[:, f * BLK : (f + 1) * BLK]
        for l in range(8):
            new = q[l] + mix * (q[max(l - 1, 0)] + q[min(l + 1, 7)] - 2.0 * q[l])
            out[f, l] = new
            if l == 0:
                surface.append((wet * new).astype(bf16))
    surface = jnp.concatenate(surface, 1)
    lanes = iota((DEVICES, OCEAN_ROWS), 1).astype(f32)
    for j in range(CAP):
        pick = (offsets[:, j : j + 1] == lanes).astype(f32).astype(bf16)
        rows = jnp.dot(pick, surface, preferred_element_type=f32)
        for f in range(FIELDS):
            ret[pl.ds(j * FIELDS + f, DEVICES, stride=BACK), :] = rows[:, f * BLK : (f + 1) * BLK]
    back[...] = ret[...].astype(bf16)


def ocean_step(payload, ocean, mixing, mask):
    return pl.pallas_call(
        ocean_kernel,
        out_shape=(
            jax.ShapeDtypeStruct(ocean.shape, f32),
            jax.ShapeDtypeStruct((DEVICES * BACK, BLK), bf16),
        ),
        scratch_shapes=[
            pltpu.VMEM((DEVICES * CHUNK, BLK), f32),
            pltpu.VMEM((DEVICES * BACK, BLK), f32),
        ],
        compiler_params=params(),
        cost_estimate=pl.CostEstimate(flops=100000000, bytes_accessed=4000000, transcendentals=0),
        name="ocean_step",
    )(payload, ocean, mixing, mask)


def return_kernel(src, row, payload, tiles, out, got, total):
    g = pl.program_id(0)

    @pl.when(g == 0)
    def _():
        got[0:8, :] = jnp.zeros((8, BLK), f32)
        got[8 : 8 + DEVICES * BACK, :] = payload[...].astype(f32)
        got[8 + DEVICES * BACK :, :] = jnp.zeros((8, BLK), f32)
        total[...] = jnp.zeros(total.shape, f32)

    for t in range(0, GROUP, 4):
        at = [row[g * GROUP + t + i] for i in range(4)]
        w = jnp.concatenate(
            [
                jnp.concatenate([tiles[t], tiles[t + 1]], 1),
                jnp.concatenate([tiles[t + 2], tiles[t + 3]], 1),
            ],
            0,
        )
        r = lax.dot_general(
            four_rows(got, at), w, (((1,), (1,)), ((), ())), preferred_element_type=f32
        )
        for i, piece in enumerate(four_results(r)):
            here = pl.ds(src[g * GROUP + t + i], 4)
            total[here, :] = total[here, :] + piece

    @pl.when(g == ENTRIES // GROUP - 1)
    def _():
        for f in range(FIELDS):
            for c in range(COLS // BLK):
                out[f, :, c * BLK : (c + 1) * BLK] = total[pl.ds(c * FIELDS + f, ROWS, stride=24), :]


def return_blocks(src, row, payload, tiles):
    smem = pl.BlockSpec(memory_space=pltpu.SMEM)
    return pl.pallas_call(
        return_kernel,
        out_shape=jax.ShapeDtypeStruct((FIELDS, ROWS, COLS), f32),
        grid=(ENTRIES // GROUP,),
        in_specs=[
            smem,
            smem,
            pl.BlockSpec((DEVICES * BACK, BLK), lambda g: (0, 0)),
            pl.BlockSpec((GROUP, BLK, BLK), lambda g: (g, 0, 0)),
        ],
        out_specs=pl.BlockSpec((FIELDS, ROWS, COLS), lambda g: (0, 0, 0)),
        scratch_shapes=[
            pltpu.VMEM((DEVICES * BACK + 16, BLK), f32),
            pltpu.VMEM((ROWS * 24, BLK), f32),
        ],
        compiler_params=params(),
        cost_estimate=pl.CostEstimate(flops=40000000, bytes_accessed=11000000, transcendentals=0),
        name="return_blocks",
    )(src, row, payload, tiles)


def routes(src_block, owner, offset, tile_index):
    ids = jnp.arange(ENTRIES, dtype=jnp.int32)
    pick = tile_index[0][:, None] == ids[None, :]
    by_tile = lambda v: jnp.sum(jnp.where(pick, v[:, None], 0), axis=0)
    src, dest, place = by_tile(src_block[0]), by_tile(owner[0, :, 0]), by_tile(offset[0])
    earlier = (ids[None, :] < ids[:, None]) & (dest[:, None] == dest[None, :])
    rank = jnp.sum(earlier.astype(jnp.int32), axis=1)
    devices = jnp.arange(DEVICES, dtype=jnp.int32)
    to_dest = (devices[:, None] == dest[None, :]).astype(bf16)
    at_rank = jnp.where(rank[:, None] == devices[None, :], (place + 1)[:, None], 0).astype(bf16)
    offsets = jnp.dot(to_dest, at_rank, preferred_element_type=f32) - 1.0
    return src * FIELDS, dest * CHUNK + rank * FIELDS, dest * BACK + rank * FIELDS, offsets


def exchange(x, rows):
    x = x.reshape(DEVICES * CAP, rows // CAP, BLK) if rows == BACK else x.reshape(-1, 2, BLK)
    x = lax.all_to_all(x, ("face", "tile"), split_axis=0, concat_axis=0, tiled=True)
    return x.reshape(DEVICES * rows, BLK)


def shards(
    atmos_state,
    courant,
    level_weights,
    remap_tiles,
    src_block,
    owner,
    offset,
    tile_index,
    ocean_state,
    mixing,
    land_mask,
):
    faces, tile_count = lax.axis_size("face"), lax.axis_size("tile")
    sib, nxt = row_messages(atmos_state, courant)
    sib = lax.ppermute(sib, "tile", [(i, i ^ 1) for i in range(tile_count)])
    inner = [(i, i + 1) for i in range(1, tile_count - 1, 2)]
    nxt = lax.ppermute(nxt, "tile", inner + [(b, a) for a, b in inner])
    src, out_row, back_row, offsets = routes(src_block, owner, offset, tile_index)
    strip, coef, send_w, send_e = column_messages(atmos_state, courant, sib, nxt)
    from_e = lax.ppermute(send_w, "face", [((i + 1) % faces, i) for i in range(faces)])
    from_w = lax.ppermute(send_e, "face", [(i, (i + 1) % faces) for i in range(faces)])
    air, flux = main_stencil(level_weights, atmos_state, courant, sib, nxt)
    message, fixed = send_blocks(
        src, out_row, level_weights, flux, strip, coef, from_w, from_e, offsets, remap_tiles
    )
    message = exchange(message, CHUNK)
    air_state = patch_columns(fixed, air)
    ocean_out, back = ocean_step(message, ocean_state, mixing, land_mask)
    back = exchange(back, BACK)
    atmos_surface = return_blocks(src, back_row, back, remap_tiles)
    return air_state, ocean_out, atmos_surface


def solution(mesh):
    return jax.shard_map(
        shards,
        mesh=mesh,
        in_specs=(
            P(None, None, "tile", "face"),
            P(None, "tile", "face"),
            P(),
            P(("face", "tile"), None, None),
            P(("face", "tile"), None),
            P(("face", "tile"), None, None),
            P(("face", "tile"), None),
            P(("face", "tile"), None),
            P(None, None, "face", "tile"),
            P("face", "tile"),
            P("face", "tile"),
        ),
        out_specs=(
            P(None, None, "tile", "face"),
            P(None, None, "face", "tile"),
            P(None, "tile", "face"),
        ),
        check_vma=False,
    )
```

time: 170 us -> 91.1 us (0.54)
  starting transfers between devices: 51.7 us -> 12.5 us
  waiting for transfers between devices: 51.3 us -> 16.1 us
  Pallas kernels: 0 us -> 31.4 us
  local copies, waits for them, and re-layouts: 31 us -> 2.64 us
  blocking collectives: 0 us -> 26.3 us
  matrix products: 22.4 us -> 0.29 us
  other arithmetic: 11.7 us -> 0.55 us
    pallas_call x0 -> x7, Pallas kernels: none -> 31.4 us  [the longest x1 9.72 us: main_stencil(): pl.pallas_call(main_kernel, out_shape=(jax.ShapeDtypeStruct((FIELDS, LEVE...]
    all_to_all x3 -> x1, waiting for transfers between devices: 43.7 us -> 13.1 us  [exchange(): lax.all_to_all(x, ('face', 'tile'), split_axis=0, concat_axis=0, tiled=True)]
    all_to_all x0 -> x1, blocking collectives: none -> 26.3 us  [exchange(): lax.all_to_all(x, ('face', 'tile'), split_axis=0, concat_axis=0, tiled=True)]
    dot_general x8 -> x1, matrix products: 22.4 us -> 0.29 us  [routes(): offsets = jnp.dot(to_dest, at_rank, preferred_element_type=f32) - 1.0]
    all_to_all x3 -> x1, starting transfers between devices: 24.4 us -> 4.58 us  [exchange(): lax.all_to_all(x, ('face', 'tile'), split_axis=0, concat_axis=0, tiled=True)]
    ppermute x12 -> x4, starting transfers between devices: 27.3 us -> 7.9 us  [the longest x1 3.66 us: shards(): nxt = lax.ppermute(nxt, 'tile', inner + [(b, a) for a, b in inner])]
    reshape x8 -> x0, local copies, waits for them, and re-layouts: 10.3 us -> none  [the longest x2 3.34 us: shards(): flux_blocks = air_flux.reshape(fields, -1, block_size)]
    add x5 -> x1, other arithmetic: 8.79 us -> 0.01 us  [routes(): dest * BACK + rank * FIELDS]
  transfers between devices with their start and end apart: 15 -> 5, of which waited for: 7 -> 2; matrix products, arithmetic and copies ran while one was open for 24% -> 1% of each run, Pallas kernels for 0% -> 13%
where the time goes in v1:
time: 91.1 us; the launch traced here: 90.6 us
  Pallas kernels  31.4 us (34%)
  blocking collectives  26.3 us (29%)
  waiting for transfers between devices  16.1 us (18%)
  starting transfers between devices  12.5 us (14%)
  local copies, waits for them, and re-layouts  2.64 us (3%)
    all_to_all x1, blocking collectives, exchange(): lax.all_to_all(x, ('face', 'tile'), split_axis=0, concat_axis=0, tiled=True)  26.3 us
    all_to_all x1, waiting for transfers between devices, exchange(): lax.all_to_all(x, ('face', 'tile'), split_axis=0, concat_axis=0, tiled=True)  13.1 us
    pallas_call x1, Pallas kernels, main_stencil(): pl.pallas_call(main_kernel, out_shape=(jax.ShapeDtypeStruct((FIELDS, LEVE...  9.72 us
    pallas_call x1, Pallas kernels, return_blocks(): pl.pallas_call(return_kernel, out_shape=jax.ShapeDtypeStruct((FIELDS, ROW...  8.59 us
    pallas_call x1, Pallas kernels, send_blocks(): pl.pallas_call(send_kernel, out_shape=(jax.ShapeDtypeStruct((DEVICES * CH...  7.97 us
    all_to_all x1, starting transfers between devices, exchange(): lax.all_to_all(x, ('face', 'tile'), split_axis=0, concat_axis=0, tiled=True)  4.58 us
    ppermute x1, starting transfers between devices, shards(): nxt = lax.ppermute(nxt, 'tile', inner + [(b, a) for a, b in inner])  3.66 us
    ppermute x1, waiting for transfers between devices, shards(): nxt = lax.ppermute(nxt, 'tile', inner + [(b, a) for a, b in inner])  2.98 us
  transfers between devices with their start and end apart: 5, of which 2 were waited for; matrix products, arithmetic and copies ran while one was open for 1% of the time, Pallas kernels for 13%

profile of v1, /device:TPU:1, one launch (start us, length us, event | category | flops | bytes accessed | tf_op | source)
XLA Modules:
  0.0 90.6 jit_solution(18283796357130338362)
XLA Ops:
  0.6 1.7 %copy-done = f32[4,8,24,768]{3,2,1,0:T(8,128)S(1)} copy-done((f32[4,8,24,768]{3,2,1,0:T(8,128)S(1)}, f32[4,8,24,768]{3,2,1,0:T(8,128)}, u32[]{:S(2)}) %copy-start) | copy-done | bytes 2359320
  2.3 0.9 %copy-done.2 = f32[3,24,768]{2,1,0:T(8,128)S(1)} copy-done((f32[3,24,768]{2,1,0:T(8,128)S(1)}, f32[3,24,768]{2,1,0:T(8,128)}, u32[]{:S(2)}) %copy-start.2) | copy-done | bytes 221208
  3.3 0.2 row_messages.1
  3.5 1.5 %collective-permute-start = (bf16[144,768]{1,0:T(8,128)(2,1)S(1)}, bf16[144,768]{1,0:T(8,128)(2,1)S(1)}, u32[]{:S(2)}, u32[]{:S(2)}) collective-permute-start(bf16[144,768]{1,0:T(8,128)(2,1)S(1)} %get-tuple-element.15), channel_id=1, source_target_pairs={{0,1},{1,0},{2,3},{3,2},{4,5},{5,4},{6,7},{7,6},{8,9},{9,8},{10,11... | collective-permute-start | bytes 663560 | tf_op jit(solution)/shard_map/ppermute | solution.py:528
  5.0 3.7 %collective-permute-start.1 = (bf16[144,768]{1,0:T(8,128)(2,1)S(1)}, bf16[144,768]{1,0:T(8,128)(2,1)S(1)}, u32[]{:S(2)}, u32[]{:S(2)}) collective-permute-start(bf16[144,768]{1,0:T(8,128)(2,1)S(1)} %get-tuple-element.16), channel_id=1, source_target_pairs={{1,2},{3,4},{5,6},{7,8},{9,10},{11,12},{13,14},{15,16},{17,18},{19... | collective-permute-start | bytes 663560 | tf_op jit(solution)/shard_map/ppermute | solution.py:530
  8.8 0.2 select_reduce_fusion
  9.0 0.2 convert_reduce_fusion
  9.2 0.3 convolution_add_fusion.offsets
  9.5 0.0 copy-start.7
  9.6 3.0 %collective-permute-done.1.nxt.cour_nxt.w_nxt.e_nxt = bf16[144,768]{1,0:T(8,128)(2,1)S(1)} collective-permute-done((bf16[144,768]{1,0:T(8,128)(2,1)S(1)}, bf16[144,768]{1,0:T(8,128)(2,1)S(1)}, u32[]{:S(2)}, u32[]{:S(2)}) %collective-permute-start.1) | collective-permute-done | bytes 221216 | tf_op jit(solution)/shard_map/ppermute | solution.py:530
  12.5 1.2 %column_messages.1 = (f32[2,4,32,128]{3,2,1,0:T(8,128)S(1)}, f32[2,3,32,128]{3,2,1,0:T(8,128)S(1)}, f32[32,128]{1,0:T(8,128)S(1)}, f32[32,128]{1,0:T(8,128)S(1)}) custom-call(f32[4,8,24,768]{3,2,1,0:T(8,128)S(1)} %copy-done.1, f32[4,8,24,768]{3,2,1,0:T(8,128)S(1)} %copy-done.1, f32[3,24,768]{2,1,0:T(8,128)S(1)} %copy-done.3, f32[3,24,768]{2,1,0:T(8,128)S(1)} %copy-done.3, ...), custom_call_target="tpu_custom_call" | custom-call | flops 400000 | bytes 1200000 | tf_op jit(solution)/shard_map/column_messages/pallas_call | solution.py:134
  13.7 1.0 %collective-permute-start.2 = (f32[32,128]{1,0:T(8,128)S(1)}, f32[32,128]{1,0:T(8,128)S(1)}, u32[]{:S(2)}, u32[]{:S(2)}) collective-permute-start(f32[32,128]{1,0:T(8,128)S(1)} %get-tuple-element.20), channel_id=1, source_target_pairs={{0,32},{32,64},{64,96},{96,0},{1,33},{33,65},{65,97},{97,1},{2,34}... | collective-permute-start | bytes 49160 | tf_op jit(solution)/shard_map/ppermute | solution.py:534
  14.8 1.7 %collective-permute-start.3 = (f32[32,128]{1,0:T(8,128)S(1)}, f32[32,128]{1,0:T(8,128)S(1)}, u32[]{:S(2)}, u32[]{:S(2)}) collective-permute-start(f32[32,128]{1,0:T(8,128)S(1)} %get-tuple-element.21), channel_id=1, source_target_pairs={{32,0},{64,32},{96,64},{0,96},{33,1},{65,33},{97,65},{1,97},{34,2}... | collective-permute-start | bytes 49160 | tf_op jit(solution)/shard_map/ppermute | solution.py:533
  16.5 9.7 %main_stencil.1 = (f32[4,8,24,768]{3,2,1,0:T(8,128)}, f32[576,128]{1,0:T(8,128)S(1)}) custom-call(f32[4,8]{1,0:T(4,128)S(1)} %copy-done.7, f32[4,8,24,768]{3,2,1,0:T(8,128)S(1)} %copy-done.1, f32[3,24,768]{2,1,0:T(8,128)S(1)} %copy-done.3, bf16[144,768]{1,0:T(8,128)(2,1)S(1)} %collective-permute-done.sib.cour_sib.w_sib.e_sib, ...), custom_call_target="tpu_custom_call" | custom-call | flops 30000000 | bytes 6000000 | tf_op jit(solution)/shard_map/main_stencil/pallas_call | solution.py:205
  26.2 0.0 collective-permute-done.2.from_w
  26.2 0.0 copy-start.5
  26.2 0.0 copy-start.6
  26.2 8.0 %send_blocks.1 = (bf16[2816,128]{1,0:T(8,128)(2,1)S(1)}, f32[2,4,24,128]{3,2,1,0:T(8,128)S(1)}) custom-call(s32[288]{0:T(512)S(1)} %broadcast_multiply_fusion.src, s32[288]{0:T(512)S(1)} %get-tuple-element.31.row, f32[4,8]{1,0:T(4,128)S(1)} %copy-done.7, f32[576,128]{1,0:T(8,128)S(1)} %get-tuple-element.17.flux_in, ...), custom_call_target="tpu_custom_call" | custom-call | flops 40000000 | bytes 11000000 | tf_op jit(solution)/shard_map/send_blocks/pallas_call | solution.py:320
  34.2 26.3 %all_to_all.10 = bf16[1408,2,128]{2,1,0:T(2,128)(2,1)S(1)} all-to-all(bf16[1408,2,128]{2,1,0:T(2,128)(2,1)S(1)} %bitcast.6), channel_id=1, replica_groups=mesh['face'=4,'tile'=32] {'face','tile'}, dimensions={0} | all-to-all | bytes 1441792 | tf_op jit(solution)/shard_map/all_to_all | solution.py:509
  60.6 1.7 %ocean_step.1 = (f32[4,8,64,128]{3,2,1,0:T(8,128)}, bf16[2560,128]{1,0:T(8,128)(2,1)}) custom-call(bf16[2816,128]{1,0:T(8,128)(2,1)S(1)} %bitcast.4, f32[4,8,64,128]{3,2,1,0:T(8,128)S(1)} %copy-done.4, f32[64,128]{1,0:T(8,128)S(1)} %copy-done.5, s32[64,128]{1,0:T(8,128)S(1)} %copy-done.6), custom_call_target="tpu_custom_call" | custom-call | flops 100000000 | bytes 4000000 | tf_op jit(solution)/shard_map/ocean_step/pallas_call | solution.py:421
  62.2 4.6 %all-to-all-start.1 = ((bf16[640,4,128]{2,1,0:T(4,128)(2,1)}), bf16[640,4,128]{2,1,0:T(4,128)(2,1)S(1)}, u32[]{:S(2)}, u32[]{:S(2)}) async-start(bf16[640,4,128]{2,1,0:T(4,128)(2,1)} %bitcast.2), calls=%async_computation.1 | async-start | bytes 1310720 | tf_op jit(solution)/shard_map/all_to_all | solution.py:509
  66.8 2.1 %patch_columns.1 = f32[4,8,24,768]{3,2,1,0:T(8,128)} custom-call(f32[2,4,24,128]{3,2,1,0:T(8,128)S(1)} %get-tuple-element.22.fixed, f32[4,8,24,768]{3,2,1,0:T(8,128)} %get-tuple-element.23.air), custom_call_target="tpu_custom_call", output_to_operand_aliasing={{}: (1, {})} | custom-call | flops 400000 | bytes 1600000 | tf_op jit(solution)/shard_map/patch_columns/pallas_call | solution.py:373
  68.9 13.1 %all-to-all-done.1 = bf16[640,4,128]{2,1,0:T(4,128)(2,1)S(1)} async-done(((bf16[640,4,128]{2,1,0:T(4,128)(2,1)}), bf16[640,4,128]{2,1,0:T(4,128)(2,1)S(1)}, u32[]{:S(2)}, u32[]{:S(2)}) %all-to-all-start.1) | async-done | bytes 655392 | tf_op jit(solution)/shard_map/all_to_all | solution.py:509
  82.0 8.6 %return_blocks.1 = f32[4,24,768]{2,1,0:T(8,128)} custom-call(s32[288]{0:T(512)S(1)} %broadcast_multiply_fusion.src, s32[288]{0:T(512)S(1)} %get-tuple-element.30.row, bf16[2560,128]{1,0:T(8,128)(2,1)S(1)} %bitcast.5, bf16[288,128,128]{2,1,0:T(8,128)(2,1)} %tiles.3), custom_call_target="tpu_custom_call" | custom-call | flops 40000000 | bytes 11000000 | tf_op jit(solution)/shard_map/return_blocks/pallas_call | solution.py:472
  (27 shorter events, 0.1 us)
Async XLA Ops:
  0.6 1.7 %copy-start = (f32[4,8,24,768]{3,2,1,0:T(8,128)S(1)}, f32[4,8,24,768]{3,2,1,0:T(8,128)}, u32[]{:S(2)}) copy-start(f32[4,8,24,768]{3,2,1,0:T(8,128)} %e_air.1) | copy-start | bytes 7077892
  2.3 0.9 %copy-start.2 = (f32[3,24,768]{2,1,0:T(8,128)S(1)}, f32[3,24,768]{2,1,0:T(8,128)}, u32[]{:S(2)}) copy-start(f32[3,24,768]{2,1,0:T(8,128)} %e_cour.1) | copy-start | bytes 663556
  3.2 5.4 %copy-start.8 = (s32[1,288]{1,0:T(1,128)S(1)}, s32[1,288]{1,0:T(1,128)}, u32[]{:S(2)}) copy-start(s32[1,288]{1,0:T(1,128)} %param.15) | copy-start | bytes 3460
  3.2 5.4 %copy-start.9 = (s32[1,288,1]{1,2,0:T(1,128)S(1)}, s32[1,288,1]{1,2,0:T(1,128)}, u32[]{:S(2)}) copy-start(s32[1,288,1]{1,2,0:T(1,128)} %param.16) | copy-start | bytes 3460
  3.2 5.5 %copy-start.10 = (s32[1,288]{1,0:T(1,128)S(1)}, s32[1,288]{1,0:T(1,128)}, u32[]{:S(2)}) copy-start(s32[1,288]{1,0:T(1,128)} %param.17) | copy-start | bytes 3460
  3.2 5.5 %copy-start.11 = (s32[1,288]{1,0:T(1,128)S(1)}, s32[1,288]{1,0:T(1,128)}, u32[]{:S(2)}) copy-start(s32[1,288]{1,0:T(1,128)} %param.18) | copy-start | bytes 3460
  3.2 9.3 %copy-start.1 = (f32[4,8,24,768]{3,2,1,0:T(8,128)S(1)}, f32[4,8,24,768]{3,2,1,0:T(8,128)}, u32[]{:S(2)}) copy-start(f32[4,8,24,768]{3,2,1,0:T(8,128)} %e_air.1) | copy-start | bytes 7077892
  3.3 9.3 %copy-start.3 = (f32[3,24,768]{2,1,0:T(8,128)S(1)}, f32[3,24,768]{2,1,0:T(8,128)}, u32[]{:S(2)}) copy-start(f32[3,24,768]{2,1,0:T(8,128)} %e_cour.1) | copy-start | bytes 663556
  3.5 6.1 %collective-permute-start = (bf16[144,768]{1,0:T(8,128)(2,1)S(1)}, bf16[144,768]{1,0:T(8,128)(2,1)S(1)}, u32[]{:S(2)}, u32[]{:S(2)}) collective-permute-start(bf16[144,768]{1,0:T(8,128)(2,1)S(1)} %get-tuple-element.15), channel_id=1, source_target_pairs={{0,1},{1,0},{2,3},{3,2},{4,5},{5,4},{6,7},{7,6},{8,9},{9,8},{10,11... | collective-permute-start | bytes 663560 | tf_op jit(solution)/shard_map/ppermute | solution.py:528
  5.0 7.6 %collective-permute-start.1 = (bf16[144,768]{1,0:T(8,128)(2,1)S(1)}, bf16[144,768]{1,0:T(8,128)(2,1)S(1)}, u32[]{:S(2)}, u32[]{:S(2)}) collective-permute-start(bf16[144,768]{1,0:T(8,128)(2,1)S(1)} %get-tuple-element.16), channel_id=1, source_target_pairs={{1,2},{3,4},{5,6},{7,8},{9,10},{11,12},{13,14},{15,16},{17,18},{19... | collective-permute-start | bytes 663560 | tf_op jit(solution)/shard_map/ppermute | solution.py:530
  9.5 6.9 %copy-start.7 = (f32[4,8]{1,0:T(4,128)S(1)}, f32[4,8]{1,0:T(4,128)}, u32[]{:S(2)}) copy-start(f32[4,8]{1,0:T(4,128)} %weights.3) | copy-start | bytes 388
  13.7 12.5 %collective-permute-start.2 = (f32[32,128]{1,0:T(8,128)S(1)}, f32[32,128]{1,0:T(8,128)S(1)}, u32[]{:S(2)}, u32[]{:S(2)}) collective-permute-start(f32[32,128]{1,0:T(8,128)S(1)} %get-tuple-element.20), channel_id=1, source_target_pairs={{0,32},{32,64},{64,96},{96,0},{1,33},{33,65},{65,97},{97,1},{2,34}... | collective-permute-start | bytes 49160 | tf_op jit(solution)/shard_map/ppermute | solution.py:534
  14.8 11.4 %collective-permute-start.3 = (f32[32,128]{1,0:T(8,128)S(1)}, f32[32,128]{1,0:T(8,128)S(1)}, u32[]{:S(2)}, u32[]{:S(2)}) collective-permute-start(f32[32,128]{1,0:T(8,128)S(1)} %get-tuple-element.21), channel_id=1, source_target_pairs={{32,0},{64,32},{96,64},{0,96},{33,1},{65,33},{97,65},{1,97},{34,2}... | collective-permute-start | bytes 49160 | tf_op jit(solution)/shard_map/ppermute | solution.py:533
  26.2 34.3 %copy-start.4 = (f32[4,8,64,128]{3,2,1,0:T(8,128)S(1)}, f32[4,8,64,128]{3,2,1,0:T(8,128)}, u32[]{:S(2)}) copy-start(f32[4,8,64,128]{3,2,1,0:T(8,128)} %ocean.1) | copy-start | bytes 3145732
  26.2 34.3 %copy-start.5 = (f32[64,128]{1,0:T(8,128)S(1)}, f32[64,128]{1,0:T(8,128)}, u32[]{:S(2)}) copy-start(f32[64,128]{1,0:T(8,128)} %mixing.1) | copy-start | bytes 98308
  26.2 34.3 %copy-start.6 = (s32[64,128]{1,0:T(8,128)S(1)}, s32[64,128]{1,0:T(8,128)}, u32[]{:S(2)}) copy-start(s32[64,128]{1,0:T(8,128)} %mask.1) | copy-start | bytes 98308
  62.2 19.8 %all-to-all-start.1 = ((bf16[640,4,128]{2,1,0:T(4,128)(2,1)}), bf16[640,4,128]{2,1,0:T(4,128)(2,1)S(1)}, u32[]{:S(2)}, u32[]{:S(2)}) async-start(bf16[640,4,128]{2,1,0:T(4,128)(2,1)} %bitcast.2), calls=%async_computation.1 | async-start | bytes 1310720 | tf_op jit(solution)/shard_map/all_to_all | solution.py:509

commit v2 on v1

v2 whole, which is shorter than its diff:
```python
import jax
import jax.numpy as jnp
from jax import lax
from jax.experimental import pallas as pl
from jax.experimental.pallas import tpu as pltpu
from jax.sharding import PartitionSpec as P

STEPS = 3
FIELDS, LEVELS, ROWS, COLS, BLK = 4, 8, 24, 768, 128
MESSAGE = 112
ENTRIES, DEVICES, CAP, OCEAN_ROWS = 288, 128, 5, 64
CHUNK = 22
BACK = CAP * FIELDS
f32, bf16 = jnp.float32, jnp.bfloat16


def iota(shape, dim):
    return lax.broadcasted_iota(jnp.int32, shape, dim)


def roll(x, shift, axis):
    shift = shift % x.shape[axis]
    return pltpu.roll(x, shift, axis) if shift else x


def params(mib=16):
    return pltpu.CompilerParams(vmem_limit_bytes=mib << 20)


in_vmem = pl.BlockSpec(memory_space=pltpu.VMEM)
in_smem = pl.BlockSpec(memory_space=pltpu.SMEM)
in_hbm = pl.BlockSpec(memory_space=pltpu.HBM)


def hbm(*arrays):
    return [pltpu.with_memory_space_constraint(x, pltpu.HBM) for x in arrays]


def start_all(pairs, sems):
    copies = [pltpu.make_async_copy(a, b, sems.at[i]) for i, (a, b) in enumerate(pairs)]
    for copy in copies:
        copy.start()
    return copies


def wait_all(copies):
    for copy in copies:
        copy.wait()


def start_tiles(stored, tiles, sems, bounds):
    parts = [pl.ds(a, b - a) for a, b in zip(bounds, bounds[1:])]
    pairs = [(stored.at[part], tiles.at[part]) for part in parts]
    return dict(zip(bounds, start_all(pairs, sems)))


def row_kernel(air, cour, sib_ref, nxt_ref, top, bot, top_cour, bot_cour, sems):
    copies = []
    for c in range(COLS // BLK):
        lanes = pl.ds(c * BLK, BLK)
        copies.append((air.at[:, :, pl.ds(0, 8), lanes], top.at[c]))
        copies.append((air.at[:, :, pl.ds(16, 8), lanes], bot.at[c]))
    copies.append((cour.at[:, pl.ds(0, 8), :], top_cour))
    copies.append((cour.at[:, pl.ds(16, 8), :], bot_cour))
    copies = [pltpu.make_async_copy(a, b, sems.at[i]) for i, (a, b) in enumerate(copies)]
    for copy in copies:
        copy.start()
    for copy in copies:
        copy.wait()

    def pack(out, at_top):
        first = 0 if at_top else 5
        rows, numbers = (top, top_cour) if at_top else (bot, bot_cour)
        for c in range(COLS // BLK):
            flat = rows.at[c].reshape(FIELDS * LEVELS * 8, BLK)

            def tile(i):
                return flat[pl.ds(i // 3 * 64 + first + i % 3, LEVELS, stride=8), :]

            for i in range(0, FIELDS * 3, 2):
                both = jnp.concatenate([tile(i), tile(i + 1)], 0)
                out[i * 8 : i * 8 + 16, c * BLK : (c + 1) * BLK] = both.astype(bf16)
        sub = iota((8, COLS), 0)
        pair = jnp.where(sub < 4, roll(numbers[0], -first, 0), roll(numbers[1], 4 - first, 0))
        last = jnp.where(sub < 4, roll(numbers[2], -first, 0), 0.0)
        out[96:112, :] = jnp.concatenate([pair, last], 0).astype(bf16)

    odd = lax.axis_index("tile") % 2

    @pl.when(odd == 1)
    def _():
        pack(sib_ref, True)
        pack(nxt_ref, False)

    @pl.when(odd == 0)
    def _():
        pack(sib_ref, False)
        pack(nxt_ref, True)


def row_messages(air, courant):
    shape = jax.ShapeDtypeStruct((MESSAGE, COLS), bf16)
    return pl.pallas_call(
        row_kernel,
        out_shape=(shape, shape),
        in_specs=[in_hbm] * 2,
        out_specs=(in_vmem,) * 2,
        scratch_shapes=[pltpu.VMEM((COLS // BLK, FIELDS, LEVELS, 8, BLK), f32)] * 2
        + [pltpu.VMEM((3, 8, COLS), f32)] * 2
        + [pltpu.SemaphoreType.DMA((14,))],
        compiler_params=params(),
        cost_estimate=pl.CostEstimate(flops=400000, bytes_accessed=2000000, transcendentals=0),
        name="row_messages",
    )(*hbm(air, courant))


def courant_rows(north, south, k):
    base = k // 2 * 8
    n, s = north[base : base + 8], south[base : base + 8]
    sub = iota(n.shape, 0)
    if k % 2:
        return jnp.where(sub < 3, roll(n, 4, 0), roll(s, 1, 0))
    return jnp.where(sub < 3, n, roll(s, 5, 0))


def halo_sum(weights, f, north, south):
    sub = iota((8, north.shape[1]), 0)
    scale = jnp.zeros(sub.shape, f32)
    for l in range(LEVELS):
        scale = jnp.where(sub == l, weights[f, l], scale)
    rows = jnp.zeros(sub.shape, f32)
    for j in range(3):
        at = slice((f * 3 + j) * 8, (f * 3 + j + 1) * 8)
        rows = jnp.where(sub == j, jnp.sum(north[at] * scale, axis=0, keepdims=True), rows)
        rows = jnp.where(sub == 5 + j, jnp.sum(south[at] * scale, axis=0, keepdims=True), rows)
    return rows


def north_south(sib, nxt):
    odd = lax.axis_index("tile") % 2 == 1
    a, b = sib.astype(f32), nxt.astype(f32)
    return jnp.where(odd, b, a), jnp.where(odd, a, b)


SHIFTS = (3, 6)


def edge_lanes(side):
    return slice(0, BLK) if side == 0 else slice(COLS - BLK, COLS)


def own_columns(side, rows):
    lane = iota((rows, 128), 1)
    return lane < 6 if side == 0 else lane >= 122


def gather_levels(level, shift):
    total = roll(level(0), shift, 1)
    for l in range(1, LEVELS):
        total = total + roll(level(l), l * 16 + shift, 1)
    return total


def spread(x):
    for s in (16, 32, 64):
        x = x + roll(x, s, 1)
    return x


def message_rows(strips, coefs, sums):
    lane = iota(strips[0].shape, 1)
    place = lane % 16
    middle = (place >= 3) & (place < 6)
    message = jnp.zeros(strips[0].shape, f32)
    for f in range(FIELDS):
        message = message + roll(jnp.where(middle, strips[f], 0.0), 3 * f - 3, 1)
    for k in range(3):
        mine = middle & (lane // 16 == k)
        message = message + roll(jnp.where(mine, coefs[k], 0.0), 9, 1)
    return message + roll(jnp.where(middle & (lane < 64), sums, 0.0), 57, 1)


def level_lanes(weights, f, rows):
    lane = iota((rows, 128), 1) // 16
    scale = jnp.zeros((rows, 128), f32)
    for l in range(LEVELS):
        scale = jnp.where(lane == l, weights[f, l], scale)
    return scale


def sum_strip(weights, strips):
    rows = strips[0].shape[0]
    group = iota((rows, 128), 1) // 16
    total = jnp.zeros((rows, 128), f32)
    for f in range(FIELDS):
        whole = spread(strips[f] * level_lanes(weights, f, rows))
        total = jnp.where(group == f, whole, total)
    return total


def route(src, owner, offset, tile_index, routes, offsets):
    row = lambda ref: ref[...].astype(f32)
    sub = iota((8, ENTRIES), 0)
    known = jnp.where(sub == 0, row(src), jnp.where(sub == 1, row(owner), row(offset))).astype(bf16)
    pick = (iota((ENTRIES, ENTRIES), 0) == tile_index[...]).astype(f32).astype(bf16)
    along = (((1,), (1,)), ((), ()))
    by_tile = lax.dot_general(known, pick, along, preferred_element_type=f32)
    down = lax.dot_general(pick, known, along, preferred_element_type=f32)
    source, dest, place = by_tile[0:1], by_tile[1:2], by_tile[2:3]
    earlier = iota((ENTRIES, ENTRIES), 0) < iota((ENTRIES, ENTRIES), 1)
    same = jnp.where(earlier & (down[:, 1:2] == dest), 1.0, 0.0)
    rank = jnp.sum(same, axis=0, keepdims=True)
    numbers = jnp.where(
        sub == 0,
        source * FIELDS,
        jnp.where(sub == 1, dest * CHUNK + rank * FIELDS, dest * BACK + rank * FIELDS),
    )
    routes[...] = numbers.astype(jnp.int32)
    device = iota((DEVICES, ENTRIES), 0).astype(f32)
    to_dest = (device == dest).astype(f32).astype(bf16)
    at_rank = jnp.where(device == rank, place + 1.0, 0.0).astype(bf16)
    offsets[...] = lax.dot_general(to_dest, at_rank, along, preferred_element_type=f32) - 1.0


def own_kernel(weights, *refs):
    given, (strip_out, coef, message, sums, level_sum, routes, offsets, tiles), refs = (
        refs[:7],
        refs[7:15],
        refs[15:],
    )
    here, (strip, sems) = refs[:6], refs[6:]
    copies = start_all(zip(given, (*here, tiles)), sems)
    wait_all(copies[:4])
    route(*here[:4], routes, offsets)
    wait_all(copies[4:6])
    air, cour = here[4:6]
    for side in range(2):
        lanes, own, shift = edge_lanes(side), own_columns(side, ROWS), SHIFTS[side]
        strips, coefs = [], []
        for f in range(FIELDS):
            level = lambda l: jnp.where(own, air[f, l, :, lanes], 0.0)
            strips.append(gather_levels(level, shift))
            strip[side, f] = strips[f]
        for k in range(3):
            coefs.append(spread(roll(jnp.where(own, cour[k, :, lanes], 0.0), shift, 1)))
            coef[side, k] = coefs[k]
        sums[side] = sum_strip(weights, strips)
        message[side] = message_rows(strips, coefs, sums[side])
    copy = pltpu.make_async_copy(strip, strip_out, sems.at[7])
    copy.start()
    for f in range(FIELDS):
        total = weights[f, 0] * air[f, 0]
        for l in range(1, LEVELS):
            total = total + weights[f, l] * air[f, l]
        level_sum[f] = total
    copy.wait()
    copies[6].wait()


def own_parts(weights, *given):
    return pl.pallas_call(
        own_kernel,
        out_shape=(
            pltpu.HBM((2, FIELDS, ROWS, 128), f32),
            jax.ShapeDtypeStruct((2, 3, ROWS, 128), f32),
            jax.ShapeDtypeStruct((2, ROWS, 128), f32),
            jax.ShapeDtypeStruct((2, ROWS, 128), f32),
            jax.ShapeDtypeStruct((FIELDS, ROWS, COLS), f32),
            jax.ShapeDtypeStruct((8, ENTRIES), jnp.int32),
            jax.ShapeDtypeStruct((DEVICES, 128), f32),
            pltpu.VMEM(given[6].shape, bf16),
        ),
        in_specs=[in_smem] + [in_hbm] * 7,
        out_specs=(in_hbm,) + (in_vmem,) * 7,
        scratch_shapes=[pltpu.VMEM(x.shape, x.dtype) for x in given[:6]]
        + [pltpu.VMEM((2, FIELDS, ROWS, 128), f32), pltpu.SemaphoreType.DMA((8,))],
        compiler_params=params(),
        cost_estimate=pl.CostEstimate(flops=1600000, bytes_accessed=1200000, transcendentals=0),
        name="own_parts",
    )(*hbm(weights, *given))


def halo_kernel(weights, sib, nxt, own_message, strip, coef, sums, send_w, send_e, halo):
    for side, send in enumerate((send_w, send_e)):
        lanes, own, shift = edge_lanes(side), own_columns(side, 8), SHIFTS[side]
        north, south = north_south(sib[:, lanes], nxt[:, lanes])
        for f in range(FIELDS):
            for j in range(3):
                at = f * 64 + j * 8
                halo[side, at : at + 8, :] = north[(f * 3 + j) * 8 : (f * 3 + j + 1) * 8]
                halo[side, at + 40 : at + 48, :] = south[(f * 3 + j) * 8 : (f * 3 + j + 1) * 8]
            halo[side, f * 64 + 24 : f * 64 + 40, :] = jnp.zeros((16, BLK), f32)
        strips, coefs = [], []
        for f in range(FIELDS):
            level = lambda l: jnp.where(own, halo[side, pl.ds(f * 64 + l, 8, stride=8), :], 0.0)
            strips.append(gather_levels(level, shift))
            strip[side, f] = strips[f]
        for k in range(3):
            rows = courant_rows(north[96:112], south[96:112], k)
            coefs.append(spread(roll(jnp.where(own, rows, 0.0), shift, 1)))
            coef[side, k] = coefs[k]
        total = jnp.zeros((8, BLK), f32)
        for f in range(FIELDS):
            rows = jnp.where(own, halo_sum(weights, f, north, south), 0.0)
            total = total + roll(rows, f * 16 + shift, 1)
        sums[side] = total
        send[:ROWS] = own_message[side]
        send[ROWS:] = message_rows(strips, coefs, sums[side])


def column_messages(weights, sib, nxt, own_message):
    message = jax.ShapeDtypeStruct((32, 128), f32)
    return pl.pallas_call(
        halo_kernel,
        out_shape=(
            jax.ShapeDtypeStruct((2, FIELDS, 8, 128), f32),
            jax.ShapeDtypeStruct((2, 3, 8, 128), f32),
            jax.ShapeDtypeStruct((2, 8, 128), f32),
            message,
            message,
        ),
        in_specs=[in_smem] + [in_vmem] * 3,
        out_specs=(in_vmem,) * 5,
        scratch_shapes=[pltpu.VMEM((2, FIELDS * 64, BLK), f32)],
        compiler_params=params(),
        cost_estimate=pl.CostEstimate(flops=100000, bytes_accessed=400000, transcendentals=0),
        name="column_messages",
    )(*hbm(weights), sib, nxt, own_message)


def received(side, got):
    lane = iota((32, 128), 1)
    place, group = lane % 16, lane // 16
    first = 0 if side == 0 else 6
    here = (place >= first) & (place < first + 3)
    spare = (place >= 12) & (place < 15)
    numbers = [
        spread(roll(jnp.where((group == k) & spare, got, 0.0), first - 12, 1)) for k in range(3)
    ]
    return here, numbers, roll(got, first - 60, 1)


def coefficients(cx, cy, kd):
    return 1.0 - cx - cy - 4.0 * kd, cx + kd, cy + kd, kd


def step(q, c):
    return (
        q * c[0]
        + roll(q, 1, 1) * c[1]
        + roll(q, 1, 0) * c[2]
        + (roll(q, -1, 1) + roll(q, -1, 0)) * c[3]
    )


def level_weight(weights, f, shape):
    scale = jnp.zeros(shape, f32)
    for l in range(LEVELS):
        scale = jnp.where(iota(shape, 0) == l, weights[f, l], scale)
    return scale


def flux_kernel(weights, level_sum, given, sib, nxt, flux, sib_out, nxt_out, cour, sems):
    copies = start_all([(given, cour), (sib, sib_out), (nxt, nxt_out)], sems)
    copies[0].wait()
    north, south = north_south(sib[...], nxt[...])
    three = [
        jnp.concatenate([cour[k], courant_rows(north[96:], south[96:], k)], 0) for k in range(3)
    ]
    coefs = coefficients(*three)
    for f in range(FIELDS):
        rows = halo_sum(weights, f, north, south)
        q = jnp.concatenate([level_sum[f], rows], 0)
        for _ in range(STEPS):
            q = step(q, coefs)
        q = q[:ROWS].astype(bf16).astype(f32)
        for c in range(COLS // BLK):
            flux[pl.ds(c * FIELDS + f, ROWS, stride=24), :] = q[:, c * BLK : (c + 1) * BLK]
    wait_all(copies[1:])


def flux_stencil(weights, level_sum, courant, sib, nxt):
    return pl.pallas_call(
        flux_kernel,
        out_shape=(
            jax.ShapeDtypeStruct((ROWS * 24, BLK), f32),
            pltpu.HBM(sib.shape, bf16),
            pltpu.HBM(nxt.shape, bf16),
        ),
        in_specs=[in_smem, in_vmem, in_hbm, in_vmem, in_vmem],
        out_specs=(in_vmem, in_hbm, in_hbm),
        scratch_shapes=[pltpu.VMEM(courant.shape, f32), pltpu.SemaphoreType.DMA((3,))],
        compiler_params=params(),
        cost_estimate=pl.CostEstimate(flops=3000000, bytes_accessed=1000000, transcendentals=0),
        name="flux_stencil",
    )(*hbm(weights), level_sum, *hbm(courant), sib, nxt)


def advance(c, q, below, above):
    return q * c[0] + roll(q, 1, 1) * c[1] + below * c[2] + (roll(q, -1, 1) + above) * c[3]


def sweep(coef, starts, done, emits):
    for r in range(-3, ROWS + 3):
        for start, d in zip(starts, done):
            d[0][r] = start(r)
        for s in range(3):
            at = r - 1 - s
            if s - 2 <= at < ROWS + 2 - s:
                c = [coef[k, at % 32 : at % 32 + 1, :] for k in range(4)]
                for d in done:
                    d[s + 1][at] = advance(c, d[s][at], d[s][at - 1], d[s][at + 1])
                if s == 2:
                    for emit, d in zip(emits, done):
                        emit(at, d[3][at])


def air_kernel(air, *refs):
    given, (out, ocean_out, *here), refs = refs[:12], refs[12:26], refs[26:]
    into, done, halo, coef, levels, in_sems, out_sems, sems = refs
    flux, ocean, mixing, mask, cour, sib, nxt, own_strip, halo_strip, strip_coef, from_w, from_e = here
    parts = COLS // BLK

    def copy_in(f, c):
        source = air.at[f, :, :, pl.ds(c * BLK, BLK)]
        return pltpu.make_async_copy(source, into.at[f, c], in_sems.at[f, c])

    def copy_out(f, c):
        target = out.at[f, :, :, pl.ds(c * BLK, BLK)]
        return pltpu.make_async_copy(done.at[f, c], target, out_sems.at[f, c])

    small = start_all(zip(given, here), sems)
    for f in range(FIELDS):
        for c in range(parts):
            copy_in(f, c).start()
    wait_all(small)
    ocean_copy = pltpu.make_async_copy(levels, ocean_out, sems.at[12])
    ocean_levels(flux, ocean, mixing, mask, levels)
    ocean_copy.start()
    north, south = north_south(sib[...], nxt[...])
    halo[0] = south[:96]
    halo[1] = north[:96]
    three = [
        jnp.concatenate([cour[k], courant_rows(north[96:], south[96:], k)], 0) for k in range(3)
    ]
    for k, c in enumerate(coefficients(*three)):
        coef[k] = c
    edges = []
    for side, got in enumerate((from_w, from_e)):
        here, _, _ = received(side, got[...])
        numbers = coefficients(*(strip_coef[side, k] for k in range(3)))
        first = 0 if side == 0 else 6
        for f in range(FIELDS):
            mine = jnp.concatenate([own_strip[side, f], halo_strip[side, f]], 0)
            q = jnp.where(here, roll(got[...], first - 3 * f, 1), mine)
            for _ in range(STEPS):
                q = step(q, numbers)
            edges.append(q[:ROWS])

    def starter(f):
        flat = [into.at[f, c].reshape(LEVELS * ROWS, BLK) for c in range(parts)]

        def start(r):
            if r < 0:
                return halo[0, f * 24 + (r + 3) * 8 : f * 24 + (r + 4) * 8, :]
            if r >= ROWS:
                return halo[1, f * 24 + (r - ROWS) * 8 : f * 24 + (r - ROWS + 1) * 8, :]
            return jnp.concatenate([x[pl.ds(r, LEVELS, stride=ROWS), :] for x in flat], 1)

        return start

    def emitter(f):
        flat = [done.at[f, c].reshape(LEVELS * ROWS, BLK) for c in range(parts)]

        def emit(r, q):
            for c in range(parts):
                flat[c][pl.ds(r, LEVELS, stride=ROWS), :] = q[:, c * BLK : (c + 1) * BLK]

        return emit

    column = iota((ROWS, 128), 1)
    for fields in ((0, 1), (2, 3)):
        for f in fields:
            for c in range(parts):
                copy_in(f, c).wait()
        sweep(
            coef,
            [starter(f) for f in fields],
            [[{}, {}, {}, {}] for f in fields],
            [emitter(f) for f in fields],
        )
        for f in fields:
            for c in range(1, parts - 1):
                copy_out(f, c).start()
            for l in range(LEVELS):
                west, east = roll(edges[f], -l * 16 - 3, 1), roll(edges[FIELDS + f], 122 - l * 16, 1)
                done[f, 0, l] = jnp.where(column < 3, west, done[f, 0, l])
                done[f, parts - 1, l] = jnp.where(column >= 125, east, done[f, parts - 1, l])
            copy_out(f, 0).start()
            copy_out(f, parts - 1).start()
    for f in range(FIELDS):
        for c in range(parts):
            copy_out(f, c).wait()
    ocean_copy.wait()


def ocean_levels(flux, ocean, mixing, mask, out):
    wet = mask[...].astype(f32)
    mix = wet * mixing[...]
    for f in range(FIELDS):
        q = [ocean[f, l] for l in range(8)]
        q[0] = q[0] + wet * flux[f]
        for l in range(8):
            out[f, l] = q[l] + mix * (q[max(l - 1, 0)] + q[min(l + 1, 7)] - 2.0 * q[l])


def air_steps(air, *given):
    parts = COLS // BLK
    return pl.pallas_call(
        air_kernel,
        out_shape=(pltpu.HBM(air.shape, f32), pltpu.HBM(given[1].shape, f32)),
        in_specs=[in_hbm] * 13,
        out_specs=(in_hbm, in_hbm),
        scratch_shapes=[pltpu.VMEM(x.shape, x.dtype) for x in given]
        + [
            pltpu.VMEM((FIELDS, parts, LEVELS, ROWS, BLK), f32),
            pltpu.VMEM((FIELDS, parts, LEVELS, ROWS, BLK), f32),
            pltpu.VMEM((2, 96, COLS), f32),
            pltpu.VMEM((4, 32, COLS), f32),
            pltpu.VMEM(given[1].shape, f32),
            pltpu.SemaphoreType.DMA((FIELDS, parts)),
            pltpu.SemaphoreType.DMA((FIELDS, parts)),
            pltpu.SemaphoreType.DMA((13,)),
        ],
        compiler_params=params(),
        cost_estimate=pl.CostEstimate(flops=30000000, bytes_accessed=6000000, transcendentals=0),
        name="air_steps",
    )(*hbm(air, *given))


def fix_edges(own_sums, halo_sums, own_coef, halo_coef, from_w, from_e, coef_out, flux):
    lane = iota((32, 128), 1)
    column = iota((ROWS, 128), 1)
    for side, got in enumerate((from_w, from_e)):
        here, numbers, sums = received(side, got[...])
        three = []
        for k in range(3):
            mine = jnp.concatenate([own_coef[side, k], halo_coef[side, k]], 0)
            three.append(jnp.where(here, numbers[k], mine))
            coef_out[side, k] = three[k]
        coefs = coefficients(*three)
        mine = jnp.concatenate([own_sums[side], halo_sums[side]], 0)
        q = jnp.where(here & (lane < 64), sums, mine)
        for _ in range(STEPS):
            q = step(q, coefs)
        q = q[:ROWS].astype(bf16).astype(f32)
        for f in range(FIELDS):
            at = pl.ds(8 + f + (0 if side == 0 else 20), ROWS, stride=24)
            if side == 0:
                flux[at, :] = jnp.where(column < 3, roll(q, -f * 16 - 3, 1), flux[at, :])
            else:
                flux[at, :] = jnp.where(column >= 125, roll(q, 122 - f * 16, 1), flux[at, :])


def block_rows(ref, at, low):
    half = iota((8, BLK), 0) < 4
    if low:
        return jnp.where(half, ref[pl.ds(at + 8, 8), :], 0.0)
    return jnp.where(half, 0.0, ref[pl.ds(at + 4, 8), :])


def four_rows(ref, at):
    left = jnp.concatenate([block_rows(ref, at[0], True), block_rows(ref, at[2], True)], 0)
    right = jnp.concatenate([block_rows(ref, at[1], False), block_rows(ref, at[3], False)], 0)
    return jnp.concatenate([left, right], 1).astype(bf16)


def four_results(r):
    return r[0:4, :BLK], r[4:8, :BLK], r[8:12, BLK:], r[12:16, BLK:]


def send_kernel(routes, flux_in, halo_strip, *refs):
    edges, (offsets, tiles, out, *kept, flux, total, coef, sems) = refs[:6], refs[6:]
    copies = start_all(zip((halo_strip, *edges[4:6]), kept), sems)
    flux[0:8, :] = jnp.zeros((8, BLK), f32)
    flux[8 : 8 + ROWS * 24, :] = flux_in[...]
    flux[8 + ROWS * 24 :, :] = jnp.zeros((8, BLK), f32)
    fix_edges(*edges, coef, flux)
    copies.append(pltpu.make_async_copy(coef, kept[3], sems.at[3]))
    copies[3].start()
    total[...] = jnp.zeros(total.shape, f32)
    total[pl.ds(BACK, DEVICES, stride=CHUNK), :] = offsets[...]
    for t in range(0, ENTRIES, 4):
        at = [routes[0, t + i] for i in range(4)]
        w = jnp.concatenate(
            [
                jnp.concatenate([tiles[t], tiles[t + 1]], 0),
                jnp.concatenate([tiles[t + 2], tiles[t + 3]], 0),
            ],
            1,
        )
        r = jnp.dot(four_rows(flux, at), w, preferred_element_type=f32)
        for i, piece in enumerate(four_results(r)):
            total[pl.ds(routes[1, t + i], 4), :] = piece
    out[...] = total[...].astype(bf16)
    wait_all(copies)


def send_blocks(routes, flux, halo_strip, edges, offsets, tiles):
    return pl.pallas_call(
        send_kernel,
        out_shape=(
            jax.ShapeDtypeStruct((DEVICES * CHUNK, BLK), bf16),
            pltpu.HBM(halo_strip.shape, f32),
            pltpu.HBM((32, 128), f32),
            pltpu.HBM((32, 128), f32),
            pltpu.HBM((2, 3, 32, 128), f32),
        ),
        in_specs=[in_smem] + [in_vmem] * 10,
        out_specs=(in_vmem,) + (in_hbm,) * 4,
        scratch_shapes=[
            pltpu.VMEM((ROWS * 24 + 16, BLK), f32),
            pltpu.VMEM((DEVICES * CHUNK, BLK), f32),
            pltpu.VMEM((2, 3, 32, 128), f32),
            pltpu.SemaphoreType.DMA((4,)),
        ],
        compiler_params=params(),
        cost_estimate=pl.CostEstimate(flops=40000000, bytes_accessed=11000000, transcendentals=0),
        name="send_blocks",
    )(routes, flux, halo_strip, *edges, offsets, tiles)


def ocean_kernel(payload, ocean, mixing, mask, flux_out, back, got, ret, packed, kept, sems):
    got[...] = payload[...].astype(f32)
    offsets = got[pl.ds(BACK, DEVICES, stride=CHUNK), :]
    by_slot = offsets.T
    blocks = iota((OCEAN_ROWS, DEVICES), 0).astype(f32)
    flux = None
    for j in range(CAP):
        place = (by_slot[j : j + 1, :] == blocks).astype(f32).astype(bf16)
        data = jnp.concatenate(
            [got[pl.ds(j * FIELDS + f, DEVICES, stride=CHUNK), :] for f in range(FIELDS)], 1
        ).astype(bf16)
        part = jnp.dot(place, data, preferred_element_type=f32)
        flux = part if j == 0 else flux + part
    wet = mask[...].astype(f32)
    mix = wet * mixing[...]
    surface = []
    for f in range(FIELDS):
        piece = flux[:, f * BLK : (f + 1) * BLK]
        kept[f] = piece
        top, below = ocean[f, 0] + wet * piece, ocean[f, 1]
        new = top + mix * (top + below - 2.0 * top)
        surface.append((wet * new).astype(bf16))
    copies = [pltpu.make_async_copy(kept, flux_out, sems.at[0])]
    copies[0].start()
    surface = jnp.concatenate(surface, 1)
    lanes = iota((DEVICES, OCEAN_ROWS), 1).astype(f32)
    for j in range(CAP):
        pick = (offsets[:, j : j + 1] == lanes).astype(f32).astype(bf16)
        rows = jnp.dot(pick, surface, preferred_element_type=f32)
        for f in range(FIELDS):
            ret[pl.ds(j * FIELDS + f, DEVICES, stride=BACK), :] = rows[:, f * BLK : (f + 1) * BLK]
    packed[...] = ret[...].astype(bf16)
    copies.append(pltpu.make_async_copy(packed, back, sems.at[1]))
    copies[1].start()
    for copy in copies:
        copy.wait()


def ocean_surface(payload, ocean, mixing, mask):
    return pl.pallas_call(
        ocean_kernel,
        out_shape=(
            pltpu.HBM((FIELDS, OCEAN_ROWS, BLK), f32),
            pltpu.HBM((DEVICES * BACK, BLK), bf16),
        ),
        in_specs=[in_vmem] * 4,
        out_specs=(in_hbm, in_hbm),
        scratch_shapes=[
            pltpu.VMEM((DEVICES * CHUNK, BLK), f32),
            pltpu.VMEM((DEVICES * BACK, BLK), f32),
            pltpu.VMEM((DEVICES * BACK, BLK), bf16),
            pltpu.VMEM((FIELDS, OCEAN_ROWS, BLK), f32),
            pltpu.SemaphoreType.DMA((2,)),
        ],
        compiler_params=params(),
        cost_estimate=pl.CostEstimate(flops=100000000, bytes_accessed=4000000, transcendentals=0),
        name="ocean_surface",
    )(payload, ocean, mixing, mask)


def return_kernel(routes, payload, stored, out, got, total, arrived, tiles, sems):
    first = start_all([(payload, arrived)], sems)[0]
    waits = start_tiles(stored, tiles, sems.at[pl.ds(1, 6)], (0, 48, 96, 144, 192, 240, ENTRIES))
    got[0:8, :] = jnp.zeros((8, BLK), f32)
    got[8 + DEVICES * BACK :, :] = jnp.zeros((8, BLK), f32)
    total[...] = jnp.zeros(total.shape, f32)
    first.wait()
    got[8 : 8 + DEVICES * BACK, :] = arrived[...].astype(f32)
    for t in range(0, ENTRIES, 4):
        if t in waits:
            waits[t].wait()
        at = [routes[2, t + i] for i in range(4)]
        w = jnp.concatenate(
            [
                jnp.concatenate([tiles[t], tiles[t + 1]], 1),
                jnp.concatenate([tiles[t + 2], tiles[t + 3]], 1),
            ],
            0,
        )
        r = lax.dot_general(
            four_rows(got, at), w, (((1,), (1,)), ((), ())), preferred_element_type=f32
        )
        for i, piece in enumerate(four_results(r)):
            here = pl.ds(routes[0, t + i], 4)
            total[here, :] = total[here, :] + piece
    for f in range(FIELDS):
        for c in range(COLS // BLK):
            out[f, :, c * BLK : (c + 1) * BLK] = total[pl.ds(c * FIELDS + f, ROWS, stride=24), :]


def return_blocks(routes, payload, tiles):
    return pl.pallas_call(
        return_kernel,
        out_shape=jax.ShapeDtypeStruct((FIELDS, ROWS, COLS), f32),
        in_specs=[in_smem, pl.BlockSpec(memory_space=pl.ANY), in_hbm],
        scratch_shapes=[
            pltpu.VMEM((DEVICES * BACK + 16, BLK), f32),
            pltpu.VMEM((ROWS * 24, BLK), f32),
            pltpu.VMEM((DEVICES * BACK, BLK), bf16),
            pltpu.VMEM((ENTRIES, BLK, BLK), bf16),
            pltpu.SemaphoreType.DMA((7,)),
        ],
        compiler_params=params(24),
        cost_estimate=pl.CostEstimate(flops=40000000, bytes_accessed=11000000, transcendentals=0),
        name="return_blocks",
    )(routes, payload, *hbm(tiles))


def exchange(x, rows):
    x = x.reshape(DEVICES * CAP, rows // CAP, BLK) if rows == BACK else x.reshape(-1, 2, BLK)
    x = lax.all_to_all(x, ("face", "tile"), split_axis=0, concat_axis=0, tiled=True)
    return x.reshape(DEVICES * rows, BLK)


def shards(
    atmos_state,
    courant,
    level_weights,
    remap_tiles,
    src_block,
    owner,
    offset,
    tile_index,
    ocean_state,
    mixing,
    land_mask,
):
    faces, tile_count = lax.axis_size("face"), lax.axis_size("tile")
    sib, nxt = row_messages(atmos_state, courant)
    inner = [(i, i + 1) for i in range(1, tile_count - 1, 2)]
    nxt = lax.ppermute(nxt, "tile", inner + [(b, a) for a, b in inner])
    sib = lax.ppermute(sib, "tile", [(i, i ^ 1) for i in range(tile_count)])
    own_strip, own_coef, own_message, own_sums, level_sum, routes, offsets, tiles = own_parts(
        *(level_weights, src_block, owner.reshape(1, -1), offset, tile_index),
        *(atmos_state, courant, remap_tiles),
    )
    halo_strip, halo_coef, halo_sums, send_w, send_e = column_messages(
        level_weights, sib, nxt, own_message
    )
    from_e = lax.ppermute(send_w, "face", [((i + 1) % faces, i) for i in range(faces)])
    from_w = lax.ppermute(send_e, "face", [(i, (i + 1) % faces) for i in range(faces)])
    flux, sib, nxt = flux_stencil(level_weights, level_sum, courant, sib, nxt)
    edges = (own_sums, halo_sums, own_coef, halo_coef, from_w, from_e)
    message, *edges = send_blocks(routes, flux, halo_strip, edges, offsets, tiles)
    halo_strip, from_w, from_e, strip_coef = edges
    message = exchange(message, CHUNK)
    ocean_flux, back = ocean_surface(message, ocean_state, mixing, land_mask)
    back = exchange(back, BACK)
    ocean_inputs = (ocean_flux, ocean_state, mixing, land_mask)
    edges = (own_strip, halo_strip, strip_coef, from_w, from_e)
    air_state, ocean_out = air_steps(atmos_state, *ocean_inputs, courant, sib, nxt, *edges)
    atmos_surface = return_blocks(routes, back, remap_tiles)
    return air_state, ocean_out, atmos_surface


def solution(mesh):
    return jax.shard_map(
        shards,
        mesh=mesh,
        in_specs=(
            P(None, None, "tile", "face"),
            P(None, "tile", "face"),
            P(),
            P(("face", "tile"), None, None),
            P(("face", "tile"), None),
            P(("face", "tile"), None, None),
            P(("face", "tile"), None),
            P(("face", "tile"), None),
            P(None, None, "face", "tile"),
            P("face", "tile"),
            P("face", "tile"),
        ),
        out_specs=(
            P(None, None, "tile", "face"),
            P(None, None, "face", "tile"),
            P(None, "tile", "face"),
        ),
        check_vma=False,
    )
```

time: 91.1 us -> 75.6 us (0.83)
  waiting for transfers between devices: 16.1 us -> 5.85 us
  local copies, waits for them, and re-layouts: 2.64 us -> 0.02 us
  blocking collectives: 26.3 us -> 24.3 us
    all_to_all x1, waiting for transfers between devices: 13.1 us -> 5.83 us  [exchange(): lax.all_to_all(x, ('face', 'tile'), split_axis=0, concat_axis=0, tiled=True)]
    pallas_call x5 -> x6, Pallas kernels: 14.9 us -> 22.1 us  [the longest x1 9.35 us: air_steps(): pl.pallas_call(air_kernel, out_shape=(pltpu.HBM(air.shape, f32), pltpu.HB...]
    pallas_call x1, Pallas kernels: 7.97 us -> 3.33 us  [send_blocks(): pl.pallas_call(send_kernel, out_shape=(jax.ShapeDtypeStruct((DEVICES * CH...]
    ppermute x1, waiting for transfers between devices: 2.98 us -> 0.01 us  [shards(): nxt = lax.ppermute(nxt, 'tile', inner + [(b, a) for a, b in inner])]
    unnamed x24 -> x6, local copies, waits for them, and re-layouts: 2.64 us -> 0.02 us
    pallas_call x1, Pallas kernels: 8.59 us -> 6.43 us  [return_blocks(): pl.pallas_call(return_kernel, out_shape=jax.ShapeDtypeStruct((FIELDS, ROW...]
    all_to_all x1, blocking collectives: 26.3 us -> 24.3 us  [exchange(): lax.all_to_all(x, ('face', 'tile'), split_axis=0, concat_axis=0, tiled=True)]
  transfers between devices with their start and end apart: 5 -> 5, of which waited for: 2 -> 1; matrix products, arithmetic and copies ran while one was open for 1% -> 0% of each run, Pallas kernels for 13% -> 23%
where the time goes in v2:
time: 75.6 us; the launch traced here: 75.3 us
  Pallas kernels  31.8 us (42%)
  blocking collectives  24.3 us (32%)
  starting transfers between devices  12.3 us (16%)
  waiting for transfers between devices  5.85 us (8%)
  between operations  0.92 us (1%)
    all_to_all x1, blocking collectives, exchange(): lax.all_to_all(x, ('face', 'tile'), split_axis=0, concat_axis=0, tiled=True)  24.3 us
    pallas_call x1, Pallas kernels, air_steps(): pl.pallas_call(air_kernel, out_shape=(pltpu.HBM(air.shape, f32), pltpu.HB...  9.35 us
    pallas_call x1, Pallas kernels, return_blocks(): pl.pallas_call(return_kernel, out_shape=jax.ShapeDtypeStruct((FIELDS, ROW...  6.43 us
    all_to_all x1, waiting for transfers between devices, exchange(): lax.all_to_all(x, ('face', 'tile'), split_axis=0, concat_axis=0, tiled=True)  5.83 us
    pallas_call x1, Pallas kernels, own_parts(): pl.pallas_call(own_kernel, out_shape=(pltpu.HBM((2, FIELDS, ROWS, 128), f...  5.45 us
    all_to_all x1, starting transfers between devices, exchange(): lax.all_to_all(x, ('face', 'tile'), split_axis=0, concat_axis=0, tiled=True)  4.61 us
    ppermute x1, starting transfers between devices, shards(): nxt = lax.ppermute(nxt, 'tile', inner + [(b, a) for a, b in inner])  3.53 us
    pallas_call x1, Pallas kernels, send_blocks(): pl.pallas_call(send_kernel, out_shape=(jax.ShapeDtypeStruct((DEVICES * CH...  3.33 us
  transfers between devices with their start and end apart: 5, of which 1 were waited for; matrix products, arithmetic and copies ran while one was open for 0% of the time, Pallas kernels for 23%

profile of v2, /device:TPU:1, one launch (start us, length us, event | category | flops | bytes accessed | tf_op | source)
XLA Modules:
  0.0 75.3 jit_solution(12411275402783977236)
XLA Ops:
  0.6 1.8 %row_messages.1 = (bf16[112,768]{1,0:T(8,128)(2,1)S(1)}, bf16[112,768]{1,0:T(8,128)(2,1)S(1)}) custom-call(f32[4,8,24,768]{3,2,1,0:T(8,128)} %air.3, f32[3,24,768]{2,1,0:T(8,128)} %refs_4_.3), custom_call_target="tpu_custom_call" | custom-call | flops 400000 | bytes 2000000 | tf_op jit(solution)/shard_map/row_messages/pallas_call | solution.py:103
  2.4 1.5 %collective-permute-start = (bf16[112,768]{1,0:T(8,128)(2,1)S(1)}, bf16[112,768]{1,0:T(8,128)(2,1)S(1)}, u32[]{:S(2)}, u32[]{:S(2)}) collective-permute-start(bf16[112,768]{1,0:T(8,128)(2,1)S(1)} %get-tuple-element.32), channel_id=1, source_target_pairs={{0,1},{1,0},{2,3},{3,2},{4,5},{5,4},{6,7},{7,6},{8,9},{9,8},{10,11... | collective-permute-start | bytes 516104 | tf_op jit(solution)/shard_map/ppermute | solution.py:764
  3.9 3.5 %collective-permute-start.1 = (bf16[112,768]{1,0:T(8,128)(2,1)S(1)}, bf16[112,768]{1,0:T(8,128)(2,1)S(1)}, u32[]{:S(2)}, u32[]{:S(2)}) collective-permute-start(bf16[112,768]{1,0:T(8,128)(2,1)S(1)} %get-tuple-element.33), channel_id=1, source_target_pairs={{1,2},{3,4},{5,6},{7,8},{9,10},{11,12},{13,14},{15,16},{17,18},{19... | collective-permute-start | bytes 516104 | tf_op jit(solution)/shard_map/ppermute | solution.py:763
  7.4 0.0 copy-start
  7.4 0.0 copy-start.1
  7.5 0.0 copy-start.2
  7.5 5.5 %own_parts.1 = (f32[2,4,24,128]{3,2,1,0:T(8,128)}, f32[2,3,24,128]{3,2,1,0:T(8,128)S(1)}, f32[2,24,128]{2,1,0:T(8,128)S(1)}, f32[2,24,128]{2,1,0:T(8,128)S(1)}, ...) custom-call(f32[4,8]{1,0:T(4,128)} %weights.5, ...), custom_call_target="tpu_custom_call" | custom-call | flops 1600000 | bytes 1200000 | tf_op jit(solution)/shard_map/own_parts/pallas_call | solution.py:261
  12.9 0.0 collective-permute-done.sib
  12.9 0.0 collective-permute-done.1.nxt
  12.9 1.1 %column_messages.1 = (f32[2,4,8,128]{3,2,1,0:T(8,128)S(1)}, f32[2,3,8,128]{3,2,1,0:T(8,128)S(1)}, f32[2,8,128]{2,1,0:T(8,128)S(1)}, f32[32,128]{1,0:T(8,128)S(1)}, f32[32,128]{1,0:T(8,128)S(1)}) custom-call(f32[4,8]{1,0:T(4,128)} %weights.5, bf16[112,768]{1,0:T(8,128)(2,1)S(1)} %collective-permute-done.sib, bf16[112,768]{1,0:T(8,128)(2,1)S(1)} %collective-permute-done.1.nxt, ...), custom_call_target="tpu_custom_call" | custom-call | flops 100000 | bytes 400000 | tf_op jit(solution)/shard_map/column_messages/pallas_call | solution.py:313
  14.0 1.2 %collective-permute-start.2 = (f32[32,128]{1,0:T(8,128)S(1)}, f32[32,128]{1,0:T(8,128)S(1)}, u32[]{:S(2)}, u32[]{:S(2)}) collective-permute-start(f32[32,128]{1,0:T(8,128)S(1)} %get-tuple-element.41), channel_id=1, source_target_pairs={{0,32},{32,64},{64,96},{96,0},{1,33},{33,65},{65,97},{97,1},{2,34}... | collective-permute-start | bytes 49160 | tf_op jit(solution)/shard_map/ppermute | solution.py:773
  15.2 1.5 %collective-permute-start.3 = (f32[32,128]{1,0:T(8,128)S(1)}, f32[32,128]{1,0:T(8,128)S(1)}, u32[]{:S(2)}, u32[]{:S(2)}) collective-permute-start(f32[32,128]{1,0:T(8,128)S(1)} %get-tuple-element.42), channel_id=1, source_target_pairs={{32,0},{64,32},{96,64},{0,96},{33,1},{65,33},{97,65},{1,97},{34,2}... | collective-permute-start | bytes 49160 | tf_op jit(solution)/shard_map/ppermute | solution.py:772
  16.7 2.9 %flux_stencil.1 = (f32[576,128]{1,0:T(8,128)S(1)}, bf16[112,768]{1,0:T(8,128)(2,1)}, bf16[112,768]{1,0:T(8,128)(2,1)}) custom-call(f32[4,8]{1,0:T(4,128)} %weights.5, f32[4,24,768]{2,1,0:T(8,128)S(1)} %get-tuple-element.31.level_sum, f32[3,24,768]{2,1,0:T(8,128)} %refs_4_.3, bf16[112,768]{1,0:T(8,128)(2,1)S(1)} %collective-permute-done.sib, ...), custom_call_target="tpu_custom_call" | custom-call | flops 3000000 | bytes 1000000 | tf_op jit(solution)/shard_map/flux_stencil/pallas_call | solution.py:383
  19.6 0.0 collective-permute-done.2.refs_4_
  19.6 0.0 collective-permute-done.3.refs_5_
  19.6 3.3 %send_blocks.1 = (bf16[2816,128]{1,0:T(8,128)(2,1)S(1)}, f32[2,4,8,128]{3,2,1,0:T(8,128)}, f32[32,128]{1,0:T(8,128)}, f32[32,128]{1,0:T(8,128)}, f32[2,3,32,128]{3,2,1,0:T(8,128)}) custom-call(s32[8,288]{1,0:T(8,128)S(1)} %get-tuple-element.30.routes, f32[576,128]{1,0:T(8,128)S(1)} %get-tuple-element.34.flux_in, ...), custom_call_target="tpu_custom_call" | custom-call | flops 40000000 | bytes 11000000 | tf_op jit(solution)/shard_map/send_blocks/pallas_call | solution.py:610
  23.0 24.3 %all_to_all.10 = bf16[1408,2,128]{2,1,0:T(2,128)(2,1)S(1)} all-to-all(bf16[1408,2,128]{2,1,0:T(2,128)(2,1)S(1)} %bitcast.7), channel_id=1, replica_groups=mesh['face'=4,'tile'=32] {'face','tile'}, dimensions={0} | all-to-all | bytes 1441792 | tf_op jit(solution)/shard_map/all_to_all | solution.py:743
  47.3 0.0 copy-done
  47.3 0.0 copy-done.1
  47.3 1.6 %ocean_surface.1 = (f32[4,64,128]{2,1,0:T(8,128)}, bf16[2560,128]{1,0:T(8,128)(2,1)}) custom-call(bf16[2816,128]{1,0:T(8,128)(2,1)S(1)} %bitcast.5, f32[4,8,64,128]{3,2,1,0:T(8,128)S(1)} %copy-done, f32[64,128]{1,0:T(8,128)S(1)} %copy-done.1, s32[64,128]{1,0:T(8,128)S(1)} %copy-done.2), custom_call_target="tpu_custom_call" | custom-call | flops 100000000 | bytes 4000000 | tf_op jit(solution)/shard_map/ocean_surface/pallas_call | solution.py:672
  48.9 4.6 %all-to-all-start.1 = ((bf16[640,4,128]{2,1,0:T(4,128)(2,1)}), bf16[640,4,128]{2,1,0:T(4,128)(2,1)S(1)}, u32[]{:S(2)}, u32[]{:S(2)}) async-start(bf16[640,4,128]{2,1,0:T(4,128)(2,1)} %bitcast.8), calls=%async_computation.1 | async-start | bytes 1310720 | tf_op jit(solution)/shard_map/all_to_all | solution.py:743
  53.5 9.4 %air_steps.1 = (f32[4,8,24,768]{3,2,1,0:T(8,128)}, f32[4,8,64,128]{3,2,1,0:T(8,128)}) custom-call(f32[4,8,24,768]{3,2,1,0:T(8,128)} %air.3, f32[4,64,128]{2,1,0:T(8,128)} %get-tuple-element.46.refs_0_, f32[4,8,64,128]{3,2,1,0:T(8,128)} %refs_1_.1, f32[64,128]{1,0:T(8,128)} %refs_2_.3, s32[64,128]{1,0:T(8,128)} %refs_3_.3, f32[3,24,768]{2,1,0:T(8,128)} %refs_4_.3, ...), custom_call_target="tpu_custom_call" | custom-call | flops 30000000 | bytes 6000000 | tf_op jit(solution)/shard_map/air_steps/pallas_call | solution.py:519
  62.9 5.8 %all-to-all-done.1 = bf16[640,4,128]{2,1,0:T(4,128)(2,1)S(1)} async-done(((bf16[640,4,128]{2,1,0:T(4,128)(2,1)}), bf16[640,4,128]{2,1,0:T(4,128)(2,1)S(1)}, u32[]{:S(2)}, u32[]{:S(2)}) %all-to-all-start.1) | async-done | bytes 655392 | tf_op jit(solution)/shard_map/all_to_all | solution.py:743
  68.7 6.4 %return_blocks.1 = f32[4,24,768]{2,1,0:T(8,128)} custom-call(s32[8,288]{1,0:T(8,128)S(1)} %get-tuple-element.30.routes, bf16[2560,128]{1,0:T(8,128)(2,1)S(1)} %bitcast.6, bf16[288,128,128]{2,1,0:T(8,128)(2,1)} %stored.1), custom_call_target="tpu_custom_call" | custom-call | flops 40000000 | bytes 11000000 | tf_op jit(solution)/shard_map/return_blocks/pallas_call | solution.py:724
  (1 shorter events, 0.0 us)
Async XLA Ops:
  2.4 10.5 %collective-permute-start = (bf16[112,768]{1,0:T(8,128)(2,1)S(1)}, bf16[112,768]{1,0:T(8,128)(2,1)S(1)}, u32[]{:S(2)}, u32[]{:S(2)}) collective-permute-start(bf16[112,768]{1,0:T(8,128)(2,1)S(1)} %get-tuple-element.32), channel_id=1, source_target_pairs={{0,1},{1,0},{2,3},{3,2},{4,5},{5,4},{6,7},{7,6},{8,9},{9,8},{10,11... | collective-permute-start | bytes 516104 | tf_op jit(solution)/shard_map/ppermute | solution.py:764
  3.9 9.0 %collective-permute-start.1 = (bf16[112,768]{1,0:T(8,128)(2,1)S(1)}, bf16[112,768]{1,0:T(8,128)(2,1)S(1)}, u32[]{:S(2)}, u32[]{:S(2)}) collective-permute-start(bf16[112,768]{1,0:T(8,128)(2,1)S(1)} %get-tuple-element.33), channel_id=1, source_target_pairs={{1,2},{3,4},{5,6},{7,8},{9,10},{11,12},{13,14},{15,16},{17,18},{19... | collective-permute-start | bytes 516104 | tf_op jit(solution)/shard_map/ppermute | solution.py:763
  7.4 39.9 %copy-start = (f32[4,8,64,128]{3,2,1,0:T(8,128)S(1)}, f32[4,8,64,128]{3,2,1,0:T(8,128)}, u32[]{:S(2)}) copy-start(f32[4,8,64,128]{3,2,1,0:T(8,128)} %refs_1_.1) | copy-start | bytes 3145732
  7.4 39.8 %copy-start.1 = (f32[64,128]{1,0:T(8,128)S(1)}, f32[64,128]{1,0:T(8,128)}, u32[]{:S(2)}) copy-start(f32[64,128]{1,0:T(8,128)} %refs_2_.3) | copy-start | bytes 98308
  7.5 39.8 %copy-start.2 = (s32[64,128]{1,0:T(8,128)S(1)}, s32[64,128]{1,0:T(8,128)}, u32[]{:S(2)}) copy-start(s32[64,128]{1,0:T(8,128)} %refs_3_.3) | copy-start | bytes 98308
  14.0 5.6 %collective-permute-start.2 = (f32[32,128]{1,0:T(8,128)S(1)}, f32[32,128]{1,0:T(8,128)S(1)}, u32[]{:S(2)}, u32[]{:S(2)}) collective-permute-start(f32[32,128]{1,0:T(8,128)S(1)} %get-tuple-element.41), channel_id=1, source_target_pairs={{0,32},{32,64},{64,96},{96,0},{1,33},{33,65},{65,97},{97,1},{2,34}... | collective-permute-start | bytes 49160 | tf_op jit(solution)/shard_map/ppermute | solution.py:773
  15.2 4.4 %collective-permute-start.3 = (f32[32,128]{1,0:T(8,128)S(1)}, f32[32,128]{1,0:T(8,128)S(1)}, u32[]{:S(2)}, u32[]{:S(2)}) collective-permute-start(f32[32,128]{1,0:T(8,128)S(1)} %get-tuple-element.42), channel_id=1, source_target_pairs={{32,0},{64,32},{96,64},{0,96},{33,1},{65,33},{97,65},{1,97},{34,2}... | collective-permute-start | bytes 49160 | tf_op jit(solution)/shard_map/ppermute | solution.py:772
  48.9 19.8 %all-to-all-start.1 = ((bf16[640,4,128]{2,1,0:T(4,128)(2,1)}), bf16[640,4,128]{2,1,0:T(4,128)(2,1)S(1)}, u32[]{:S(2)}, u32[]{:S(2)}) async-start(bf16[640,4,128]{2,1,0:T(4,128)(2,1)} %bitcast.8), calls=%async_computation.1 | async-start | bytes 1310720 | tf_op jit(solution)/shard_map/all_to_all | solution.py:743

commit v3 on v2

--- a/solution.py
+++ b/solution.py
@@ -11,6 +11,7 @@
 ENTRIES, DEVICES, CAP, OCEAN_ROWS = 288, 128, 5, 64
 CHUNK = 22
 BACK = CAP * FIELDS
+HALF = 208
 f32, bf16 = jnp.float32, jnp.bfloat16
 
 
@@ -28,7 +29,6 @@
 
 
 in_vmem = pl.BlockSpec(memory_space=pltpu.VMEM)
-in_smem = pl.BlockSpec(memory_space=pltpu.SMEM)
 in_hbm = pl.BlockSpec(memory_space=pltpu.HBM)
 
 
@@ -55,47 +55,49 @@
 
 
 def row_kernel(air, cour, sib_ref, nxt_ref, top, bot, top_cour, bot_cour, sems):
-    copies = []
+    pairs = [(cour.at[:, pl.ds(0, 8), :], top_cour), (cour.at[:, pl.ds(16, 8), :], bot_cour)]
     for c in range(COLS // BLK):
         lanes = pl.ds(c * BLK, BLK)
-        copies.append((air.at[:, :, pl.ds(0, 8), lanes], top.at[c]))
-        copies.append((air.at[:, :, pl.ds(16, 8), lanes], bot.at[c]))
-    copies.append((cour.at[:, pl.ds(0, 8), :], top_cour))
-    copies.append((cour.at[:, pl.ds(16, 8), :], bot_cour))
-    copies = [pltpu.make_async_copy(a, b, sems.at[i]) for i, (a, b) in enumerate(copies)]
-    for copy in copies:
-        copy.start()
-    for copy in copies:
-        copy.wait()
-
-    def pack(out, at_top):
-        first = 0 if at_top else 5
-        rows, numbers = (top, top_cour) if at_top else (bot, bot_cour)
-        for c in range(COLS // BLK):
-            flat = rows.at[c].reshape(FIELDS * LEVELS * 8, BLK)
-
-            def tile(i):
-                return flat[pl.ds(i // 3 * 64 + first + i % 3, LEVELS, stride=8), :]
-
-            for i in range(0, FIELDS * 3, 2):
-                both = jnp.concatenate([tile(i), tile(i + 1)], 0)
-                out[i * 8 : i * 8 + 16, c * BLK : (c + 1) * BLK] = both.astype(bf16)
+        pairs.append((air.at[:, :, pl.ds(0, 8), lanes], top.at[c]))
+        pairs.append((air.at[:, :, pl.ds(16, 8), lanes], bot.at[c]))
+    copies = start_all(pairs, sems)
+
+    def pack_numbers(out, at_top):
+        first, numbers = (0, top_cour) if at_top else (5, bot_cour)
         sub = iota((8, COLS), 0)
         pair = jnp.where(sub < 4, roll(numbers[0], -first, 0), roll(numbers[1], 4 - first, 0))
         last = jnp.where(sub < 4, roll(numbers[2], -first, 0), 0.0)
         out[96:112, :] = jnp.concatenate([pair, last], 0).astype(bf16)
 
+    def pack(out, at_top, c):
+        first, rows = (0, top) if at_top else (5, bot)
+        flat = rows.at[c].reshape(FIELDS * LEVELS * 8, BLK)
+
+        def tile(i):
+            return flat[pl.ds(i // 3 * 64 + first + i % 3, LEVELS, stride=8), :]
+
+        for i in range(0, FIELDS * 3, 2):
+            both = jnp.concatenate([tile(i), tile(i + 1)], 0)
+            out[i * 8 : i * 8 + 16, c * BLK : (c + 1) * BLK] = both.astype(bf16)
+
+    def send(to_top, to_bot):
+        wait_all(copies[:2])
+        pack_numbers(to_top, True)
+        pack_numbers(to_bot, False)
+        for c in range(COLS // BLK):
+            wait_all(copies[2 * c + 2 : 2 * c + 4])
+            pack(to_top, True, c)
+            pack(to_bot, False, c)
+
     odd = lax.axis_index("tile") % 2
 
     @pl.when(odd == 1)
     def _():
-        pack(sib_ref, True)
-        pack(nxt_ref, False)
+        send(sib_ref, nxt_ref)
 
     @pl.when(odd == 0)
     def _():
-        pack(sib_ref, False)
-        pack(nxt_ref, True)
+        send(nxt_ref, sib_ref)
 
 
 def row_messages(air, courant):
@@ -123,16 +125,14 @@
     return jnp.where(sub < 3, n, roll(s, 5, 0))
 
 
-def halo_sum(weights, f, north, south):
+def halo_sum(scale, f, north, south):
     sub = iota((8, north.shape[1]), 0)
-    scale = jnp.zeros(sub.shape, f32)
-    for l in range(LEVELS):
-        scale = jnp.where(sub == l, weights[f, l], scale)
+    weight = jnp.concatenate([scale[f]] * (north.shape[1] // BLK), 1)
     rows = jnp.zeros(sub.shape, f32)
     for j in range(3):
         at = slice((f * 3 + j) * 8, (f * 3 + j + 1) * 8)
-        rows = jnp.where(sub == j, jnp.sum(north[at] * scale, axis=0, keepdims=True), rows)
-        rows = jnp.where(sub == 5 + j, jnp.sum(south[at] * scale, axis=0, keepdims=True), rows)
+        rows = jnp.where(sub == j, jnp.sum(north[at] * weight, axis=0, keepdims=True), rows)
+        rows = jnp.where(sub == 5 + j, jnp.sum(south[at] * weight, axis=0, keepdims=True), rows)
     return rows
 
 
@@ -222,18 +222,23 @@
     offsets[...] = lax.dot_general(to_dest, at_rank, along, preferred_element_type=f32) - 1.0
 
 
-def own_kernel(weights, *refs):
-    given, (strip_out, coef, message, sums, level_sum, routes, offsets, tiles), refs = (
-        refs[:7],
-        refs[7:15],
-        refs[15:],
-    )
-    here, (strip, sems) = refs[:6], refs[6:]
-    copies = start_all(zip(given, (*here, tiles)), sems)
-    wait_all(copies[:4])
-    route(*here[:4], routes, offsets)
-    wait_all(copies[4:6])
-    air, cour = here[4:6]
+def own_kernel(*refs):
+    given, made, refs = refs[:8], refs[8:18], refs[18:]
+    strip_out, coef, message, sums, level_sum, scale, numbers, routes, offsets, tiles = made
+    here, (strip, sems) = refs[:7], refs[7:]
+    half = given[7].at[pl.ds(0, HALF)]
+    copies = start_all(zip((*given[:7], half), (*here, tiles)), sems)
+    wait_all(copies[:5])
+    route(*here[1:5], routes, offsets)
+    weights, (air, cour) = here[0], here[5:7]
+    for f in range(FIELDS):
+        total = jnp.zeros((8, BLK), f32)
+        for l in range(LEVELS):
+            total = jnp.where(iota((8, BLK), 0) == l, weights[f, l], total)
+        scale[f] = total
+    wait_all(copies[5:7])
+    for k in range(3):
+        numbers[k] = cour[k]
     for side in range(2):
         lanes, own, shift = edge_lanes(side), own_columns(side, ROWS), SHIFTS[side]
         strips, coefs = [], []
@@ -246,7 +251,7 @@
             coef[side, k] = coefs[k]
         sums[side] = sum_strip(weights, strips)
         message[side] = message_rows(strips, coefs, sums[side])
-    copy = pltpu.make_async_copy(strip, strip_out, sems.at[7])
+    copy = pltpu.make_async_copy(strip, strip_out, sems.at[8])
     copy.start()
     for f in range(FIELDS):
         total = weights[f, 0] * air[f, 0]
@@ -254,10 +259,10 @@
             total = total + weights[f, l] * air[f, l]
         level_sum[f] = total
     copy.wait()
-    copies[6].wait()
-
-
-def own_parts(weights, *given):
+    copies[7].wait()
+
+
+def own_parts(*given):
     return pl.pallas_call(
         own_kernel,
         out_shape=(
@@ -266,21 +271,24 @@
             jax.ShapeDtypeStruct((2, ROWS, 128), f32),
             jax.ShapeDtypeStruct((2, ROWS, 128), f32),
             jax.ShapeDtypeStruct((FIELDS, ROWS, COLS), f32),
+            jax.ShapeDtypeStruct((FIELDS, 8, BLK), f32),
+            jax.ShapeDtypeStruct((3, ROWS, COLS), f32),
             jax.ShapeDtypeStruct((8, ENTRIES), jnp.int32),
             jax.ShapeDtypeStruct((DEVICES, 128), f32),
-            pltpu.VMEM(given[6].shape, bf16),
+            pltpu.VMEM((HALF, BLK, BLK), bf16),
         ),
-        in_specs=[in_smem] + [in_hbm] * 7,
-        out_specs=(in_hbm,) + (in_vmem,) * 7,
-        scratch_shapes=[pltpu.VMEM(x.shape, x.dtype) for x in given[:6]]
-        + [pltpu.VMEM((2, FIELDS, ROWS, 128), f32), pltpu.SemaphoreType.DMA((8,))],
+        in_specs=[in_hbm] * 8,
+        out_specs=(in_hbm,) + (in_vmem,) * 9,
+        scratch_shapes=[pltpu.SMEM(given[0].shape, f32)]
+        + [pltpu.VMEM(x.shape, x.dtype) for x in given[1:7]]
+        + [pltpu.VMEM((2, FIELDS, ROWS, 128), f32), pltpu.SemaphoreType.DMA((9,))],
         compiler_params=params(),
         cost_estimate=pl.CostEstimate(flops=1600000, bytes_accessed=1200000, transcendentals=0),
         name="own_parts",
-    )(*hbm(weights, *given))
-
-
-def halo_kernel(weights, sib, nxt, own_message, strip, coef, sums, send_w, send_e, halo):
+    )(*hbm(*given))
+
+
+def halo_kernel(scale, sib, nxt, own_message, strip, coef, sums, send_w, send_e, halo):
     for side, send in enumerate((send_w, send_e)):
         lanes, own, shift = edge_lanes(side), own_columns(side, 8), SHIFTS[side]
         north, south = north_south(sib[:, lanes], nxt[:, lanes])
@@ -301,14 +309,14 @@
             coef[side, k] = coefs[k]
         total = jnp.zeros((8, BLK), f32)
         for f in range(FIELDS):
-            rows = jnp.where(own, halo_sum(weights, f, north, south), 0.0)
+            rows = jnp.where(own, halo_sum(scale, f, north, south), 0.0)
             total = total + roll(rows, f * 16 + shift, 1)
         sums[side] = total
         send[:ROWS] = own_message[side]
         send[ROWS:] = message_rows(strips, coefs, sums[side])
 
 
-def column_messages(weights, sib, nxt, own_message):
+def column_messages(scale, sib, nxt, own_message):
     message = jax.ShapeDtypeStruct((32, 128), f32)
     return pl.pallas_call(
         halo_kernel,
@@ -319,13 +327,13 @@
             message,
             message,
         ),
-        in_specs=[in_smem] + [in_vmem] * 3,
+        in_specs=[in_vmem] * 4,
         out_specs=(in_vmem,) * 5,
         scratch_shapes=[pltpu.VMEM((2, FIELDS * 64, BLK), f32)],
         compiler_params=params(),
         cost_estimate=pl.CostEstimate(flops=100000, bytes_accessed=400000, transcendentals=0),
         name="column_messages",
-    )(*hbm(weights), sib, nxt, own_message)
+    )(scale, sib, nxt, own_message)
 
 
 def received(side, got):
@@ -360,40 +368,41 @@
     return scale
 
 
-def flux_kernel(weights, level_sum, given, sib, nxt, flux, sib_out, nxt_out, cour, sems):
-    copies = start_all([(given, cour), (sib, sib_out), (nxt, nxt_out)], sems)
-    copies[0].wait()
+def flux_kernel(scale, level_sum, cour, sib, nxt, stored, flux, sib_out, nxt_out, tiles, sems):
+    half = stored.at[pl.ds(HALF, ENTRIES - HALF)]
+    copies = start_all([(half, tiles), (sib, sib_out), (nxt, nxt_out)], sems)
     north, south = north_south(sib[...], nxt[...])
     three = [
         jnp.concatenate([cour[k], courant_rows(north[96:], south[96:], k)], 0) for k in range(3)
     ]
     coefs = coefficients(*three)
     for f in range(FIELDS):
-        rows = halo_sum(weights, f, north, south)
+        rows = halo_sum(scale, f, north, south)
         q = jnp.concatenate([level_sum[f], rows], 0)
         for _ in range(STEPS):
             q = step(q, coefs)
         q = q[:ROWS].astype(bf16).astype(f32)
         for c in range(COLS // BLK):
             flux[pl.ds(c * FIELDS + f, ROWS, stride=24), :] = q[:, c * BLK : (c + 1) * BLK]
-    wait_all(copies[1:])
-
-
-def flux_stencil(weights, level_sum, courant, sib, nxt):
+    wait_all(copies)
+
+
+def flux_stencil(scale, level_sum, courant, sib, nxt, tiles):
     return pl.pallas_call(
         flux_kernel,
         out_shape=(
             jax.ShapeDtypeStruct((ROWS * 24, BLK), f32),
             pltpu.HBM(sib.shape, bf16),
             pltpu.HBM(nxt.shape, bf16),
+            pltpu.VMEM((ENTRIES - HALF, BLK, BLK), bf16),
         ),
-        in_specs=[in_smem, in_vmem, in_hbm, in_vmem, in_vmem],
-        out_specs=(in_vmem, in_hbm, in_hbm),
-        scratch_shapes=[pltpu.VMEM(courant.shape, f32), pltpu.SemaphoreType.DMA((3,))],
+        in_specs=[in_vmem] * 5 + [in_hbm],
+        out_specs=(in_vmem, in_hbm, in_hbm, in_vmem),
+        scratch_shapes=[pltpu.SemaphoreType.DMA((3,))],
         compiler_params=params(),
         cost_estimate=pl.CostEstimate(flops=3000000, bytes_accessed=1000000, transcendentals=0),
         name="flux_stencil",
-    )(*hbm(weights), level_sum, *hbm(courant), sib, nxt)
+    )(scale, level_sum, courant, sib, nxt, *hbm(tiles))
 
 
 def advance(c, q, below, above):
@@ -580,7 +589,9 @@
 
 
 def send_kernel(routes, flux_in, halo_strip, *refs):
-    edges, (offsets, tiles, out, *kept, flux, total, coef, sems) = refs[:6], refs[6:]
+    edges, (offsets, early, late, out, *kept, flux, total, coef, numbers, sems) = refs[:6], refs[6:]
+    listed = pltpu.make_async_copy(routes, numbers, sems.at[4])
+    listed.start()
     copies = start_all(zip((halo_strip, *edges[4:6]), kept), sems)
     flux[0:8, :] = jnp.zeros((8, BLK), f32)
     flux[8 : 8 + ROWS * 24, :] = flux_in[...]
@@ -590,23 +601,25 @@
     copies[3].start()
     total[...] = jnp.zeros(total.shape, f32)
     total[pl.ds(BACK, DEVICES, stride=CHUNK), :] = offsets[...]
+    listed.wait()
     for t in range(0, ENTRIES, 4):
-        at = [routes[0, t + i] for i in range(4)]
+        at = [numbers[0, t + i] for i in range(4)]
+        tiles, u = (early, t) if t < HALF else (late, t - HALF)
         w = jnp.concatenate(
             [
-                jnp.concatenate([tiles[t], tiles[t + 1]], 0),
-                jnp.concatenate([tiles[t + 2], tiles[t + 3]], 0),
+                jnp.concatenate([tiles[u], tiles[u + 1]], 0),
+                jnp.concatenate([tiles[u + 2], tiles[u + 3]], 0),
             ],
             1,
         )
         r = jnp.dot(four_rows(flux, at), w, preferred_element_type=f32)
         for i, piece in enumerate(four_results(r)):
-            total[pl.ds(routes[1, t + i], 4), :] = piece
+            total[pl.ds(numbers[1, t + i], 4), :] = piece
     out[...] = total[...].astype(bf16)
     wait_all(copies)
 
 
-def send_blocks(routes, flux, halo_strip, edges, offsets, tiles):
+def send_blocks(routes, flux, halo_strip, edges, offsets, early, late):
     return pl.pallas_call(
         send_kernel,
         out_shape=(
@@ -616,18 +629,19 @@
             pltpu.HBM((32, 128), f32),
             pltpu.HBM((2, 3, 32, 128), f32),
         ),
-        in_specs=[in_smem] + [in_vmem] * 10,
+        in_specs=[in_vmem] * 12,
         out_specs=(in_vmem,) + (in_hbm,) * 4,
         scratch_shapes=[
             pltpu.VMEM((ROWS * 24 + 16, BLK), f32),
             pltpu.VMEM((DEVICES * CHUNK, BLK), f32),
             pltpu.VMEM((2, 3, 32, 128), f32),
-            pltpu.SemaphoreType.DMA((4,)),
+            pltpu.SMEM((8, ENTRIES), jnp.int32),
+            pltpu.SemaphoreType.DMA((5,)),
         ],
         compiler_params=params(),
         cost_estimate=pl.CostEstimate(flops=40000000, bytes_accessed=11000000, transcendentals=0),
         name="send_blocks",
-    )(routes, flux, halo_strip, *edges, offsets, tiles)
+    )(routes, flux, halo_strip, *edges, offsets, early, late)
 
 
 def ocean_kernel(payload, ocean, mixing, mask, flux_out, back, got, ret, packed, kept, sems):
@@ -655,17 +669,21 @@
     copies = [pltpu.make_async_copy(kept, flux_out, sems.at[0])]
     copies[0].start()
     surface = jnp.concatenate(surface, 1)
-    lanes = iota((DEVICES, OCEAN_ROWS), 1).astype(f32)
-    for j in range(CAP):
-        pick = (offsets[:, j : j + 1] == lanes).astype(f32).astype(bf16)
-        rows = jnp.dot(pick, surface, preferred_element_type=f32)
-        for f in range(FIELDS):
-            ret[pl.ds(j * FIELDS + f, DEVICES, stride=BACK), :] = rows[:, f * BLK : (f + 1) * BLK]
-    packed[...] = ret[...].astype(bf16)
-    copies.append(pltpu.make_async_copy(packed, back, sems.at[1]))
-    copies[1].start()
-    for copy in copies:
-        copy.wait()
+    half = DEVICES // 2
+    lanes = iota((half, OCEAN_ROWS), 1).astype(f32)
+    for h in range(2):
+        mine = offsets[h * half : (h + 1) * half]
+        for j in range(CAP):
+            pick = (mine[:, j : j + 1] == lanes).astype(f32).astype(bf16)
+            rows = jnp.dot(pick, surface, preferred_element_type=f32)
+            for f in range(FIELDS):
+                at = pl.ds(h * half * BACK + j * FIELDS + f, half, stride=BACK)
+                ret[at, :] = rows[:, f * BLK : (f + 1) * BLK]
+        at = pl.ds(h * half * BACK, half * BACK)
+        packed[at, :] = ret[at, :].astype(bf16)
+        copies.append(pltpu.make_async_copy(packed.at[at], back.at[at], sems.at[1 + h]))
+        copies[1 + h].start()
+    wait_all(copies)
 
 
 def ocean_surface(payload, ocean, mixing, mask):
@@ -682,7 +700,7 @@
             pltpu.VMEM((DEVICES * BACK, BLK), f32),
             pltpu.VMEM((DEVICES * BACK, BLK), bf16),
             pltpu.VMEM((FIELDS, OCEAN_ROWS, BLK), f32),
-            pltpu.SemaphoreType.DMA((2,)),
+            pltpu.SemaphoreType.DMA((3,)),
         ],
         compiler_params=params(),
         cost_estimate=pl.CostEstimate(flops=100000000, bytes_accessed=4000000, transcendentals=0),
@@ -690,18 +708,21 @@
     )(payload, ocean, mixing, mask)
 
 
-def return_kernel(routes, payload, stored, out, got, total, arrived, tiles, sems):
-    first = start_all([(payload, arrived)], sems)[0]
-    waits = start_tiles(stored, tiles, sems.at[pl.ds(1, 6)], (0, 48, 96, 144, 192, 240, ENTRIES))
+PARTS = (0, 16, 56, 104, 160, 224, ENTRIES)
+
+
+def return_kernel(routes, payload, stored, out, got, total, numbers, tiles, done, sems):
+    listed = start_all([(routes, numbers)], sems)[0]
+    waits = start_tiles(stored, tiles, sems.at[pl.ds(1, 6)], PARTS)
     got[0:8, :] = jnp.zeros((8, BLK), f32)
+    got[8 : 8 + DEVICES * BACK, :] = payload[...].astype(f32)
     got[8 + DEVICES * BACK :, :] = jnp.zeros((8, BLK), f32)
     total[...] = jnp.zeros(total.shape, f32)
-    first.wait()
-    got[8 : 8 + DEVICES * BACK, :] = arrived[...].astype(f32)
+    listed.wait()
     for t in range(0, ENTRIES, 4):
         if t in waits:
             waits[t].wait()
-        at = [routes[2, t + i] for i in range(4)]
+        at = [numbers[2, t + i] for i in range(4)]
         w = jnp.concatenate(
             [
                 jnp.concatenate([tiles[t], tiles[t + 1]], 1),
@@ -713,24 +734,30 @@
             four_rows(got, at), w, (((1,), (1,)), ((), ())), preferred_element_type=f32
         )
         for i, piece in enumerate(four_results(r)):
-            here = pl.ds(routes[0, t + i], 4)
+            here = pl.ds(numbers[0, t + i], 4)
             total[here, :] = total[here, :] + piece
+    copies = []
     for f in range(FIELDS):
         for c in range(COLS // BLK):
-            out[f, :, c * BLK : (c + 1) * BLK] = total[pl.ds(c * FIELDS + f, ROWS, stride=24), :]
+            done[f, :, c * BLK : (c + 1) * BLK] = total[pl.ds(c * FIELDS + f, ROWS, stride=24), :]
+        copies.append(pltpu.make_async_copy(done.at[f], out.at[f], sems.at[7 + f]))
+        copies[f].start()
+    wait_all(copies)
 
 
 def return_blocks(routes, payload, tiles):
     return pl.pallas_call(
         return_kernel,
-        out_shape=jax.ShapeDtypeStruct((FIELDS, ROWS, COLS), f32),
-        in_specs=[in_smem, pl.BlockSpec(memory_space=pl.ANY), in_hbm],
+        out_shape=pltpu.HBM((FIELDS, ROWS, COLS), f32),
+        in_specs=[in_vmem, in_vmem, in_hbm],
+        out_specs=in_hbm,
         scratch_shapes=[
             pltpu.VMEM((DEVICES * BACK + 16, BLK), f32),
             pltpu.VMEM((ROWS * 24, BLK), f32),
-            pltpu.VMEM((DEVICES * BACK, BLK), bf16),
+            pltpu.SMEM((8, ENTRIES), jnp.int32),
             pltpu.VMEM((ENTRIES, BLK, BLK), bf16),
-            pltpu.SemaphoreType.DMA((7,)),
+            pltpu.VMEM((FIELDS, ROWS, COLS), f32),
+            pltpu.SemaphoreType.DMA((11,)),
         ],
         compiler_params=params(24),
         cost_estimate=pl.CostEstimate(flops=40000000, bytes_accessed=11000000, transcendentals=0),
@@ -762,18 +789,21 @@
     inner = [(i, i + 1) for i in range(1, tile_count - 1, 2)]
     nxt = lax.ppermute(nxt, "tile", inner + [(b, a) for a, b in inner])
     sib = lax.ppermute(sib, "tile", [(i, i ^ 1) for i in range(tile_count)])
-    own_strip, own_coef, own_message, own_sums, level_sum, routes, offsets, tiles = own_parts(
+    own_strip, own_coef, own_message, own_sums, level_sum, scale, numbers, *rest = own_parts(
         *(level_weights, src_block, owner.reshape(1, -1), offset, tile_index),
         *(atmos_state, courant, remap_tiles),
     )
+    routes, offsets, early = rest
     halo_strip, halo_coef, halo_sums, send_w, send_e = column_messages(
-        level_weights, sib, nxt, own_message
+        scale, sib, nxt, own_message
     )
     from_e = lax.ppermute(send_w, "face", [((i + 1) % faces, i) for i in range(faces)])
     from_w = lax.ppermute(send_e, "face", [(i, (i + 1) % faces) for i in range(faces)])
-    flux, sib, nxt = flux_stencil(level_weights, level_sum, courant, sib, nxt)
+    flux, sib, nxt, late = flux_stencil(scale, level_sum, numbers, sib, nxt, remap_tiles)
     edges = (own_sums, halo_sums, own_coef, halo_coef, from_w, from_e)
-    message, *edges = send_blocks(routes, flux, halo_strip, edges, offsets, tiles)
+    message, *edges = send_blocks(
+        routes, flux, halo_strip, edges, offsets, early, late
+    )
     halo_strip, from_w, from_e, strip_coef = edges
     message = exchange(message, CHUNK)
     ocean_flux, back = ocean_surface(message, ocean_state, mixing, land_mask)

time: 75.6 us -> 72.3 us (0.956)
  Pallas kernels: 31.8 us -> 26.7 us
  blocking collectives: 24.3 us -> 26.2 us
    all_to_all x1, blocking collectives: 24.3 us -> 26.2 us  [exchange(): lax.all_to_all(x, ('face', 'tile'), split_axis=0, concat_axis=0, tiled=True)]
    pallas_call x1, Pallas kernels: 5.45 us -> 3.87 us  [own_parts(): pl.pallas_call(own_kernel, out_shape=(pltpu.HBM((2, FIELDS, ROWS, 128), f...]
    pallas_call x1, Pallas kernels: 6.43 us -> 5.36 us  [return_blocks(): pl.pallas_call(return_kernel, out_shape=pltpu.HBM((FIELDS, ROWS, COLS), f...]
    pallas_call x1, Pallas kernels: 2.88 us -> 1.91 us  [flux_stencil(): pl.pallas_call(flux_kernel, out_shape=(jax.ShapeDtypeStruct((ROWS * 24, B...]
  transfers between devices with their start and end apart: 5 -> 5, of which waited for: 1 -> 1; matrix products, arithmetic and copies ran while one was open for 0% -> 0% of each run, Pallas kernels for 23% -> 21%
where the time goes in v3:
time: 72.3 us; the launch traced here: 72.1 us
  Pallas kernels  26.7 us (37%)
  blocking collectives  26.2 us (36%)
  starting transfers between devices  12.3 us (17%)
  waiting for transfers between devices  5.85 us (8%)
  between operations  0.92 us (1%)
    all_to_all x1, blocking collectives, exchange(): lax.all_to_all(x, ('face', 'tile'), split_axis=0, concat_axis=0, tiled=True)  26.2 us
    pallas_call x1, Pallas kernels, air_steps(): pl.pallas_call(air_kernel, out_shape=(pltpu.HBM(air.shape, f32), pltpu.HB...  9.35 us
    all_to_all x1, waiting for transfers between devices, exchange(): lax.all_to_all(x, ('face', 'tile'), split_axis=0, concat_axis=0, tiled=True)  5.83 us
    pallas_call x1, Pallas kernels, return_blocks(): pl.pallas_call(return_kernel, out_shape=pltpu.HBM((FIELDS, ROWS, COLS), f...  5.36 us
    all_to_all x1, starting transfers between devices, exchange(): lax.all_to_all(x, ('face', 'tile'), split_axis=0, concat_axis=0, tiled=True)  4.61 us
    pallas_call x1, Pallas kernels, own_parts(): pl.pallas_call(own_kernel, out_shape=(pltpu.HBM((2, FIELDS, ROWS, 128), f...  3.87 us
    ppermute x1, starting transfers between devices, shards(): nxt = lax.ppermute(nxt, 'tile', inner + [(b, a) for a, b in inner])  3.53 us
    pallas_call x1, Pallas kernels, send_blocks(): pl.pallas_call(send_kernel, out_shape=(jax.ShapeDtypeStruct((DEVICES * CH...  2.71 us
  transfers between devices with their start and end apart: 5, of which 1 were waited for; matrix products, arithmetic and copies ran while one was open for 0% of the time, Pallas kernels for 21%

profile of v3, /device:TPU:1, one launch (start us, length us, event | category | flops | bytes accessed | tf_op | source)
XLA Modules:
  0.0 72.1 jit_solution(17502395211383139742)
XLA Ops:
  0.6 1.7 %row_messages.1 = (bf16[112,768]{1,0:T(8,128)(2,1)S(1)}, bf16[112,768]{1,0:T(8,128)(2,1)S(1)}) custom-call(f32[4,8,24,768]{3,2,1,0:T(8,128)} %air.3, f32[3,24,768]{2,1,0:T(8,128)} %refs_4_.3), custom_call_target="tpu_custom_call" | custom-call | flops 400000 | bytes 2000000 | tf_op jit(solution)/shard_map/row_messages/pallas_call | solution.py:105
  2.3 1.5 %collective-permute-start = (bf16[112,768]{1,0:T(8,128)(2,1)S(1)}, bf16[112,768]{1,0:T(8,128)(2,1)S(1)}, u32[]{:S(2)}, u32[]{:S(2)}) collective-permute-start(bf16[112,768]{1,0:T(8,128)(2,1)S(1)} %get-tuple-element.37), channel_id=1, source_target_pairs={{0,1},{1,0},{2,3},{3,2},{4,5},{5,4},{6,7},{7,6},{8,9},{9,8},{10,11... | collective-permute-start | bytes 516104 | tf_op jit(solution)/shard_map/ppermute | solution.py:791
  3.8 3.5 %collective-permute-start.1 = (bf16[112,768]{1,0:T(8,128)(2,1)S(1)}, bf16[112,768]{1,0:T(8,128)(2,1)S(1)}, u32[]{:S(2)}, u32[]{:S(2)}) collective-permute-start(bf16[112,768]{1,0:T(8,128)(2,1)S(1)} %get-tuple-element.38), channel_id=1, source_target_pairs={{1,2},{3,4},{5,6},{7,8},{9,10},{11,12},{13,14},{15,16},{17,18},{19... | collective-permute-start | bytes 516104 | tf_op jit(solution)/shard_map/ppermute | solution.py:790
  7.3 3.9 %own_parts.1 = (f32[2,4,24,128]{3,2,1,0:T(8,128)}, f32[2,3,24,128]{3,2,1,0:T(8,128)S(1)}, f32[2,24,128]{2,1,0:T(8,128)S(1)}, f32[2,24,128]{2,1,0:T(8,128)S(1)}, ...) custom-call(f32[4,8]{1,0:T(4,128)} %refs_0_.1, ...), custom_call_target="tpu_custom_call" | custom-call | flops 1600000 | bytes 1200000 | tf_op jit(solution)/shard_map/own_parts/pallas_call | solution.py:266
  11.2 0.0 collective-permute-done.sib
  11.2 0.0 collective-permute-done.1.nxt
  11.2 0.4 column_messages.1
  11.6 1.2 %collective-permute-start.2 = (f32[32,128]{1,0:T(8,128)S(1)}, f32[32,128]{1,0:T(8,128)S(1)}, u32[]{:S(2)}, u32[]{:S(2)}) collective-permute-start(f32[32,128]{1,0:T(8,128)S(1)} %get-tuple-element.46), channel_id=1, source_target_pairs={{0,32},{32,64},{64,96},{96,0},{1,33},{33,65},{65,97},{97,1},{2,34}... | collective-permute-start | bytes 49160 | tf_op jit(solution)/shard_map/ppermute | solution.py:801
  12.8 1.5 %collective-permute-start.3 = (f32[32,128]{1,0:T(8,128)S(1)}, f32[32,128]{1,0:T(8,128)S(1)}, u32[]{:S(2)}, u32[]{:S(2)}) collective-permute-start(f32[32,128]{1,0:T(8,128)S(1)} %get-tuple-element.47), channel_id=1, source_target_pairs={{32,0},{64,32},{96,64},{0,96},{33,1},{65,33},{97,65},{1,97},{34,2}... | collective-permute-start | bytes 49160 | tf_op jit(solution)/shard_map/ppermute | solution.py:800
  14.3 1.9 %flux_stencil.1 = (f32[576,128]{1,0:T(8,128)S(1)}, bf16[112,768]{1,0:T(8,128)(2,1)}, bf16[112,768]{1,0:T(8,128)(2,1)}, bf16[80,128,128]{2,1,0:T(8,128)(2,1)S(1)}) custom-call(f32[4,8,128]{2,1,0:T(8,128)S(1)} %get-tuple-element.34.scale, f32[4,24,768]{2,1,0:T(8,128)S(1)} %get-tuple-element.35.level_sum, f32[3,24,768]{2,1,0:T(8,128)S(1)} %get-tuple-element.36.cour, ...), custom_call_target="tpu_custom_call" | custom-call | flops 3000000 | bytes 1000000 | tf_op jit(solution)/shard_map/flux_stencil/pallas_call | solution.py:391
  16.2 0.0 collective-permute-done.2.refs_4_
  16.2 0.0 collective-permute-done.3.refs_5_
  16.2 0.0 copy-start
  16.2 0.0 copy-start.1
  16.3 0.0 copy-start.2
  16.3 2.7 %send_blocks.1 = (bf16[2816,128]{1,0:T(8,128)(2,1)S(1)}, f32[2,4,8,128]{3,2,1,0:T(8,128)}, f32[32,128]{1,0:T(8,128)}, f32[32,128]{1,0:T(8,128)}, f32[2,3,32,128]{3,2,1,0:T(8,128)}) custom-call(s32[8,288]{1,0:T(8,128)S(1)} %get-tuple-element.33.routes, f32[576,128]{1,0:T(8,128)S(1)} %get-tuple-element.39.flux_in, ...), custom_call_target="tpu_custom_call" | custom-call | flops 40000000 | bytes 11000000 | tf_op jit(solution)/shard_map/send_blocks/pallas_call | solution.py:623
  19.0 26.2 %all_to_all.10 = bf16[1408,2,128]{2,1,0:T(2,128)(2,1)S(1)} all-to-all(bf16[1408,2,128]{2,1,0:T(2,128)(2,1)S(1)} %bitcast.7), channel_id=1, replica_groups=mesh['face'=4,'tile'=32] {'face','tile'}, dimensions={0} | all-to-all | bytes 1441792 | tf_op jit(solution)/shard_map/all_to_all | solution.py:770
  45.2 0.0 copy-done
  45.2 0.0 copy-done.1
  45.2 1.5 %ocean_surface.1 = (f32[4,64,128]{2,1,0:T(8,128)}, bf16[2560,128]{1,0:T(8,128)(2,1)}) custom-call(bf16[2816,128]{1,0:T(8,128)(2,1)S(1)} %bitcast.5, f32[4,8,64,128]{3,2,1,0:T(8,128)S(1)} %copy-done, f32[64,128]{1,0:T(8,128)S(1)} %copy-done.1, s32[64,128]{1,0:T(8,128)S(1)} %copy-done.2), custom_call_target="tpu_custom_call" | custom-call | flops 100000000 | bytes 4000000 | tf_op jit(solution)/shard_map/ocean_surface/pallas_call | solution.py:690
  46.7 4.6 %all-to-all-start.1 = ((bf16[640,4,128]{2,1,0:T(4,128)(2,1)}), bf16[640,4,128]{2,1,0:T(4,128)(2,1)S(1)}, u32[]{:S(2)}, u32[]{:S(2)}) async-start(bf16[640,4,128]{2,1,0:T(4,128)(2,1)} %bitcast.8), calls=%async_computation.1 | async-start | bytes 1310720 | tf_op jit(solution)/shard_map/all_to_all | solution.py:770
  51.3 9.4 %air_steps.1 = (f32[4,8,24,768]{3,2,1,0:T(8,128)}, f32[4,8,64,128]{3,2,1,0:T(8,128)}) custom-call(f32[4,8,24,768]{3,2,1,0:T(8,128)} %air.3, f32[4,64,128]{2,1,0:T(8,128)} %get-tuple-element.52.refs_0_, f32[4,8,64,128]{3,2,1,0:T(8,128)} %refs_1_.3, f32[64,128]{1,0:T(8,128)} %refs_2_.1, s32[64,128]{1,0:T(8,128)} %refs_3_.3, f32[3,24,768]{2,1,0:T(8,128)} %refs_4_.3, ...), custom_call_target="tpu_custom_call" | custom-call | flops 30000000 | bytes 6000000 | tf_op jit(solution)/shard_map/air_steps/pallas_call | solution.py:528
  60.7 5.8 %all-to-all-done.1 = bf16[640,4,128]{2,1,0:T(4,128)(2,1)S(1)} async-done(((bf16[640,4,128]{2,1,0:T(4,128)(2,1)}), bf16[640,4,128]{2,1,0:T(4,128)(2,1)S(1)}, u32[]{:S(2)}, u32[]{:S(2)}) %all-to-all-start.1) | async-done | bytes 655392 | tf_op jit(solution)/shard_map/all_to_all | solution.py:770
  66.5 5.4 %return_blocks.1 = f32[4,24,768]{2,1,0:T(8,128)} custom-call(s32[8,288]{1,0:T(8,128)S(1)} %get-tuple-element.33.routes, bf16[2560,128]{1,0:T(8,128)(2,1)S(1)} %bitcast.6, bf16[288,128,128]{2,1,0:T(8,128)(2,1)} %stored.3), custom_call_target="tpu_custom_call" | custom-call | flops 40000000 | bytes 11000000 | tf_op jit(solution)/shard_map/return_blocks/pallas_call | solution.py:749
  (1 shorter events, 0.0 us)
Async XLA Ops:
  2.3 8.9 %collective-permute-start = (bf16[112,768]{1,0:T(8,128)(2,1)S(1)}, bf16[112,768]{1,0:T(8,128)(2,1)S(1)}, u32[]{:S(2)}, u32[]{:S(2)}) collective-permute-start(bf16[112,768]{1,0:T(8,128)(2,1)S(1)} %get-tuple-element.37), channel_id=1, source_target_pairs={{0,1},{1,0},{2,3},{3,2},{4,5},{5,4},{6,7},{7,6},{8,9},{9,8},{10,11... | collective-permute-start | bytes 516104 | tf_op jit(solution)/shard_map/ppermute | solution.py:791
  3.8 7.4 %collective-permute-start.1 = (bf16[112,768]{1,0:T(8,128)(2,1)S(1)}, bf16[112,768]{1,0:T(8,128)(2,1)S(1)}, u32[]{:S(2)}, u32[]{:S(2)}) collective-permute-start(bf16[112,768]{1,0:T(8,128)(2,1)S(1)} %get-tuple-element.38), channel_id=1, source_target_pairs={{1,2},{3,4},{5,6},{7,8},{9,10},{11,12},{13,14},{15,16},{17,18},{19... | collective-permute-start | bytes 516104 | tf_op jit(solution)/shard_map/ppermute | solution.py:790
  11.6 4.6 %collective-permute-start.2 = (f32[32,128]{1,0:T(8,128)S(1)}, f32[32,128]{1,0:T(8,128)S(1)}, u32[]{:S(2)}, u32[]{:S(2)}) collective-permute-start(f32[32,128]{1,0:T(8,128)S(1)} %get-tuple-element.46), channel_id=1, source_target_pairs={{0,32},{32,64},{64,96},{96,0},{1,33},{33,65},{65,97},{97,1},{2,34}... | collective-permute-start | bytes 49160 | tf_op jit(solution)/shard_map/ppermute | solution.py:801
  12.8 3.4 %collective-permute-start.3 = (f32[32,128]{1,0:T(8,128)S(1)}, f32[32,128]{1,0:T(8,128)S(1)}, u32[]{:S(2)}, u32[]{:S(2)}) collective-permute-start(f32[32,128]{1,0:T(8,128)S(1)} %get-tuple-element.47), channel_id=1, source_target_pairs={{32,0},{64,32},{96,64},{0,96},{33,1},{65,33},{97,65},{1,97},{34,2}... | collective-permute-start | bytes 49160 | tf_op jit(solution)/shard_map/ppermute | solution.py:800
  16.2 29.0 %copy-start = (f32[4,8,64,128]{3,2,1,0:T(8,128)S(1)}, f32[4,8,64,128]{3,2,1,0:T(8,128)}, u32[]{:S(2)}) copy-start(f32[4,8,64,128]{3,2,1,0:T(8,128)} %refs_1_.3) | copy-start | bytes 3145732
  16.2 29.0 %copy-start.1 = (f32[64,128]{1,0:T(8,128)S(1)}, f32[64,128]{1,0:T(8,128)}, u32[]{:S(2)}) copy-start(f32[64,128]{1,0:T(8,128)} %refs_2_.1) | copy-start | bytes 98308
  16.3 29.0 %copy-start.2 = (s32[64,128]{1,0:T(8,128)S(1)}, s32[64,128]{1,0:T(8,128)}, u32[]{:S(2)}) copy-start(s32[64,128]{1,0:T(8,128)} %refs_3_.3) | copy-start | bytes 98308
  46.7 19.8 %all-to-all-start.1 = ((bf16[640,4,128]{2,1,0:T(4,128)(2,1)}), bf16[640,4,128]{2,1,0:T(4,128)(2,1)S(1)}, u32[]{:S(2)}, u32[]{:S(2)}) async-start(bf16[640,4,128]{2,1,0:T(4,128)(2,1)} %bitcast.8), calls=%async_computation.1 | async-start | bytes 1310720 | tf_op jit(solution)/shard_map/all_to_all | solution.py:770

commit v4 on v3

--- a/solution.py
+++ b/solution.py
@@ -54,12 +54,12 @@
     return dict(zip(bounds, start_all(pairs, sems)))
 
 
-def row_kernel(air, cour, sib_ref, nxt_ref, top, bot, top_cour, bot_cour, sems):
+def row_kernel(air, cour, nxt_ref, sib_ref, top, bot, top_cour, bot_cour, sems):
     pairs = [(cour.at[:, pl.ds(0, 8), :], top_cour), (cour.at[:, pl.ds(16, 8), :], bot_cour)]
     for c in range(COLS // BLK):
         lanes = pl.ds(c * BLK, BLK)
-        pairs.append((air.at[:, :, pl.ds(0, 8), lanes], top.at[c]))
-        pairs.append((air.at[:, :, pl.ds(16, 8), lanes], bot.at[c]))
+        pairs.append((air.at[:, :, pl.ds(0, 4), lanes], top.at[c]))
+        pairs.append((air.at[:, :, pl.ds(20, 4), lanes], bot.at[c]))
     copies = start_all(pairs, sems)
 
     def pack_numbers(out, at_top):
@@ -70,11 +70,11 @@
         out[96:112, :] = jnp.concatenate([pair, last], 0).astype(bf16)
 
     def pack(out, at_top, c):
-        first, rows = (0, top) if at_top else (5, bot)
-        flat = rows.at[c].reshape(FIELDS * LEVELS * 8, BLK)
+        first, rows = (0, top) if at_top else (1, bot)
+        flat = rows.at[c].reshape(FIELDS * LEVELS * 4, BLK)
 
         def tile(i):
-            return flat[pl.ds(i // 3 * 64 + first + i % 3, LEVELS, stride=8), :]
+            return flat[pl.ds(i // 3 * 32 + first + i % 3, LEVELS, stride=4), :]
 
         for i in range(0, FIELDS * 3, 2):
             both = jnp.concatenate([tile(i), tile(i + 1)], 0)
@@ -107,7 +107,7 @@
         out_shape=(shape, shape),
         in_specs=[in_hbm] * 2,
         out_specs=(in_vmem,) * 2,
-        scratch_shapes=[pltpu.VMEM((COLS // BLK, FIELDS, LEVELS, 8, BLK), f32)] * 2
+        scratch_shapes=[pltpu.VMEM((COLS // BLK, FIELDS, LEVELS, 4, BLK), f32)] * 2
         + [pltpu.VMEM((3, 8, COLS), f32)] * 2
         + [pltpu.SemaphoreType.DMA((14,))],
         compiler_params=params(),
@@ -288,7 +288,7 @@
     )(*hbm(*given))
 
 
-def halo_kernel(scale, sib, nxt, own_message, strip, coef, sums, send_w, send_e, halo):
+def halo_kernel(scale, nxt, sib, own_message, strip, coef, sums, send_w, send_e, halo):
     for side, send in enumerate((send_w, send_e)):
         lanes, own, shift = edge_lanes(side), own_columns(side, 8), SHIFTS[side]
         north, south = north_south(sib[:, lanes], nxt[:, lanes])
@@ -316,7 +316,7 @@
         send[ROWS:] = message_rows(strips, coefs, sums[side])
 
 
-def column_messages(scale, sib, nxt, own_message):
+def column_messages(scale, nxt, sib, own_message):
     message = jax.ShapeDtypeStruct((32, 128), f32)
     return pl.pallas_call(
         halo_kernel,
@@ -333,7 +333,7 @@
         compiler_params=params(),
         cost_estimate=pl.CostEstimate(flops=100000, bytes_accessed=400000, transcendentals=0),
         name="column_messages",
-    )(scale, sib, nxt, own_message)
+    )(scale, nxt, sib, own_message)
 
 
 def received(side, got):
@@ -368,7 +368,7 @@
     return scale
 
 
-def flux_kernel(scale, level_sum, cour, sib, nxt, stored, flux, sib_out, nxt_out, tiles, sems):
+def flux_kernel(scale, level_sum, cour, nxt, sib, stored, flux, nxt_out, sib_out, tiles, sems):
     half = stored.at[pl.ds(HALF, ENTRIES - HALF)]
     copies = start_all([(half, tiles), (sib, sib_out), (nxt, nxt_out)], sems)
     north, south = north_south(sib[...], nxt[...])
@@ -387,13 +387,13 @@
     wait_all(copies)
 
 
-def flux_stencil(scale, level_sum, courant, sib, nxt, tiles):
+def flux_stencil(scale, level_sum, courant, nxt, sib, tiles):
     return pl.pallas_call(
         flux_kernel,
         out_shape=(
             jax.ShapeDtypeStruct((ROWS * 24, BLK), f32),
+            pltpu.HBM(nxt.shape, bf16),
             pltpu.HBM(sib.shape, bf16),
-            pltpu.HBM(nxt.shape, bf16),
             pltpu.VMEM((ENTRIES - HALF, BLK, BLK), bf16),
         ),
         in_specs=[in_vmem] * 5 + [in_hbm],
@@ -402,7 +402,7 @@
         compiler_params=params(),
         cost_estimate=pl.CostEstimate(flops=3000000, bytes_accessed=1000000, transcendentals=0),
         name="flux_stencil",
-    )(scale, level_sum, courant, sib, nxt, *hbm(tiles))
+    )(scale, level_sum, courant, nxt, sib, *hbm(tiles))
 
 
 def advance(c, q, below, above):
@@ -669,9 +669,9 @@
     copies = [pltpu.make_async_copy(kept, flux_out, sems.at[0])]
     copies[0].start()
     surface = jnp.concatenate(surface, 1)
-    half = DEVICES // 2
+    half = DEVICES // 4
     lanes = iota((half, OCEAN_ROWS), 1).astype(f32)
-    for h in range(2):
+    for h in range(4):
         mine = offsets[h * half : (h + 1) * half]
         for j in range(CAP):
             pick = (mine[:, j : j + 1] == lanes).astype(f32).astype(bf16)
@@ -700,7 +700,7 @@
             pltpu.VMEM((DEVICES * BACK, BLK), f32),
             pltpu.VMEM((DEVICES * BACK, BLK), bf16),
             pltpu.VMEM((FIELDS, OCEAN_ROWS, BLK), f32),
-            pltpu.SemaphoreType.DMA((3,)),
+            pltpu.SemaphoreType.DMA((5,)),
         ],
         compiler_params=params(),
         cost_estimate=pl.CostEstimate(flops=100000000, bytes_accessed=4000000, transcendentals=0),
@@ -785,7 +785,7 @@
     land_mask,
 ):
     faces, tile_count = lax.axis_size("face"), lax.axis_size("tile")
-    sib, nxt = row_messages(atmos_state, courant)
+    nxt, sib = row_messages(atmos_state, courant)
     inner = [(i, i + 1) for i in range(1, tile_count - 1, 2)]
     nxt = lax.ppermute(nxt, "tile", inner + [(b, a) for a, b in inner])
     sib = lax.ppermute(sib, "tile", [(i, i ^ 1) for i in range(tile_count)])
@@ -795,11 +795,11 @@
     )
     routes, offsets, early = rest
     halo_strip, halo_coef, halo_sums, send_w, send_e = column_messages(
-        scale, sib, nxt, own_message
+        scale, nxt, sib, own_message
     )
     from_e = lax.ppermute(send_w, "face", [((i + 1) % faces, i) for i in range(faces)])
     from_w = lax.ppermute(send_e, "face", [(i, (i + 1) % faces) for i in range(faces)])
-    flux, sib, nxt, late = flux_stencil(scale, level_sum, numbers, sib, nxt, remap_tiles)
+    flux, nxt, sib, late = flux_stencil(scale, level_sum, numbers, nxt, sib, remap_tiles)
     edges = (own_sums, halo_sums, own_coef, halo_coef, from_w, from_e)
     message, *edges = send_blocks(
         routes, flux, halo_strip, edges, offsets, early, late

time: 72.3 us -> 71.9 us (level)
    ppermute x1, starting transfers between devices: 1.5 us -> 0.09 us  [shards(): sib = lax.ppermute(sib, 'tile', [(i, i ^ 1) for i in range(tile_count)])]
    ppermute x1, starting transfers between devices: 3.53 us -> 4.94 us  [shards(): nxt = lax.ppermute(nxt, 'tile', inner + [(b, a) for a, b in inner])]
where the time goes in v4:
time: 71.9 us; the launch traced here: 71.6 us
  Pallas kernels  26.4 us (37%)
  blocking collectives  26.1 us (36%)
  starting transfers between devices  12.3 us (17%)
  waiting for transfers between devices  5.85 us (8%)
  between operations  0.92 us (1%)
    all_to_all x1, blocking collectives, exchange(): lax.all_to_all(x, ('face', 'tile'), split_axis=0, concat_axis=0, tiled=True)  26.1 us
    pallas_call x1, Pallas kernels, air_steps(): pl.pallas_call(air_kernel, out_shape=(pltpu.HBM(air.shape, f32), pltpu.HB...  9.35 us
    all_to_all x1, waiting for transfers between devices, exchange(): lax.all_to_all(x, ('face', 'tile'), split_axis=0, concat_axis=0, tiled=True)  5.83 us
    pallas_call x1, Pallas kernels, return_blocks(): pl.pallas_call(return_kernel, out_shape=pltpu.HBM((FIELDS, ROWS, COLS), f...  5.36 us
    ppermute x1, starting transfers between devices, shards(): nxt = lax.ppermute(nxt, 'tile', inner + [(b, a) for a, b in inner])  4.94 us
    all_to_all x1, starting transfers between devices, exchange(): lax.all_to_all(x, ('face', 'tile'), split_axis=0, concat_axis=0, tiled=True)  4.62 us
    pallas_call x1, Pallas kernels, own_parts(): pl.pallas_call(own_kernel, out_shape=(pltpu.HBM((2, FIELDS, ROWS, 128), f...  3.87 us
    pallas_call x1, Pallas kernels, send_blocks(): pl.pallas_call(send_kernel, out_shape=(jax.ShapeDtypeStruct((DEVICES * CH...  2.72 us
  transfers between devices with their start and end apart: 5, of which 1 were waited for; matrix products, arithmetic and copies ran while one was open for 0% of the time, Pallas kernels for 21%

profile of v4, /device:TPU:1, one launch (start us, length us, event | category | flops | bytes accessed | tf_op | source)
XLA Modules:
  0.0 71.6 jit_solution(7645785572597915455)
XLA Ops:
  0.6 1.4 %row_messages.1 = (bf16[112,768]{1,0:T(8,128)(2,1)S(1)}, bf16[112,768]{1,0:T(8,128)(2,1)S(1)}) custom-call(f32[4,8,24,768]{3,2,1,0:T(8,128)} %air.3, f32[3,24,768]{2,1,0:T(8,128)} %refs_4_.3), custom_call_target="tpu_custom_call" | custom-call | flops 400000 | bytes 2000000 | tf_op jit(solution)/shard_map/row_messages/pallas_call | solution.py:105
  2.0 4.9 %collective-permute-start = (bf16[112,768]{1,0:T(8,128)(2,1)S(1)}, bf16[112,768]{1,0:T(8,128)(2,1)S(1)}, u32[]{:S(2)}, u32[]{:S(2)}) collective-permute-start(bf16[112,768]{1,0:T(8,128)(2,1)S(1)} %get-tuple-element.37), channel_id=1, source_target_pairs={{1,2},{3,4},{5,6},{7,8},{9,10},{11,12},{13,14},{15,16},{17,18},{19... | collective-permute-start | bytes 516104 | tf_op jit(solution)/shard_map/ppermute | solution.py:790
  6.9 0.1 collective-permute-start.1
  7.0 3.9 %own_parts.1 = (f32[2,4,24,128]{3,2,1,0:T(8,128)}, f32[2,3,24,128]{3,2,1,0:T(8,128)S(1)}, f32[2,24,128]{2,1,0:T(8,128)S(1)}, f32[2,24,128]{2,1,0:T(8,128)S(1)}, ...) custom-call(f32[4,8]{1,0:T(4,128)} %refs_0_.1, ...), custom_call_target="tpu_custom_call" | custom-call | flops 1600000 | bytes 1200000 | tf_op jit(solution)/shard_map/own_parts/pallas_call | solution.py:266
  10.9 0.0 collective-permute-done.nxt
  10.9 0.0 collective-permute-done.1.sib
  10.9 0.4 column_messages.1
  11.3 1.2 %collective-permute-start.2 = (f32[32,128]{1,0:T(8,128)S(1)}, f32[32,128]{1,0:T(8,128)S(1)}, u32[]{:S(2)}, u32[]{:S(2)}) collective-permute-start(f32[32,128]{1,0:T(8,128)S(1)} %get-tuple-element.46), channel_id=1, source_target_pairs={{0,32},{32,64},{64,96},{96,0},{1,33},{33,65},{65,97},{97,1},{2,34}... | collective-permute-start | bytes 49160 | tf_op jit(solution)/shard_map/ppermute | solution.py:801
  12.5 1.5 %collective-permute-start.3 = (f32[32,128]{1,0:T(8,128)S(1)}, f32[32,128]{1,0:T(8,128)S(1)}, u32[]{:S(2)}, u32[]{:S(2)}) collective-permute-start(f32[32,128]{1,0:T(8,128)S(1)} %get-tuple-element.47), channel_id=1, source_target_pairs={{32,0},{64,32},{96,64},{0,96},{33,1},{65,33},{97,65},{1,97},{34,2}... | collective-permute-start | bytes 49160 | tf_op jit(solution)/shard_map/ppermute | solution.py:800
  14.0 1.9 %flux_stencil.1 = (f32[576,128]{1,0:T(8,128)S(1)}, bf16[112,768]{1,0:T(8,128)(2,1)}, bf16[112,768]{1,0:T(8,128)(2,1)}, bf16[80,128,128]{2,1,0:T(8,128)(2,1)S(1)}) custom-call(f32[4,8,128]{2,1,0:T(8,128)S(1)} %get-tuple-element.34.scale, f32[4,24,768]{2,1,0:T(8,128)S(1)} %get-tuple-element.35.level_sum, f32[3,24,768]{2,1,0:T(8,128)S(1)} %get-tuple-element.36.cour, ...), custom_call_target="tpu_custom_call" | custom-call | flops 3000000 | bytes 1000000 | tf_op jit(solution)/shard_map/flux_stencil/pallas_call | solution.py:391
  15.9 0.0 collective-permute-done.2.refs_4_
  15.9 0.0 collective-permute-done.3.refs_5_
  15.9 0.0 copy-start
  15.9 0.0 copy-start.1
  16.0 0.0 copy-start.2
  16.0 2.7 %send_blocks.1 = (bf16[2816,128]{1,0:T(8,128)(2,1)S(1)}, f32[2,4,8,128]{3,2,1,0:T(8,128)}, f32[32,128]{1,0:T(8,128)}, f32[32,128]{1,0:T(8,128)}, f32[2,3,32,128]{3,2,1,0:T(8,128)}) custom-call(s32[8,288]{1,0:T(8,128)S(1)} %get-tuple-element.33.routes, f32[576,128]{1,0:T(8,128)S(1)} %get-tuple-element.39.flux_in, ...), custom_call_target="tpu_custom_call" | custom-call | flops 40000000 | bytes 11000000 | tf_op jit(solution)/shard_map/send_blocks/pallas_call | solution.py:623
  18.7 26.1 %all_to_all.10 = bf16[1408,2,128]{2,1,0:T(2,128)(2,1)S(1)} all-to-all(bf16[1408,2,128]{2,1,0:T(2,128)(2,1)S(1)} %bitcast.7), channel_id=1, replica_groups=mesh['face'=4,'tile'=32] {'face','tile'}, dimensions={0} | all-to-all | bytes 1441792 | tf_op jit(solution)/shard_map/all_to_all | solution.py:770
  44.8 0.0 copy-done
  44.8 0.0 copy-done.1
  44.8 1.5 %ocean_surface.1 = (f32[4,64,128]{2,1,0:T(8,128)}, bf16[2560,128]{1,0:T(8,128)(2,1)}) custom-call(bf16[2816,128]{1,0:T(8,128)(2,1)S(1)} %bitcast.5, f32[4,8,64,128]{3,2,1,0:T(8,128)S(1)} %copy-done, f32[64,128]{1,0:T(8,128)S(1)} %copy-done.1, s32[64,128]{1,0:T(8,128)S(1)} %copy-done.2), custom_call_target="tpu_custom_call" | custom-call | flops 100000000 | bytes 4000000 | tf_op jit(solution)/shard_map/ocean_surface/pallas_call | solution.py:690
  46.3 4.6 %all-to-all-start.1 = ((bf16[640,4,128]{2,1,0:T(4,128)(2,1)}), bf16[640,4,128]{2,1,0:T(4,128)(2,1)S(1)}, u32[]{:S(2)}, u32[]{:S(2)}) async-start(bf16[640,4,128]{2,1,0:T(4,128)(2,1)} %bitcast.8), calls=%async_computation.1 | async-start | bytes 1310720 | tf_op jit(solution)/shard_map/all_to_all | solution.py:770
  50.9 9.4 %air_steps.1 = (f32[4,8,24,768]{3,2,1,0:T(8,128)}, f32[4,8,64,128]{3,2,1,0:T(8,128)}) custom-call(f32[4,8,24,768]{3,2,1,0:T(8,128)} %air.3, f32[4,64,128]{2,1,0:T(8,128)} %get-tuple-element.52.refs_0_, f32[4,8,64,128]{3,2,1,0:T(8,128)} %refs_1_.3, f32[64,128]{1,0:T(8,128)} %refs_2_.1, s32[64,128]{1,0:T(8,128)} %refs_3_.3, f32[3,24,768]{2,1,0:T(8,128)} %refs_4_.3, ...), custom_call_target="tpu_custom_call" | custom-call | flops 30000000 | bytes 6000000 | tf_op jit(solution)/shard_map/air_steps/pallas_call | solution.py:528
  60.3 5.8 %all-to-all-done.1 = bf16[640,4,128]{2,1,0:T(4,128)(2,1)S(1)} async-done(((bf16[640,4,128]{2,1,0:T(4,128)(2,1)}), bf16[640,4,128]{2,1,0:T(4,128)(2,1)S(1)}, u32[]{:S(2)}, u32[]{:S(2)}) %all-to-all-start.1) | async-done | bytes 655392 | tf_op jit(solution)/shard_map/all_to_all | solution.py:770
  66.1 5.4 %return_blocks.1 = f32[4,24,768]{2,1,0:T(8,128)} custom-call(s32[8,288]{1,0:T(8,128)S(1)} %get-tuple-element.33.routes, bf16[2560,128]{1,0:T(8,128)(2,1)S(1)} %bitcast.6, bf16[288,128,128]{2,1,0:T(8,128)(2,1)} %stored.3), custom_call_target="tpu_custom_call" | custom-call | flops 40000000 | bytes 11000000 | tf_op jit(solution)/shard_map/return_blocks/pallas_call | solution.py:749
  (1 shorter events, 0.0 us)
Async XLA Ops:
  2.0 8.9 %collective-permute-start = (bf16[112,768]{1,0:T(8,128)(2,1)S(1)}, bf16[112,768]{1,0:T(8,128)(2,1)S(1)}, u32[]{:S(2)}, u32[]{:S(2)}) collective-permute-start(bf16[112,768]{1,0:T(8,128)(2,1)S(1)} %get-tuple-element.37), channel_id=1, source_target_pairs={{1,2},{3,4},{5,6},{7,8},{9,10},{11,12},{13,14},{15,16},{17,18},{19... | collective-permute-start | bytes 516104 | tf_op jit(solution)/shard_map/ppermute | solution.py:790
  6.9 4.0 %collective-permute-start.1 = (bf16[112,768]{1,0:T(8,128)(2,1)S(1)}, bf16[112,768]{1,0:T(8,128)(2,1)S(1)}, u32[]{:S(2)}, u32[]{:S(2)}) collective-permute-start(bf16[112,768]{1,0:T(8,128)(2,1)S(1)} %get-tuple-element.38), channel_id=1, source_target_pairs={{0,1},{1,0},{2,3},{3,2},{4,5},{5,4},{6,7},{7,6},{8,9},{9,8},{10,11... | collective-permute-start | bytes 516104 | tf_op jit(solution)/shard_map/ppermute | solution.py:791
  11.3 4.6 %collective-permute-start.2 = (f32[32,128]{1,0:T(8,128)S(1)}, f32[32,128]{1,0:T(8,128)S(1)}, u32[]{:S(2)}, u32[]{:S(2)}) collective-permute-start(f32[32,128]{1,0:T(8,128)S(1)} %get-tuple-element.46), channel_id=1, source_target_pairs={{0,32},{32,64},{64,96},{96,0},{1,33},{33,65},{65,97},{97,1},{2,34}... | collective-permute-start | bytes 49160 | tf_op jit(solution)/shard_map/ppermute | solution.py:801
  12.5 3.4 %collective-permute-start.3 = (f32[32,128]{1,0:T(8,128)S(1)}, f32[32,128]{1,0:T(8,128)S(1)}, u32[]{:S(2)}, u32[]{:S(2)}) collective-permute-start(f32[32,128]{1,0:T(8,128)S(1)} %get-tuple-element.47), channel_id=1, source_target_pairs={{32,0},{64,32},{96,64},{0,96},{33,1},{65,33},{97,65},{1,97},{34,2}... | collective-permute-start | bytes 49160 | tf_op jit(solution)/shard_map/ppermute | solution.py:800
  15.9 28.9 %copy-start = (f32[4,8,64,128]{3,2,1,0:T(8,128)S(1)}, f32[4,8,64,128]{3,2,1,0:T(8,128)}, u32[]{:S(2)}) copy-start(f32[4,8,64,128]{3,2,1,0:T(8,128)} %refs_1_.3) | copy-start | bytes 3145732
  15.9 28.9 %copy-start.1 = (f32[64,128]{1,0:T(8,128)S(1)}, f32[64,128]{1,0:T(8,128)}, u32[]{:S(2)}) copy-start(f32[64,128]{1,0:T(8,128)} %refs_2_.1) | copy-start | bytes 98308
  16.0 28.8 %copy-start.2 = (s32[64,128]{1,0:T(8,128)S(1)}, s32[64,128]{1,0:T(8,128)}, u32[]{:S(2)}) copy-start(s32[64,128]{1,0:T(8,128)} %refs_3_.3) | copy-start | bytes 98308
  46.3 19.8 %all-to-all-start.1 = ((bf16[640,4,128]{2,1,0:T(4,128)(2,1)}), bf16[640,4,128]{2,1,0:T(4,128)(2,1)S(1)}, u32[]{:S(2)}, u32[]{:S(2)}) async-start(bf16[640,4,128]{2,1,0:T(4,128)(2,1)} %bitcast.8), calls=%async_computation.1 | async-start | bytes 1310720 | tf_op jit(solution)/shard_map/all_to_all | solution.py:770

commit v5 on v4

--- a/solution.py
+++ b/solution.py
@@ -342,9 +342,12 @@
     first = 0 if side == 0 else 6
     here = (place >= first) & (place < first + 3)
     spare = (place >= 12) & (place < 15)
-    numbers = [
-        spread(roll(jnp.where((group == k) & spare, got, 0.0), first - 12, 1)) for k in range(3)
-    ]
+    numbers = []
+    for k in range(3):
+        mine = jnp.where((group == k) & spare, got, 0.0)
+        four = [roll(mine, (g - k) * 16 + first - 12, 1) for g in range(4)]
+        four = (four[0] + four[1]) + (four[2] + four[3])
+        numbers.append(four + roll(four, 64, 1))
     return here, numbers, roll(got, first - 60, 1)
 
 

time: 71.9 us -> 71.8 us (level)
  no operation moved by 1% of the time
where the time goes in v5:
time: 71.8 us; the launch traced here: 71.5 us
  Pallas kernels  26.2 us (36%)
  blocking collectives  26.1 us (36%)
  starting transfers between devices  12.3 us (17%)
  waiting for transfers between devices  5.85 us (8%)
  between operations  0.92 us (1%)
    all_to_all x1, blocking collectives, exchange(): lax.all_to_all(x, ('face', 'tile'), split_axis=0, concat_axis=0, tiled=True)  26.1 us
    pallas_call x1, Pallas kernels, air_steps(): pl.pallas_call(air_kernel, out_shape=(pltpu.HBM(air.shape, f32), pltpu.HB...  9.35 us
    all_to_all x1, waiting for transfers between devices, exchange(): lax.all_to_all(x, ('face', 'tile'), split_axis=0, concat_axis=0, tiled=True)  5.83 us
    pallas_call x1, Pallas kernels, return_blocks(): pl.pallas_call(return_kernel, out_shape=pltpu.HBM((FIELDS, ROWS, COLS), f...  5.36 us
    ppermute x1, starting transfers between devices, shards(): nxt = lax.ppermute(nxt, 'tile', inner + [(b, a) for a, b in inner])  4.94 us
    all_to_all x1, starting transfers between devices, exchange(): lax.all_to_all(x, ('face', 'tile'), split_axis=0, concat_axis=0, tiled=True)  4.61 us
    pallas_call x1, Pallas kernels, own_parts(): pl.pallas_call(own_kernel, out_shape=(pltpu.HBM((2, FIELDS, ROWS, 128), f...  3.87 us
    pallas_call x1, Pallas kernels, send_blocks(): pl.pallas_call(send_kernel, out_shape=(jax.ShapeDtypeStruct((DEVICES * CH...  2.56 us
  transfers between devices with their start and end apart: 5, of which 1 were waited for; matrix products, arithmetic and copies ran while one was open for 0% of the time, Pallas kernels for 21%

profile of v5, /device:TPU:1, one launch (start us, length us, event | category | flops | bytes accessed | tf_op | source)
XLA Modules:
  0.0 71.5 jit_solution(7765765441198420956)
XLA Ops:
  0.6 1.4 %row_messages.1 = (bf16[112,768]{1,0:T(8,128)(2,1)S(1)}, bf16[112,768]{1,0:T(8,128)(2,1)S(1)}) custom-call(f32[4,8,24,768]{3,2,1,0:T(8,128)} %air.3, f32[3,24,768]{2,1,0:T(8,128)} %refs_4_.3), custom_call_target="tpu_custom_call" | custom-call | flops 400000 | bytes 2000000 | tf_op jit(solution)/shard_map/row_messages/pallas_call | solution.py:105
  2.0 4.9 %collective-permute-start = (bf16[112,768]{1,0:T(8,128)(2,1)S(1)}, bf16[112,768]{1,0:T(8,128)(2,1)S(1)}, u32[]{:S(2)}, u32[]{:S(2)}) collective-permute-start(bf16[112,768]{1,0:T(8,128)(2,1)S(1)} %get-tuple-element.37), channel_id=1, source_target_pairs={{1,2},{3,4},{5,6},{7,8},{9,10},{11,12},{13,14},{15,16},{17,18},{19... | collective-permute-start | bytes 516104 | tf_op jit(solution)/shard_map/ppermute | solution.py:793
  6.9 0.1 collective-permute-start.1
  7.0 3.9 %own_parts.1 = (f32[2,4,24,128]{3,2,1,0:T(8,128)}, f32[2,3,24,128]{3,2,1,0:T(8,128)S(1)}, f32[2,24,128]{2,1,0:T(8,128)S(1)}, f32[2,24,128]{2,1,0:T(8,128)S(1)}, ...) custom-call(f32[4,8]{1,0:T(4,128)} %refs_0_.1, ...), custom_call_target="tpu_custom_call" | custom-call | flops 1600000 | bytes 1200000 | tf_op jit(solution)/shard_map/own_parts/pallas_call | solution.py:266
  10.9 0.0 collective-permute-done.nxt
  10.9 0.0 collective-permute-done.1.sib
  10.9 0.4 column_messages.1
  11.3 1.2 %collective-permute-start.2 = (f32[32,128]{1,0:T(8,128)S(1)}, f32[32,128]{1,0:T(8,128)S(1)}, u32[]{:S(2)}, u32[]{:S(2)}) collective-permute-start(f32[32,128]{1,0:T(8,128)S(1)} %get-tuple-element.46), channel_id=1, source_target_pairs={{0,32},{32,64},{64,96},{96,0},{1,33},{33,65},{65,97},{97,1},{2,34}... | collective-permute-start | bytes 49160 | tf_op jit(solution)/shard_map/ppermute | solution.py:804
  12.5 1.5 %collective-permute-start.3 = (f32[32,128]{1,0:T(8,128)S(1)}, f32[32,128]{1,0:T(8,128)S(1)}, u32[]{:S(2)}, u32[]{:S(2)}) collective-permute-start(f32[32,128]{1,0:T(8,128)S(1)} %get-tuple-element.47), channel_id=1, source_target_pairs={{32,0},{64,32},{96,64},{0,96},{33,1},{65,33},{97,65},{1,97},{34,2}... | collective-permute-start | bytes 49160 | tf_op jit(solution)/shard_map/ppermute | solution.py:803
  14.0 1.9 %flux_stencil.1 = (f32[576,128]{1,0:T(8,128)S(1)}, bf16[112,768]{1,0:T(8,128)(2,1)}, bf16[112,768]{1,0:T(8,128)(2,1)}, bf16[80,128,128]{2,1,0:T(8,128)(2,1)S(1)}) custom-call(f32[4,8,128]{2,1,0:T(8,128)S(1)} %get-tuple-element.34.scale, f32[4,24,768]{2,1,0:T(8,128)S(1)} %get-tuple-element.35.level_sum, f32[3,24,768]{2,1,0:T(8,128)S(1)} %get-tuple-element.36.cour, ...), custom_call_target="tpu_custom_call" | custom-call | flops 3000000 | bytes 1000000 | tf_op jit(solution)/shard_map/flux_stencil/pallas_call | solution.py:394
  15.9 0.0 collective-permute-done.2.refs_4_
  15.9 0.0 collective-permute-done.3.refs_5_
  15.9 0.0 copy-start
  15.9 0.0 copy-start.1
  16.0 0.0 copy-start.2
  16.0 2.6 %send_blocks.1 = (bf16[2816,128]{1,0:T(8,128)(2,1)S(1)}, f32[2,4,8,128]{3,2,1,0:T(8,128)}, f32[32,128]{1,0:T(8,128)}, f32[32,128]{1,0:T(8,128)}, f32[2,3,32,128]{3,2,1,0:T(8,128)}) custom-call(s32[8,288]{1,0:T(8,128)S(1)} %get-tuple-element.33.routes, f32[576,128]{1,0:T(8,128)S(1)} %get-tuple-element.39.flux_in, ...), custom_call_target="tpu_custom_call" | custom-call | flops 40000000 | bytes 11000000 | tf_op jit(solution)/shard_map/send_blocks/pallas_call | solution.py:626
  18.5 26.1 %all_to_all.10 = bf16[1408,2,128]{2,1,0:T(2,128)(2,1)S(1)} all-to-all(bf16[1408,2,128]{2,1,0:T(2,128)(2,1)S(1)} %bitcast.7), channel_id=1, replica_groups=mesh['face'=4,'tile'=32] {'face','tile'}, dimensions={0} | all-to-all | bytes 1441792 | tf_op jit(solution)/shard_map/all_to_all | solution.py:773
  44.6 0.0 copy-done
  44.7 0.0 copy-done.1
  44.7 1.5 %ocean_surface.1 = (f32[4,64,128]{2,1,0:T(8,128)}, bf16[2560,128]{1,0:T(8,128)(2,1)}) custom-call(bf16[2816,128]{1,0:T(8,128)(2,1)S(1)} %bitcast.5, f32[4,8,64,128]{3,2,1,0:T(8,128)S(1)} %copy-done, f32[64,128]{1,0:T(8,128)S(1)} %copy-done.1, s32[64,128]{1,0:T(8,128)S(1)} %copy-done.2), custom_call_target="tpu_custom_call" | custom-call | flops 100000000 | bytes 4000000 | tf_op jit(solution)/shard_map/ocean_surface/pallas_call | solution.py:693
  46.1 4.6 %all-to-all-start.1 = ((bf16[640,4,128]{2,1,0:T(4,128)(2,1)}), bf16[640,4,128]{2,1,0:T(4,128)(2,1)S(1)}, u32[]{:S(2)}, u32[]{:S(2)}) async-start(bf16[640,4,128]{2,1,0:T(4,128)(2,1)} %bitcast.8), calls=%async_computation.1 | async-start | bytes 1310720 | tf_op jit(solution)/shard_map/all_to_all | solution.py:773
  50.8 9.4 %air_steps.1 = (f32[4,8,24,768]{3,2,1,0:T(8,128)}, f32[4,8,64,128]{3,2,1,0:T(8,128)}) custom-call(f32[4,8,24,768]{3,2,1,0:T(8,128)} %air.3, f32[4,64,128]{2,1,0:T(8,128)} %get-tuple-element.52.refs_0_, f32[4,8,64,128]{3,2,1,0:T(8,128)} %refs_1_.3, f32[64,128]{1,0:T(8,128)} %refs_2_.1, s32[64,128]{1,0:T(8,128)} %refs_3_.3, f32[3,24,768]{2,1,0:T(8,128)} %refs_4_.3, ...), custom_call_target="tpu_custom_call" | custom-call | flops 30000000 | bytes 6000000 | tf_op jit(solution)/shard_map/air_steps/pallas_call | solution.py:531
  60.1 5.8 %all-to-all-done.1 = bf16[640,4,128]{2,1,0:T(4,128)(2,1)S(1)} async-done(((bf16[640,4,128]{2,1,0:T(4,128)(2,1)}), bf16[640,4,128]{2,1,0:T(4,128)(2,1)S(1)}, u32[]{:S(2)}, u32[]{:S(2)}) %all-to-all-start.1) | async-done | bytes 655392 | tf_op jit(solution)/shard_map/all_to_all | solution.py:773
  65.9 5.4 %return_blocks.1 = f32[4,24,768]{2,1,0:T(8,128)} custom-call(s32[8,288]{1,0:T(8,128)S(1)} %get-tuple-element.33.routes, bf16[2560,128]{1,0:T(8,128)(2,1)S(1)} %bitcast.6, bf16[288,128,128]{2,1,0:T(8,128)(2,1)} %stored.3), custom_call_target="tpu_custom_call" | custom-call | flops 40000000 | bytes 11000000 | tf_op jit(solution)/shard_map/return_blocks/pallas_call | solution.py:752
  (1 shorter events, 0.0 us)
Async XLA Ops:
  2.0 8.9 %collective-permute-start = (bf16[112,768]{1,0:T(8,128)(2,1)S(1)}, bf16[112,768]{1,0:T(8,128)(2,1)S(1)}, u32[]{:S(2)}, u32[]{:S(2)}) collective-permute-start(bf16[112,768]{1,0:T(8,128)(2,1)S(1)} %get-tuple-element.37), channel_id=1, source_target_pairs={{1,2},{3,4},{5,6},{7,8},{9,10},{11,12},{13,14},{15,16},{17,18},{19... | collective-permute-start | bytes 516104 | tf_op jit(solution)/shard_map/ppermute | solution.py:793
  6.9 4.0 %collective-permute-start.1 = (bf16[112,768]{1,0:T(8,128)(2,1)S(1)}, bf16[112,768]{1,0:T(8,128)(2,1)S(1)}, u32[]{:S(2)}, u32[]{:S(2)}) collective-permute-start(bf16[112,768]{1,0:T(8,128)(2,1)S(1)} %get-tuple-element.38), channel_id=1, source_target_pairs={{0,1},{1,0},{2,3},{3,2},{4,5},{5,4},{6,7},{7,6},{8,9},{9,8},{10,11... | collective-permute-start | bytes 516104 | tf_op jit(solution)/shard_map/ppermute | solution.py:794
  11.3 4.6 %collective-permute-start.2 = (f32[32,128]{1,0:T(8,128)S(1)}, f32[32,128]{1,0:T(8,128)S(1)}, u32[]{:S(2)}, u32[]{:S(2)}) collective-permute-start(f32[32,128]{1,0:T(8,128)S(1)} %get-tuple-element.46), channel_id=1, source_target_pairs={{0,32},{32,64},{64,96},{96,0},{1,33},{33,65},{65,97},{97,1},{2,34}... | collective-permute-start | bytes 49160 | tf_op jit(solution)/shard_map/ppermute | solution.py:804
  12.5 3.4 %collective-permute-start.3 = (f32[32,128]{1,0:T(8,128)S(1)}, f32[32,128]{1,0:T(8,128)S(1)}, u32[]{:S(2)}, u32[]{:S(2)}) collective-permute-start(f32[32,128]{1,0:T(8,128)S(1)} %get-tuple-element.47), channel_id=1, source_target_pairs={{32,0},{64,32},{96,64},{0,96},{33,1},{65,33},{97,65},{1,97},{34,2}... | collective-permute-start | bytes 49160 | tf_op jit(solution)/shard_map/ppermute | solution.py:803
  15.9 28.7 %copy-start = (f32[4,8,64,128]{3,2,1,0:T(8,128)S(1)}, f32[4,8,64,128]{3,2,1,0:T(8,128)}, u32[]{:S(2)}) copy-start(f32[4,8,64,128]{3,2,1,0:T(8,128)} %refs_1_.3) | copy-start | bytes 3145732
  15.9 28.7 %copy-start.1 = (f32[64,128]{1,0:T(8,128)S(1)}, f32[64,128]{1,0:T(8,128)}, u32[]{:S(2)}) copy-start(f32[64,128]{1,0:T(8,128)} %refs_2_.1) | copy-start | bytes 98308
  16.0 28.7 %copy-start.2 = (s32[64,128]{1,0:T(8,128)S(1)}, s32[64,128]{1,0:T(8,128)}, u32[]{:S(2)}) copy-start(s32[64,128]{1,0:T(8,128)} %refs_3_.3) | copy-start | bytes 98308
  46.1 19.8 %all-to-all-start.1 = ((bf16[640,4,128]{2,1,0:T(4,128)(2,1)}), bf16[640,4,128]{2,1,0:T(4,128)(2,1)S(1)}, u32[]{:S(2)}, u32[]{:S(2)}) async-start(bf16[640,4,128]{2,1,0:T(4,128)(2,1)} %bitcast.8), calls=%async_computation.1 | async-start | bytes 1310720 | tf_op jit(solution)/shard_map/all_to_all | solution.py:773

commit v6 on v5

--- a/solution.py
+++ b/solution.py
@@ -11,7 +11,7 @@
 ENTRIES, DEVICES, CAP, OCEAN_ROWS = 288, 128, 5, 64
 CHUNK = 22
 BACK = CAP * FIELDS
-HALF = 208
+HALF = 176
 f32, bf16 = jnp.float32, jnp.bfloat16
 
 

time: 71.8 us -> 71.5 us (level)
  no operation moved by 1% of the time
where the time goes in v6:
time: 71.5 us; the launch traced here: 71.2 us
  Pallas kernels  26.2 us (37%)
  blocking collectives  25.8 us (36%)
  starting transfers between devices  12.3 us (17%)
  waiting for transfers between devices  5.85 us (8%)
  between operations  0.92 us (1%)
    all_to_all x1, blocking collectives, exchange(): lax.all_to_all(x, ('face', 'tile'), split_axis=0, concat_axis=0, tiled=True)  25.8 us
    pallas_call x1, Pallas kernels, air_steps(): pl.pallas_call(air_kernel, out_shape=(pltpu.HBM(air.shape, f32), pltpu.HB...  9.35 us
    all_to_all x1, waiting for transfers between devices, exchange(): lax.all_to_all(x, ('face', 'tile'), split_axis=0, concat_axis=0, tiled=True)  5.83 us
    pallas_call x1, Pallas kernels, return_blocks(): pl.pallas_call(return_kernel, out_shape=pltpu.HBM((FIELDS, ROWS, COLS), f...  5.36 us
    ppermute x1, starting transfers between devices, shards(): nxt = lax.ppermute(nxt, 'tile', inner + [(b, a) for a, b in inner])  4.94 us
    all_to_all x1, starting transfers between devices, exchange(): lax.all_to_all(x, ('face', 'tile'), split_axis=0, concat_axis=0, tiled=True)  4.61 us
    pallas_call x1, Pallas kernels, own_parts(): pl.pallas_call(own_kernel, out_shape=(pltpu.HBM((2, FIELDS, ROWS, 128), f...  3.57 us
    pallas_call x1, Pallas kernels, send_blocks(): pl.pallas_call(send_kernel, out_shape=(jax.ShapeDtypeStruct((DEVICES * CH...  2.56 us
  transfers between devices with their start and end apart: 5, of which 1 were waited for; matrix products, arithmetic and copies ran while one was open for 0% of the time, Pallas kernels for 21%

profile of v6, /device:TPU:1, one launch (start us, length us, event | category | flops | bytes accessed | tf_op | source)
XLA Modules:
  0.0 71.2 jit_solution(16189422820342645699)
XLA Ops:
  0.6 1.4 %row_messages.1 = (bf16[112,768]{1,0:T(8,128)(2,1)S(1)}, bf16[112,768]{1,0:T(8,128)(2,1)S(1)}) custom-call(f32[4,8,24,768]{3,2,1,0:T(8,128)} %air.3, f32[3,24,768]{2,1,0:T(8,128)} %refs_4_.3), custom_call_target="tpu_custom_call" | custom-call | flops 400000 | bytes 2000000 | tf_op jit(solution)/shard_map/row_messages/pallas_call | solution.py:105
  2.0 4.9 %collective-permute-start = (bf16[112,768]{1,0:T(8,128)(2,1)S(1)}, bf16[112,768]{1,0:T(8,128)(2,1)S(1)}, u32[]{:S(2)}, u32[]{:S(2)}) collective-permute-start(bf16[112,768]{1,0:T(8,128)(2,1)S(1)} %get-tuple-element.37), channel_id=1, source_target_pairs={{1,2},{3,4},{5,6},{7,8},{9,10},{11,12},{13,14},{15,16},{17,18},{19... | collective-permute-start | bytes 516104 | tf_op jit(solution)/shard_map/ppermute | solution.py:793
  6.9 0.1 collective-permute-start.1
  7.0 3.6 %own_parts.1 = (f32[2,4,24,128]{3,2,1,0:T(8,128)}, f32[2,3,24,128]{3,2,1,0:T(8,128)S(1)}, f32[2,24,128]{2,1,0:T(8,128)S(1)}, f32[2,24,128]{2,1,0:T(8,128)S(1)}, ...) custom-call(f32[4,8]{1,0:T(4,128)} %refs_0_.1, ...), custom_call_target="tpu_custom_call" | custom-call | flops 1600000 | bytes 1200000 | tf_op jit(solution)/shard_map/own_parts/pallas_call | solution.py:266
  10.6 0.0 collective-permute-done.nxt
  10.6 0.0 collective-permute-done.1.sib
  10.6 0.4 column_messages.1
  11.0 1.2 %collective-permute-start.2 = (f32[32,128]{1,0:T(8,128)S(1)}, f32[32,128]{1,0:T(8,128)S(1)}, u32[]{:S(2)}, u32[]{:S(2)}) collective-permute-start(f32[32,128]{1,0:T(8,128)S(1)} %get-tuple-element.46), channel_id=1, source_target_pairs={{0,32},{32,64},{64,96},{96,0},{1,33},{33,65},{65,97},{97,1},{2,34}... | collective-permute-start | bytes 49160 | tf_op jit(solution)/shard_map/ppermute | solution.py:804
  12.2 1.5 %collective-permute-start.3 = (f32[32,128]{1,0:T(8,128)S(1)}, f32[32,128]{1,0:T(8,128)S(1)}, u32[]{:S(2)}, u32[]{:S(2)}) collective-permute-start(f32[32,128]{1,0:T(8,128)S(1)} %get-tuple-element.47), channel_id=1, source_target_pairs={{32,0},{64,32},{96,64},{0,96},{33,1},{65,33},{97,65},{1,97},{34,2}... | collective-permute-start | bytes 49160 | tf_op jit(solution)/shard_map/ppermute | solution.py:803
  13.7 2.2 %flux_stencil.1 = (f32[576,128]{1,0:T(8,128)S(1)}, bf16[112,768]{1,0:T(8,128)(2,1)}, bf16[112,768]{1,0:T(8,128)(2,1)}, bf16[112,128,128]{2,1,0:T(8,128)(2,1)S(1)}) custom-call(f32[4,8,128]{2,1,0:T(8,128)S(1)} %get-tuple-element.34.scale, f32[4,24,768]{2,1,0:T(8,128)S(1)} %get-tuple-element.35.level_sum, f32[3,24,768]{2,1,0:T(8,128)S(1)} %get-tuple-element.36.cour, ...), custom_call_target="tpu_custom_call" | custom-call | flops 3000000 | bytes 1000000 | tf_op jit(solution)/shard_map/flux_stencil/pallas_call | solution.py:394
  15.9 0.0 collective-permute-done.2.refs_4_
  15.9 0.0 collective-permute-done.3.refs_5_
  15.9 0.0 copy-start
  15.9 0.0 copy-start.1
  16.0 0.0 copy-start.2
  16.0 2.6 %send_blocks.1 = (bf16[2816,128]{1,0:T(8,128)(2,1)S(1)}, f32[2,4,8,128]{3,2,1,0:T(8,128)}, f32[32,128]{1,0:T(8,128)}, f32[32,128]{1,0:T(8,128)}, f32[2,3,32,128]{3,2,1,0:T(8,128)}) custom-call(s32[8,288]{1,0:T(8,128)S(1)} %get-tuple-element.33.routes, f32[576,128]{1,0:T(8,128)S(1)} %get-tuple-element.39.flux_in, ...), custom_call_target="tpu_custom_call" | custom-call | flops 40000000 | bytes 11000000 | tf_op jit(solution)/shard_map/send_blocks/pallas_call | solution.py:626
  18.5 25.8 %all_to_all.10 = bf16[1408,2,128]{2,1,0:T(2,128)(2,1)S(1)} all-to-all(bf16[1408,2,128]{2,1,0:T(2,128)(2,1)S(1)} %bitcast.7), channel_id=1, replica_groups=mesh['face'=4,'tile'=32] {'face','tile'}, dimensions={0} | all-to-all | bytes 1441792 | tf_op jit(solution)/shard_map/all_to_all | solution.py:773
  44.3 0.0 copy-done
  44.3 0.0 copy-done.1
  44.4 1.5 %ocean_surface.1 = (f32[4,64,128]{2,1,0:T(8,128)}, bf16[2560,128]{1,0:T(8,128)(2,1)}) custom-call(bf16[2816,128]{1,0:T(8,128)(2,1)S(1)} %bitcast.5, f32[4,8,64,128]{3,2,1,0:T(8,128)S(1)} %copy-done, f32[64,128]{1,0:T(8,128)S(1)} %copy-done.1, s32[64,128]{1,0:T(8,128)S(1)} %copy-done.2), custom_call_target="tpu_custom_call" | custom-call | flops 100000000 | bytes 4000000 | tf_op jit(solution)/shard_map/ocean_surface/pallas_call | solution.py:693
  45.8 4.6 %all-to-all-start.1 = ((bf16[640,4,128]{2,1,0:T(4,128)(2,1)}), bf16[640,4,128]{2,1,0:T(4,128)(2,1)S(1)}, u32[]{:S(2)}, u32[]{:S(2)}) async-start(bf16[640,4,128]{2,1,0:T(4,128)(2,1)} %bitcast.8), calls=%async_computation.1 | async-start | bytes 1310720 | tf_op jit(solution)/shard_map/all_to_all | solution.py:773
  50.4 9.4 %air_steps.1 = (f32[4,8,24,768]{3,2,1,0:T(8,128)}, f32[4,8,64,128]{3,2,1,0:T(8,128)}) custom-call(f32[4,8,24,768]{3,2,1,0:T(8,128)} %air.3, f32[4,64,128]{2,1,0:T(8,128)} %get-tuple-element.52.refs_0_, f32[4,8,64,128]{3,2,1,0:T(8,128)} %refs_1_.3, f32[64,128]{1,0:T(8,128)} %refs_2_.1, s32[64,128]{1,0:T(8,128)} %refs_3_.3, f32[3,24,768]{2,1,0:T(8,128)} %refs_4_.3, ...), custom_call_target="tpu_custom_call" | custom-call | flops 30000000 | bytes 6000000 | tf_op jit(solution)/shard_map/air_steps/pallas_call | solution.py:531
  59.8 5.8 %all-to-all-done.1 = bf16[640,4,128]{2,1,0:T(4,128)(2,1)S(1)} async-done(((bf16[640,4,128]{2,1,0:T(4,128)(2,1)}), bf16[640,4,128]{2,1,0:T(4,128)(2,1)S(1)}, u32[]{:S(2)}, u32[]{:S(2)}) %all-to-all-start.1) | async-done | bytes 655392 | tf_op jit(solution)/shard_map/all_to_all | solution.py:773
  65.6 5.4 %return_blocks.1 = f32[4,24,768]{2,1,0:T(8,128)} custom-call(s32[8,288]{1,0:T(8,128)S(1)} %get-tuple-element.33.routes, bf16[2560,128]{1,0:T(8,128)(2,1)S(1)} %bitcast.6, bf16[288,128,128]{2,1,0:T(8,128)(2,1)} %stored.3), custom_call_target="tpu_custom_call" | custom-call | flops 40000000 | bytes 11000000 | tf_op jit(solution)/shard_map/return_blocks/pallas_call | solution.py:752
  (1 shorter events, 0.0 us)
Async XLA Ops:
  2.0 8.6 %collective-permute-start = (bf16[112,768]{1,0:T(8,128)(2,1)S(1)}, bf16[112,768]{1,0:T(8,128)(2,1)S(1)}, u32[]{:S(2)}, u32[]{:S(2)}) collective-permute-start(bf16[112,768]{1,0:T(8,128)(2,1)S(1)} %get-tuple-element.37), channel_id=1, source_target_pairs={{1,2},{3,4},{5,6},{7,8},{9,10},{11,12},{13,14},{15,16},{17,18},{19... | collective-permute-start | bytes 516104 | tf_op jit(solution)/shard_map/ppermute | solution.py:793
  6.9 3.7 %collective-permute-start.1 = (bf16[112,768]{1,0:T(8,128)(2,1)S(1)}, bf16[112,768]{1,0:T(8,128)(2,1)S(1)}, u32[]{:S(2)}, u32[]{:S(2)}) collective-permute-start(bf16[112,768]{1,0:T(8,128)(2,1)S(1)} %get-tuple-element.38), channel_id=1, source_target_pairs={{0,1},{1,0},{2,3},{3,2},{4,5},{5,4},{6,7},{7,6},{8,9},{9,8},{10,11... | collective-permute-start | bytes 516104 | tf_op jit(solution)/shard_map/ppermute | solution.py:794
  11.0 4.9 %collective-permute-start.2 = (f32[32,128]{1,0:T(8,128)S(1)}, f32[32,128]{1,0:T(8,128)S(1)}, u32[]{:S(2)}, u32[]{:S(2)}) collective-permute-start(f32[32,128]{1,0:T(8,128)S(1)} %get-tuple-element.46), channel_id=1, source_target_pairs={{0,32},{32,64},{64,96},{96,0},{1,33},{33,65},{65,97},{97,1},{2,34}... | collective-permute-start | bytes 49160 | tf_op jit(solution)/shard_map/ppermute | solution.py:804
  12.2 3.7 %collective-permute-start.3 = (f32[32,128]{1,0:T(8,128)S(1)}, f32[32,128]{1,0:T(8,128)S(1)}, u32[]{:S(2)}, u32[]{:S(2)}) collective-permute-start(f32[32,128]{1,0:T(8,128)S(1)} %get-tuple-element.47), channel_id=1, source_target_pairs={{32,0},{64,32},{96,64},{0,96},{33,1},{65,33},{97,65},{1,97},{34,2}... | collective-permute-start | bytes 49160 | tf_op jit(solution)/shard_map/ppermute | solution.py:803
  15.9 28.4 %copy-start = (f32[4,8,64,128]{3,2,1,0:T(8,128)S(1)}, f32[4,8,64,128]{3,2,1,0:T(8,128)}, u32[]{:S(2)}) copy-start(f32[4,8,64,128]{3,2,1,0:T(8,128)} %refs_1_.3) | copy-start | bytes 3145732
  15.9 28.4 %copy-start.1 = (f32[64,128]{1,0:T(8,128)S(1)}, f32[64,128]{1,0:T(8,128)}, u32[]{:S(2)}) copy-start(f32[64,128]{1,0:T(8,128)} %refs_2_.1) | copy-start | bytes 98308
  16.0 28.4 %copy-start.2 = (s32[64,128]{1,0:T(8,128)S(1)}, s32[64,128]{1,0:T(8,128)}, u32[]{:S(2)}) copy-start(s32[64,128]{1,0:T(8,128)} %refs_3_.3) | copy-start | bytes 98308
  45.8 19.8 %all-to-all-start.1 = ((bf16[640,4,128]{2,1,0:T(4,128)(2,1)}), bf16[640,4,128]{2,1,0:T(4,128)(2,1)S(1)}, u32[]{:S(2)}, u32[]{:S(2)}) async-start(bf16[640,4,128]{2,1,0:T(4,128)(2,1)} %bitcast.8), calls=%async_computation.1 | async-start | bytes 1310720 | tf_op jit(solution)/shard_map/all_to_all | solution.py:773
